TPU v7x, 32 devices: a whole 2x2x4 slice. The times are simulated.
32 devices in a mesh: group: 8 (over y, x, core), ctx: 4 (over z).
Axes of the slice: x: 2, y: 2, z: 4, core: 2. Of those that a mesh axis runs over, the one named last changes fastest.
Arguments:
- query: bfloat16 [8, 4, 32, 8192], P('group', None, None, 'ctx'), may hold values from -160 to 160
- cache_keys: bfloat16 [8, 4, 2048, 1024], P('group', None, 'ctx'), may hold values from -6 to 6
- cache_values: bfloat16 [8, 4, 2048, 1024], P('group', None, 'ctx'), may hold values from -6 to 6
- new_keys: bfloat16 [8, 4, 32, 1024], P('group', None, 'ctx'), may hold values from -6 to 6
- new_values: bfloat16 [8, 4, 32, 1024], P('group', None, 'ctx'), may hold values from -6 to 6
- masks: int32 [3], replicated, may hold values from 1 to 7
- movers: int32 [3, 8], replicated, may hold values from 0 to 3
- block_lists: int32 [3, 8, 4], replicated, may hold values from 0 to 3, as said below
- lengths: int32 [8, 4], replicated, may hold values from 1 to 2048
Outputs:
- attended: bfloat16 [8, 4, 32, 8192], P('group', None, None, 'ctx')
- keys_after: bfloat16 [8, 4, 2048, 1024], P('group', None, 'ctx')
- values_after: bfloat16 [8, 4, 2048, 1024], P('group', None, 'ctx')
Inputs may be any that keep to these rules, and one draw needn't show every extreme that they name: `block_lists`: each row is a permutation of the 4 blocks.
All inputs are finite; a program needn't handle non-finite values.
Results may differ from a plain program's by a relative error of at most 0.005.
Values may be sent and summed in bfloat16 or wider, within the bound.
No kernel may reach another device: no remote copies, remote signals or barrier semaphores. Data moves between devices by JAX's collectives and lax.ppermute only.
A program may use at most 192 MiB of HBM per device.

v0:
```python
import jax
import jax.numpy as jnp
from jax import lax
from jax.sharding import PartitionSpec as P

HD = 128
NEW = 32
MATCHINGS = 3
BLOCK = 128


def swapped_2(block, axis, stride):
    count = lax.axis_size(axis)
    route = []
    for low in range(count):
        high = low | 1 << stride
        if high != low and high < count:
            route += [(low, high), (high, low)]
    return lax.ppermute(block, axis, route)


def route_blocks(payload, mask_value, groups):
    current = payload
    for bit in range(groups.bit_length() - 1):
        swapped = swapped_2(current, "group", bit)
        flag = jnp.bitwise_and(jnp.right_shift(mask_value, bit), 1) == 1
        current = jnp.where(flag, swapped, current)
    return current


def shards(
    query, cache_keys, cache_values, new_keys, new_values, masks, movers, block_lists, lengths
):
    groups = lax.axis_size("group")
    width = lax.axis_size("ctx")
    here = lax.axis_index("group")
    place = lax.axis_index("ctx")
    keys = cache_keys[0]
    values = cache_values[0]
    segment = keys.shape[1]
    features = keys.shape[2]
    nblocks = segment // BLOCK
    moving = block_lists.shape[2]
    every = jnp.arange(groups, dtype=jnp.int32)
    counts = lengths
    for step in range(MATCHINGS):
        mask_value = masks[step]
        partner = jnp.bitwise_xor(every, mask_value)
        slots = movers[step]
        slot = slots[here]
        chosen = block_lists[step, here]
        key_rows = lax.dynamic_index_in_dim(keys, slot, 0, keepdims=False).reshape(
            nblocks, BLOCK, features
        )
        value_rows = lax.dynamic_index_in_dim(values, slot, 0, keepdims=False).reshape(
            nblocks, BLOCK, features
        )
        payload = jnp.stack(
            [
                jnp.take(key_rows, chosen, axis=0).reshape(moving * BLOCK, features),
                jnp.take(value_rows, chosen, axis=0).reshape(moving * BLOCK, features),
            ]
        )
        arrived = route_blocks(payload, mask_value, groups).reshape(2, moving, BLOCK, features)
        key_rows = key_rows.at[chosen].set(arrived[0])
        value_rows = value_rows.at[chosen].set(arrived[1])
        keys = lax.dynamic_update_index_in_dim(keys, key_rows.reshape(segment, features), slot, 0)
        values = lax.dynamic_update_index_in_dim(
            values, value_rows.reshape(segment, features), slot, 0
        )
        counts = counts.at[every, slots].set(counts[partner, slots[partner]])
    own_counts = counts[here]
    gathered = lax.all_gather(query[0], "ctx", axis=2, tiled=True)
    heads = gathered.shape[2] // HD
    kv_heads = features // HD
    ratio = heads // kv_heads
    local_new = new_keys.shape[2]
    scale = 1.0 / HD**0.5
    positions = place * segment + jnp.arange(segment, dtype=jnp.int32)
    new_index = place * local_new + jnp.arange(local_new, dtype=jnp.int32)
    token_index = jnp.arange(NEW, dtype=jnp.int32)
    valid_new = new_index[None, :] <= token_index[:, None]

    def partial_attention(args):
        asked, key_block, value_block, fresh_keys, fresh_values, count = args
        heads_q = asked.reshape(NEW, kv_heads, ratio, HD)
        older = (
            jnp.einsum(
                "tkgd,skd->kgts",
                heads_q,
                key_block.reshape(segment, kv_heads, HD),
                preferred_element_type=jnp.float32,
            )
            * scale
        )
        newer = (
            jnp.einsum(
                "tkgd,skd->kgts",
                heads_q,
                fresh_keys.reshape(local_new, kv_heads, HD),
                preferred_element_type=jnp.float32,
            )
            * scale
        )
        valid_old = (positions < count)[None, None, None, :]
        older = jnp.where(valid_old, older, -1e30)
        newer = jnp.where(valid_new[None, None], newer, -1e30)
        top = jnp.maximum(jnp.max(older, axis=-1), jnp.max(newer, axis=-1))
        exp_old = jnp.where(valid_old, jnp.exp(older - top[..., None]), 0.0)
        exp_new = jnp.where(valid_new[None, None], jnp.exp(newer - top[..., None]), 0.0)
        total = jnp.sum(exp_old, axis=-1) + jnp.sum(exp_new, axis=-1)
        summed = jnp.einsum(
            "kgts,skd->tkgd",
            exp_old.astype(jnp.bfloat16),
            value_block.reshape(segment, kv_heads, HD),
            preferred_element_type=jnp.float32,
        )
        summed = summed + jnp.einsum(
            "kgts,skd->tkgd",
            exp_new.astype(jnp.bfloat16),
            fresh_values.reshape(local_new, kv_heads, HD),
            preferred_element_type=jnp.float32,
        )
        top_rows = jnp.transpose(top, (2, 0, 1)).reshape(NEW, heads)
        total_rows = jnp.transpose(total, (2, 0, 1)).reshape(NEW, heads)
        return (top_rows, total_rows, summed.reshape(NEW, heads * HD))

    top, total, summed = lax.map(
        partial_attention, (gathered, keys, values, new_keys[0], new_values[0], own_counts)
    )
    own = heads // width
    requests = summed.shape[0]
    peak = lax.pmax(top, "ctx")
    factor = jnp.exp(top - peak)
    scaled = (summed.reshape(requests, NEW, heads, HD) * factor[..., None]).reshape(summed.shape)
    numer, denom = (
        lax.psum_scatter(scaled, "ctx", scatter_dimension=2, tiled=True),
        lax.psum_scatter(total * factor, "ctx", scatter_dimension=2, tiled=True),
    )
    attended = (numer.reshape(requests, NEW, own, HD) / denom[..., None]).reshape(
        requests, NEW, own * HD
    )
    return (attended.astype(jnp.bfloat16)[None], keys[None], values[None])


def solution(mesh):
    placed = (
        P("group", None, None, "ctx"),
        P("group", None, "ctx", None),
        P("group", None, "ctx", None),
        P("group", None, "ctx", None),
        P("group", None, "ctx", None),
        P(),
        P(),
        P(),
        P(),
    )
    return jax.shard_map(
        shards,
        mesh=mesh,
        in_specs=placed,
        out_specs=(
            P("group", None, None, "ctx"),
            P("group", None, "ctx", None),
            P("group", None, "ctx", None),
        ),
        check_vma=False,
    )
```

profile of v0, /device:TPU:0, one launch (start us, length us, event | category | flops | bytes accessed | tf_op | source)
XLA Modules:
  0.0 574.0 jit_solution(9454595988241032118)
XLA Ops:
  7.2 4.8 copy.89
  12.1 2.0 copy.90
  27.2 2.9 collective-permute-done
  30.1 2.8 broadcast_select_fusion.6
  32.9 2.9 collective-permute-start.1
  36.3 45.7 %collective-permute-done.1 = bf16[2,512,1024]{2,1,0:T(8,128)(2,1)} collective-permute-done((bf16[2,512,1024]{2,1,0:T(8,128)(2,1)}, bf16[2,512,1024]{2,1,0:T(8,128)(2,1)}, u32[]{:S(2)}, u32[]{:S(2)}) %collective-permute-start.1) | collective-permute-done | bytes 2097184 | tf_op jit(solution)/shard_map/ppermute | solution.py:19
  82.0 3.4 broadcast_select_fusion.7
  90.2 42.7 %collective-permute-done.2 = bf16[2,512,1024]{2,1,0:T(8,128)(2,1)} collective-permute-done((bf16[2,512,1024]{2,1,0:T(8,128)(2,1)}, bf16[2,512,1024]{2,1,0:T(8,128)(2,1)}, u32[]{:S(2)}, u32[]{:S(2)}) %collective-permute-start.2) | collective-permute-done | bytes 2097184 | tf_op jit(solution)/shard_map/ppermute | solution.py:19
  132.9 1.8 broadcast_select_fusion.8
  135.8 1.9 scatter_fusion.4
  150.6 3.8 collective-permute-done.3
  154.4 2.8 broadcast_select_fusion.3
  159.3 45.9 %collective-permute-done.4 = bf16[2,512,1024]{2,1,0:T(8,128)(2,1)} collective-permute-done((bf16[2,512,1024]{2,1,0:T(8,128)(2,1)}, bf16[2,512,1024]{2,1,0:T(8,128)(2,1)}, u32[]{:S(2)}, u32[]{:S(2)}) %collective-permute-start.4) | collective-permute-done | bytes 2097184 | tf_op jit(solution)/shard_map/ppermute | solution.py:19
  205.2 3.4 broadcast_select_fusion.4
  212.9 43.0 %collective-permute-done.5 = bf16[2,512,1024]{2,1,0:T(8,128)(2,1)} collective-permute-done((bf16[2,512,1024]{2,1,0:T(8,128)(2,1)}, bf16[2,512,1024]{2,1,0:T(8,128)(2,1)}, u32[]{:S(2)}, u32[]{:S(2)}) %collective-permute-start.5) | collective-permute-done | bytes 2097184 | tf_op jit(solution)/shard_map/ppermute | solution.py:19
  255.8 1.8 broadcast_select_fusion.5
  258.8 1.9 scatter_fusion.6
  273.7 3.8 collective-permute-done.6
  277.5 3.5 broadcast_select_fusion
  283.4 45.6 %collective-permute-done.7 = bf16[2,512,1024]{2,1,0:T(8,128)(2,1)} collective-permute-done((bf16[2,512,1024]{2,1,0:T(8,128)(2,1)}, bf16[2,512,1024]{2,1,0:T(8,128)(2,1)}, u32[]{:S(2)}, u32[]{:S(2)}) %collective-permute-start.7) | collective-permute-done | bytes 2097184 | tf_op jit(solution)/shard_map/ppermute | solution.py:19
  329.0 4.1 broadcast_select_fusion.1
  345.8 34.5 %collective-permute-done.8 = bf16[2,512,1024]{2,1,0:T(8,128)(2,1)} collective-permute-done((bf16[2,512,1024]{2,1,0:T(8,128)(2,1)}, bf16[2,512,1024]{2,1,0:T(8,128)(2,1)}, u32[]{:S(2)}, u32[]{:S(2)}) %collective-permute-start.8) | collective-permute-done | bytes 2097184 | tf_op jit(solution)/shard_map/ppermute | solution.py:19
  380.3 1.8 broadcast_select_fusion.2
  383.2 1.9 scatter_fusion.8
  388.1 60.4 %while.15 = (s32[]{:T(128)}, f32[4,32,64]{1,2,0:T(8,128)S(1)}, f32[4,32,64]{1,2,0:T(8,128)S(1)}, f32[4,32,8192]{2,1,0:T(8,128)}, s32[4]{0:T(128)S(1)}, /*index=5...) while((s32[]{:T(128)}, f32[4,32,64]{1,2,0:T(8,128)S(1)}, ...), condition=%wide.region_14.16_spmd.clone, body=%wide.region_9.0_spmd.clone.sunk | while | flops 559297792 | bytes 44567820 | solution.py:128
  448.5 21.0 %pmax.7 = f32[4,32,64]{1,2,0:T(8,128)S(1)} all-reduce(f32[4,32,64]{1,2,0:T(8,128)S(1)} %get-tuple-element.69), channel_id=1, replica_groups=mesh['group'=8,'ctx'=4] {'ctx'}, use_global_device_ids=true, to_apply=%region_15.17 | all-reduce | flops 8192 | bytes 65536 | tf_op jit(solution)/shard_map/pmax | solution.py:133
  470.3 2.6 mul.32
  472.9 4.9 mul.33
  477.9 6.0 %mul.34 = f32[4,32,8192]{2,1,0:T(8,128)} multiply(f32[4,32,8192]{2,1,0:T(8,128)} %get-tuple-element.68, f32[4,32,8192]{2,1,0:T(8,128)} %mul.33) | non-fusion elementwise | flops 1048576 | bytes 12582912 | tf_op jit(solution)/shard_map/mul | solution.py:135
  483.9 4.0 reduce-scatter.5.cloned.1.call-done
  489.3 76.0 %reduce-scatter.3.cloned.1.call-done = f32[4,32,2048]{2,1,0:T(8,128)} async-done(((f32[4,32,8192]{2,1,0:T(8,128)}), f32[4,32,2048]{2,1,0:T(8,128)}) %reduce-scatter.3.cloned.1.call-update) | async-done | bytes 1048592 | tf_op jit(solution)/shard_map/reduce_scatter | solution.py:137
  565.3 2.2 fusion.34
  (194 shorter events, 122.4 us)
Async XLA Ops:
  7.2 380.9 %all-gather.3.cloned.1.call-start = ((), (), s32[]{:S(2)}) async-start(), calls=%async_computation.4 | async-start | bytes 2621440 | tf_op jit(solution)/shard_map/all_gather | solution.py:73
  7.2 4.8 copy-start.5
  12.0 2.0 copy-start.9
  12.0 2.0 copy-start.6
  12.0 2.3 copy-start.8
  23.9 1.6 copy-start.3
  23.9 2.1 copy-start.7
  25.5 4.6 collective-permute-start
  32.9 49.1 %collective-permute-start.1 = (bf16[2,512,1024]{2,1,0:T(8,128)(2,1)}, bf16[2,512,1024]{2,1,0:T(8,128)(2,1)}, u32[]{:S(2)}, u32[]{:S(2)}) collective-permute-start(bf16[2,512,1024]{2,1,0:T(8,128)(2,1)} %broadcast_select_fusion.6), channel_id=1, source_target_pairs={{0,8},{8,0},{4,12},{12,4},{16,24},{24,16},{20,28},{28,20},{1,9},{9... | collective-permute-start | bytes 6291464 | tf_op jit(solution)/shard_map/ppermute | solution.py:19
  85.4 47.5 %collective-permute-start.2 = (bf16[2,512,1024]{2,1,0:T(8,128)(2,1)}, bf16[2,512,1024]{2,1,0:T(8,128)(2,1)}, u32[]{:S(2)}, u32[]{:S(2)}) collective-permute-start(bf16[2,512,1024]{2,1,0:T(8,128)(2,1)} %broadcast_select_fusion.7), channel_id=1, source_target_pairs={{0,16},{16,0},{4,20},{20,4},{8,24},{24,8},{12,28},{28,12},{1,17},{... | collective-permute-start | bytes 6291464 | tf_op jit(solution)/shard_map/ppermute | solution.py:19
  148.3 1.6 copy-start.4
  149.9 4.5 collective-permute-start.3
  157.2 48.0 %collective-permute-start.4 = (bf16[2,512,1024]{2,1,0:T(8,128)(2,1)}, bf16[2,512,1024]{2,1,0:T(8,128)(2,1)}, u32[]{:S(2)}, u32[]{:S(2)}) collective-permute-start(bf16[2,512,1024]{2,1,0:T(8,128)(2,1)} %broadcast_select_fusion.3), channel_id=1, source_target_pairs={{0,8},{8,0},{4,12},{12,4},{16,24},{24,16},{20,28},{28,20},{1,9},{9... | collective-permute-start | bytes 6291464 | tf_op jit(solution)/shard_map/ppermute | solution.py:19
  208.6 47.2 %collective-permute-start.5 = (bf16[2,512,1024]{2,1,0:T(8,128)(2,1)}, bf16[2,512,1024]{2,1,0:T(8,128)(2,1)}, u32[]{:S(2)}, u32[]{:S(2)}) collective-permute-start(bf16[2,512,1024]{2,1,0:T(8,128)(2,1)} %broadcast_select_fusion.4), channel_id=1, source_target_pairs={{0,16},{16,0},{4,20},{20,4},{8,24},{24,8},{12,28},{28,12},{1,17},{... | collective-permute-start | bytes 6291464 | tf_op jit(solution)/shard_map/ppermute | solution.py:19
  271.3 1.8 copy-start.2
  273.0 4.5 collective-permute-start.6
  281.0 48.0 %collective-permute-start.7 = (bf16[2,512,1024]{2,1,0:T(8,128)(2,1)}, bf16[2,512,1024]{2,1,0:T(8,128)(2,1)}, u32[]{:S(2)}, u32[]{:S(2)}) collective-permute-start(bf16[2,512,1024]{2,1,0:T(8,128)(2,1)} %broadcast_select_fusion), channel_id=1, source_target_pairs={{0,8},{8,0},{4,12},{12,4},{16,24},{24,16},{20,28},{28,20},{1,9},{9... | collective-permute-start | bytes 6291464 | tf_op jit(solution)/shard_map/ppermute | solution.py:19
  282.5 205.5 %reduce-scatter.5.cloned.1.call-start = ((), (), s32[]{:S(2)}) async-start(), calls=%async_computation.3 | async-start | bytes 163840 | tf_op jit(solution)/shard_map/reduce_scatter | solution.py:138
  333.1 47.2 %collective-permute-start.8 = (bf16[2,512,1024]{2,1,0:T(8,128)(2,1)}, bf16[2,512,1024]{2,1,0:T(8,128)(2,1)}, u32[]{:S(2)}, u32[]{:S(2)}) collective-permute-start(bf16[2,512,1024]{2,1,0:T(8,128)(2,1)} %broadcast_select_fusion.1), channel_id=1, source_target_pairs={{0,16},{16,0},{4,20},{20,4},{8,24},{24,8},{12,28},{28,12},{1,17},{... | collective-permute-start | bytes 6291464 | tf_op jit(solution)/shard_map/ppermute | solution.py:19
  395.1 1.3 copy-start
  396.5 1.2 copy-start.1
  410.2 1.3 copy-start
  411.6 1.2 copy-start.1
  425.4 1.3 copy-start
  426.7 1.2 copy-start.1
  440.5 1.3 copy-start
  441.8 1.2 copy-start.1
  470.2 95.1 %reduce-scatter.3.cloned.1.call-start = ((), (), s32[]{:S(2)}) async-start(), calls=%async_computation.2 | async-start | bytes 5242880 | tf_op jit(solution)/shard_map/reduce_scatter | solution.py:137
Sparse Core Ops, SparseCore 0:
  282.6 46.2 all-gather.2
  470.3 17.5 reduce-scatter.4
  490.3 74.9 reduce-scatter.2
where the time goes:
time: 576 us; the launch traced here: 574 us
  waiting for transfers between devices  348 us (60%)
  local copies, waits for them, and re-layouts  91.6 us (16%)
  other arithmetic  56.6 us (10%)
  between operations  25.7 us (4%)
  blocking collectives  21 us (4%)
  matrix products  19.6 us (3%)
  starting transfers between devices  11.1 us (2%)
    ppermute x9, waiting for transfers between devices, swapped_2(): return lax.ppermute(block, axis, route)  268 us
    reduce_scatter x1, waiting for transfers between devices, shards(): lax.psum_scatter(scaled, 'ctx', scatter_dimension=2, tiled=True)  76 us
    select_n x9, other arithmetic, route_blocks(): current = jnp.where(flag, swapped, current)  25.4 us
    pmax x1, blocking collectives, shards(): peak = lax.pmax(top, 'ctx')  21 us
    dynamic_slice x16, local copies, waits for them, and re-layouts, shards(): lax.map(partial_attention, (gathered, keys, values, new_keys[0], new_valu...  20 us
  transfers between devices with their start and end apart: 12, of which 11 were waited for; matrix products, arithmetic and copies ran while one was open for 7% of the time, Pallas kernels for 0%

commit v1 on v0

v1 whole, which is shorter than its diff:
```python
import functools
import math

import jax
import jax.numpy as jnp
from jax import lax
from jax.experimental import pallas as pl
from jax.experimental.pallas import tpu as pltpu
from jax.sharding import PartitionSpec as P

HD = 128
LANES = 128
MASKED = -1e30
FLOOR = -1e29
BF16 = jnp.bfloat16
F32 = jnp.float32
ANY = pl.BlockSpec(memory_space=pl.ANY)
SMEM = pl.BlockSpec(memory_space=pltpu.SMEM)
VMEM = pl.BlockSpec(memory_space=pltpu.VMEM)


def exchange(block, axis, mask):
    return lax.ppermute(block, axis, [(i, i ^ mask) for i in range(lax.axis_size(axis))])


class Layout:
    def __init__(self, requests, nblocks, matchings):
        self.slot = 0
        self.last = requests
        self.count = 2 * requests
        self.perm = 3 * requests
        self.home = self.perm + requests * nblocks
        self.mover = self.home + requests * nblocks
        self.source = self.mover + matchings
        self.place = self.source + matchings
        self.size = self.place + 1


def plan_kernel(
    at, masks, movers, lists, lengths, keys, values, plan, key_out, value_out, sems
):
    matchings, groups, nblocks = lists.shape
    requests = lengths.shape[1]
    here = lax.axis_index("group")
    first = movers[0, here]
    copies = [
        pltpu.make_async_copy(keys.at[0, first], key_out, sems.at[0]),
        pltpu.make_async_copy(values.at[0, first], value_out, sems.at[1]),
    ]
    for copy in copies:
        copy.start()
    plan[at.place] = lax.axis_index("ctx")
    traced = []
    for slot in range(requests):
        group, where = here, jnp.int32(slot)
        last = jnp.int32(-1)
        blocks = [jnp.int32(b) for b in range(nblocks)]
        for step in reversed(range(matchings)):
            hit = movers[step, group] == where
            partner = group ^ masks[step]
            last = jnp.where(jnp.logical_and(hit, last < 0), step, last)
            moved = []
            for block in blocks:
                origin = block
                for j in range(nblocks):
                    origin = jnp.where(
                        lists[step, group, j] == block, lists[step, partner, j], origin
                    )
                moved.append(jnp.where(hit, origin, block))
            blocks = moved
            where = jnp.where(hit, movers[step, partner], where)
            group = jnp.where(hit, partner, group)
        traced.append((last, lengths[group, where], blocks))
    for slot in range(requests):
        last, count, blocks = traced[slot]
        rank = jnp.int32(0)
        for other in range(requests):
            if other != slot:
                ahead = traced[other][0] * requests + other < last * requests + slot
                rank = rank + ahead.astype(jnp.int32)
        plan[at.slot + rank] = jnp.int32(slot)
        plan[at.last + rank] = last
        plan[at.count + rank] = count
        for b in range(nblocks):
            plan[at.perm + rank * nblocks + b] = blocks[b]
            plan[at.home + rank * nblocks + blocks[b]] = jnp.int32(b)
    for step in range(matchings):
        mover = movers[step, here]
        source = jnp.int32(-1)
        for earlier in range(step):
            source = jnp.where(movers[earlier, here] == mover, earlier, source)
        plan[at.mover + step] = mover
        plan[at.source + step] = source
    for copy in copies:
        copy.wait()


def pick_kernel(at, step, plan, *refs):
    sources, (key_out, value_out), sems = refs[: 2 * step + 2], refs[-3:-1], refs[-1]
    mover, source = plan[at.mover + step], plan[at.source + step]
    for code in range(-1, step):
        pair = sources[2 * code + 2 : 2 * code + 4]

        @pl.when(source == code)
        def _():
            views = [ref.at[0, mover] for ref in pair] if code < 0 else pair
            copies = [
                pltpu.make_async_copy(view, out, sems.at[n])
                for n, (view, out) in enumerate(zip(views, (key_out, value_out)))
            ]
            for copy in copies:
                copy.start()
            for copy in copies:
                copy.wait()


def settle_kernel(at, ready, plan, *refs):
    sources, (keys_after, values_after), sems = refs[:-3], refs[-3:-1], refs[-1]
    _, requests, segment, _ = keys_after.shape
    nblocks = (at.home - at.perm) // requests
    rows = segment // nblocks
    for position in range(requests):
        slot, last = plan[at.slot + position], plan[at.last + position]
        for code in range(-1, ready[position] + 1):
            pair = sources[2 * code + 2 : 2 * code + 4]

            @pl.when(last == code)
            def _():
                views = [ref.at[0, slot] for ref in pair] if code < 0 else pair
                for n, (view, out) in enumerate(zip(views, (keys_after, values_after))):
                    for b in range(nblocks):
                        origin = plan[at.perm + position * nblocks + b]
                        begin = pl.multiple_of(origin * rows, rows)
                        pltpu.make_async_copy(
                            view.at[pl.ds(begin, rows)],
                            out.at[0, slot, pl.ds(b * rows, rows)],
                            sems.at[n, position],
                        ).start()

    for position in range(requests):
        for n, out in enumerate((keys_after, values_after)):
            whole = out.at[0, plan[at.slot + position]]
            pltpu.make_async_copy(whole, whole, sems.at[n, position]).wait()


def attend_kernel(at, positions, ready, width, tokens, plan, *refs):
    count = len(positions)
    q_refs, refs = refs[:width], refs[width:]
    (new_k, new_v), refs = refs[:2], refs[2:]
    outs, (kbuf, vbuf, qbuf, sems) = refs[-4 - width : -4], refs[-4:]
    sources = refs[: -4 - width]
    requests, local_new, features = new_k.shape
    segment = kbuf.shape[1] - LANES
    nblocks = (at.home - at.perm) // requests
    rows = segment // nblocks
    own = q_refs[0].shape[3] // HD
    shared = own * width * HD // features
    kv_own = own // shared
    place = plan[at.place]
    fresh = local_new_of(tokens, width)

    for n, position in enumerate(positions):
        slot, last = plan[at.slot + position], plan[at.last + position]
        for code in range(-1, ready[position] + 1):
            pair = sources[2 * code + 2 : 2 * code + 4]

            @pl.when(last == code)
            def _():
                views = [ref.at[0, slot] for ref in pair] if code < 0 else pair
                for view, buf, sem in zip(views, (kbuf, vbuf), (0, 1)):
                    pltpu.make_async_copy(
                        view, buf.at[n, pl.ds(0, segment)], sems.at[sem, n]
                    ).start()

        for i in range(width):
            pltpu.make_async_copy(q_refs[i].at[0, slot], qbuf.at[n, i], sems.at[2, n]).start()

    for n, position in enumerate(positions):
        slot = plan[at.slot + position]
        for buf, new in ((kbuf, new_k), (vbuf, new_v)):
            buf[n, segment:, :] = jnp.zeros((LANES, features), BF16)
            buf[n, segment : segment + local_new, :] = new[slot]

    lane = lax.broadcasted_iota(jnp.int32, (1, LANES), 1)
    queries = shared * tokens
    token = lax.broadcasted_iota(jnp.int32, (queries, LANES), 0) % tokens
    column = lax.broadcasted_iota(jnp.int32, (queries, LANES), 1)
    allowed = jnp.logical_and(column < fresh, column + place * fresh <= token)
    new_bias = jnp.where(allowed, 0.0, MASKED).astype(F32)
    stat_lane = lax.broadcasted_iota(jnp.int32, (tokens, LANES), 1)
    scale = math.log2(math.e) / HD**0.5

    for n, position in enumerate(positions):
        length = plan[at.count + position]
        biases = []
        for b in range(nblocks):
            home = plan[at.home + position * nblocks + b]
            limit = length - place * segment - home * rows
            for part in range(rows // LANES):
                biases.append(jnp.where(lane + part * LANES < limit, 0.0, MASKED).astype(F32))
        bias = jnp.concatenate(biases, axis=1)
        for buf, sem in ((kbuf, 0), (vbuf, 1)):
            view = buf.at[n, pl.ds(0, segment)]
            pltpu.make_async_copy(view, view, sems.at[sem, n]).wait()
        pltpu.make_async_copy(qbuf.at[n], qbuf.at[n], sems.at[2, n]).wait()
        for i in range(width):
            tops = jnp.zeros((tokens, LANES), F32)
            totals = jnp.zeros((tokens, LANES), F32)
            for j in range(kv_own):
                head = (place ^ i) * kv_own + j
                cols = pl.ds(pl.multiple_of(head * HD, HD), HD)
                base = j * shared * HD
                asked = jnp.concatenate(
                    [
                        qbuf[n, i, :, base + s * HD : base + (s + 1) * HD]
                        for s in range(shared)
                    ],
                    axis=0,
                )
                scores = lax.dot_general(
                    asked,
                    kbuf[n, :, cols],
                    (((1,), (1,)), ((), ())),
                    preferred_element_type=F32,
                )
                older = scores[:, :segment] * scale + bias
                newer = scores[:, segment:] * scale + new_bias
                top = jnp.maximum(
                    jnp.max(older, axis=1, keepdims=True),
                    jnp.max(newer, axis=1, keepdims=True),
                )
                top = jnp.maximum(top, FLOOR)
                older = jnp.exp2(older - top)
                newer = jnp.exp2(newer - top)
                total = jnp.sum(older, axis=1, keepdims=True) + jnp.sum(
                    newer, axis=1, keepdims=True
                )
                weights = jnp.concatenate([older.astype(BF16), newer.astype(BF16)], axis=1)
                summed = jnp.dot(
                    weights, vbuf[n, :, cols], preferred_element_type=F32
                ).astype(BF16)
                for s in range(shared):
                    part = slice(s * tokens, (s + 1) * tokens)
                    outs[i][n, :, base + s * HD : base + (s + 1) * HD] = summed[part]
                    chosen = stat_lane == j * shared + s
                    tops = jnp.where(chosen, top[part], tops)
                    totals = jnp.where(chosen, total[part], totals)
            outs[i][n, :, own * HD :] = pack_stats(tops, totals, own).astype(BF16)


def local_new_of(tokens, width):
    return tokens // width


def split(value, parts):
    result = []
    for _ in range(parts):
        result.append(value.astype(BF16).astype(F32))
        value = value - result[-1]
    return result


def pack_stats(tops, totals, own):
    packed = jnp.zeros_like(tops)
    for n, part in enumerate(split(tops, 3) + split(totals, 2)):
        packed = packed + (pltpu.roll(part, n * own, 1) if n else part)
    return packed


def unpack_stats(packed, own):
    parts = [pltpu.roll(packed, LANES - n * own, 1) if n else packed for n in range(5)]
    return (parts[0] + parts[1]) + parts[2], parts[3] + parts[4]


def combine_kernel(at, width, lots, plan, *refs):
    out = refs[-1]
    own = out.shape[3] // HD
    for lot, positions in enumerate(lots):
        pieces = refs[lot * width : (lot + 1) * width]
        for n, position in enumerate(positions):
            slot = plan[at.slot + position]
            stats = [
                unpack_stats(piece[n, :, own * HD :].astype(F32), own) for piece in pieces
            ]
            peak = functools.reduce(jnp.maximum, [top for top, _ in stats])
            factors = [jnp.exp2(top - peak) for top, _ in stats]
            denom = sum(total * factor for (_, total), factor in zip(stats, factors))
            shares = [factor / denom for factor in factors]
            for h in range(own):
                cols = slice(h * HD, (h + 1) * HD)
                mixed = sum(
                    piece[n, :, cols].astype(F32) * share[:, h : h + 1]
                    for piece, share in zip(pieces, shares)
                )
                out[0, slot, :, cols] = mixed.astype(BF16)


def shards(
    query, cache_keys, cache_values, new_keys, new_values, masks, movers, block_lists, lengths
):
    groups = lax.axis_size("group")
    width = lax.axis_size("ctx")
    _, requests, segment, features = cache_keys.shape
    tokens = query.shape[2]
    matchings, _, nblocks = block_lists.shape
    own = query.shape[3] // HD
    at = Layout(requests, nblocks, matchings)
    ready = [max(-1, n - (requests - matchings)) for n in range(requests)]
    request = jax.ShapeDtypeStruct((segment, features), BF16)
    big = pltpu.CompilerParams(vmem_limit_bytes=48 * 1024 * 1024)
    request_bytes = 2 * segment * features * 2

    plan, moving_keys, moving_values = pl.pallas_call(
        functools.partial(plan_kernel, at),
        out_shape=(jax.ShapeDtypeStruct((at.size,), jnp.int32), request, request),
        in_specs=[SMEM] * 4 + [ANY] * 2,
        out_specs=(SMEM, ANY, ANY),
        scratch_shapes=[pltpu.SemaphoreType.DMA((2,))],
        name="plan",
    )(masks, movers, block_lists, lengths, cache_keys, cache_values)

    def pick(step, sources):
        return pl.pallas_call(
            functools.partial(pick_kernel, at, step),
            out_shape=(request, request),
            in_specs=[SMEM] + [ANY] * (2 * step + 2),
            out_specs=(ANY, ANY),
            scratch_shapes=[pltpu.SemaphoreType.DMA((2,))],
            cost_estimate=pl.CostEstimate(
                flops=0, bytes_accessed=2 * request_bytes, transcendentals=0
            ),
            name=f"pick_{step}",
        )(plan, *sources[: 2 * step + 2])

    def attend(positions, asked, fresh, sources):
        count = len(positions)
        used = 2 * (max(ready[n] for n in positions) + 2)
        rows = own * width * tokens * count
        results = pl.pallas_call(
            functools.partial(attend_kernel, at, positions, ready, width, tokens),
            out_shape=[jax.ShapeDtypeStruct((count, tokens, own * HD + LANES), BF16)] * width,
            in_specs=[SMEM] + [ANY] * width + [VMEM] * 2 + [ANY] * used,
            out_specs=[VMEM] * width,
            scratch_shapes=[
                pltpu.VMEM((count, segment + LANES, features), BF16),
                pltpu.VMEM((count, segment + LANES, features), BF16),
                pltpu.VMEM((count, width, tokens, own * HD), BF16),
                pltpu.SemaphoreType.DMA((3, count)),
            ],
            compiler_params=big,
            cost_estimate=pl.CostEstimate(
                flops=4 * rows * segment * HD,
                bytes_accessed=count * request_bytes,
                transcendentals=rows * segment,
            ),
            name="attend_" + "_".join(map(str, positions)),
        )(plan, *asked, *fresh, *sources[:used])
        return results

    def send_home(results):
        return [results[0]] + [exchange(results[i], "ctx", i) for i in range(1, width)]

    def ask():
        return [query] + [exchange(query, "ctx", i) for i in range(1, width)]

    def pad_new():
        rows = new_keys.shape[2]
        extra = -rows % 16
        return [jnp.pad(new[0], ((0, 0), (0, extra), (0, 0))) for new in (new_keys, new_values)]

    sources = [cache_keys, cache_values]
    lots, pieces = [], []
    asked = fresh = None
    for step in range(matchings):
        if step:
            moving_keys, moving_values = pick(step, sources)
        positions = [n for n in range(requests) if ready[n] == step - 1 or (step == 1 and ready[n] < 0)]

        def branch(mask, moved, state):
            arrived = [exchange(block, "group", mask) for block in moved]
            if step == 0:
                return arrived, ask(), pad_new()
            asked, fresh, sources = state
            return arrived, send_home(attend(positions, asked, fresh, sources))

        result = lax.switch(
            masks[step] - 1,
            [functools.partial(branch, mask) for mask in range(1, groups)],
            [moving_keys, moving_values],
            (asked, fresh, sources),
        )
        sources = sources + result[0]
        if step == 0:
            asked, fresh = result[1:]
        else:
            lots.append(positions)
            pieces += result[1]

    positions = [n for n in range(requests) if ready[n] == matchings - 1]
    lots.append(positions)
    pieces += send_home(attend(positions, asked, fresh, sources))

    keys_after, values_after = pl.pallas_call(
        functools.partial(settle_kernel, at, ready),
        out_shape=[jax.ShapeDtypeStruct(cache_keys.shape, BF16)] * 2,
        in_specs=[SMEM] + [ANY] * len(sources),
        out_specs=[ANY, ANY],
        scratch_shapes=[pltpu.SemaphoreType.DMA((2, requests))],
        cost_estimate=pl.CostEstimate(
            flops=0, bytes_accessed=2 * requests * request_bytes, transcendentals=0
        ),
        name="settle",
    )(plan, *sources)

    attended = pl.pallas_call(
        functools.partial(combine_kernel, at, width, lots),
        out_shape=jax.ShapeDtypeStruct(query.shape, BF16),
        in_specs=[SMEM] + [VMEM] * len(pieces),
        out_specs=VMEM,
        compiler_params=big,
        name="combine",
    )(plan, *pieces)
    return attended, keys_after, values_after


def solution(mesh):
    placed = (
        P("group", None, None, "ctx"),
        P("group", None, "ctx", None),
        P("group", None, "ctx", None),
        P("group", None, "ctx", None),
        P("group", None, "ctx", None),
        P(),
        P(),
        P(),
        P(),
    )
    return jax.shard_map(
        shards,
        mesh=mesh,
        in_specs=placed,
        out_specs=(
            P("group", None, None, "ctx"),
            P("group", None, "ctx", None),
            P("group", None, "ctx", None),
        ),
        check_vma=False,
    )
```

time: 576 us -> 469 us (0.81)
  Pallas kernels: 0 us -> 288 us
  waiting for transfers between devices: 348 us -> 112 us
  local copies, waits for them, and re-layouts: 91.6 us -> 4.11 us
  other arithmetic: 56.6 us -> 0 us
  loops' own time: 0.35 us -> 28.2 us
  between operations: 25.7 us -> 2.97 us
  blocking collectives: 21 us -> 0 us
  matrix products: 19.6 us -> 0 us
  starting transfers between devices: 11.1 us -> 25.8 us
    pallas_call x0 -> x8, Pallas kernels: none -> 288 us  [the longest x1 256 us: shards(): pl.pallas_call(functools.partial(settle_kernel, at, ready), out_shape=[ja...]
    ppermute x9 -> x18, waiting for transfers between devices: 268 us -> 112 us  [exchange(): lax.ppermute(block, axis, [(i, i ^ mask) for i in range(lax.axis_size(axi...]
    reduce_scatter x2 -> x0, waiting for transfers between devices: 80.1 us -> none  [the longest x1 76 us: shards(): lax.psum_scatter(scaled, 'ctx', scatter_dimension=2, tiled=True)]
    select_n x19 -> x0, other arithmetic: 32.7 us -> none  [the longest x9 25.4 us: route_blocks(): current = jnp.where(flag, swapped, current)]
    dynamic_slice x25 -> x0, local copies, waits for them, and re-layouts: 28.6 us -> none  [the longest x16 20 us: shards(): lax.map(partial_attention, (gathered, keys, values, new_keys[0], new_valu...]
    another operation x1 -> x3, loops' own time: 0.35 us -> 28.2 us  [shards(): lax.switch(masks[step] - 1, [functools.partial(branch, mask) for mask in...]
    pmax x1 -> x0, blocking collectives: 21 us -> none  [shards(): peak = lax.pmax(top, 'ctx')]
    dot_general x16 -> x0, matrix products: 19.6 us -> none  [the longest x4 6.15 us: partial_attention(): jnp.einsum('tkgd,skd->kgts', heads_q, fresh_keys.reshape(local_new, kv_he...]
  transfers between devices with their start and end apart: 12 -> 18, of which waited for: 11 -> 9; matrix products, arithmetic and copies ran while one was open for 7% -> 0% of each run, Pallas kernels for 0% -> 59%
where the time goes in v1:
time: 469 us; the launch traced here: 462 us
  Pallas kernels  288 us (61%)
  waiting for transfers between devices  112 us (24%)
  loops' own time  28.2 us (6%)
  starting transfers between devices  25.8 us (6%)
    pallas_call x1, Pallas kernels, shards(): pl.pallas_call(functools.partial(settle_kernel, at, ready), out_shape=[ja...  256 us
    ppermute x18, waiting for transfers between devices, exchange(): lax.ppermute(block, axis, [(i, i ^ mask) for i in range(lax.axis_size(axi...  112 us
    another operation x3, loops' own time, shards(): lax.switch(masks[step] - 1, [functools.partial(branch, mask) for mask in...  28.2 us
    ppermute x18, starting transfers between devices, exchange(): lax.ppermute(block, axis, [(i, i ^ mask) for i in range(lax.axis_size(axi...  25.8 us
    pallas_call x3, Pallas kernels, attend(): pl.pallas_call(functools.partial(attend_kernel, at, positions, ready, wid...  20.3 us
  transfers between devices with their start and end apart: 18, of which 9 were waited for; matrix products, arithmetic and copies ran while one was open for 0% of the time, Pallas kernels for 59%

profile of v1, /device:TPU:0, one launch (start us, length us, event | category | flops | bytes accessed | tf_op | source)
XLA Modules:
  0.0 461.5 jit_solution(17438874188050303982)
XLA Ops:
  0.6 1.4 fusion
  3.9 1.4 copy.13.lengths
  5.3 1.4 copy.12.lists
  6.7 3.3 plan.1
  10.0 51.5 %conditional.3 = (bf16[512,1024]{1,0:T(8,128)(2,1)}, bf16[512,1024]{1,0:T(8,128)(2,1)}, bf16[1,4,32,2048]{3,2,1,0:T(8,128)(2,1)}, bf16[1,4,32,2048]{3,2,1,0:T(8,...) conditional(s32[]{:T(128)} %bitcast.15, ...), branch_computations={%region_0.1_spmd, %region_1.2_spmd, %region_2.3_spmd, %region_3.4_... | conditional | bytes 15073540 | solution.py:386
  10.1 3.0 collective-permute-start.15
  13.2 4.0 collective-permute-start.19
  17.8 12.4 %collective-permute-done.19 = bf16[1,4,32,2048]{3,2,1,0:T(8,128)(2,1)} collective-permute-done((bf16[1,4,32,2048]{3,2,1,0:T(8,128)(2,1)S(1)}, bf16[1,4,32,2048]{3,2,1,0:T(8,128)(2,1)}, u32[]{:S(2)}, u32[]{:S(2)}) %collective-permute-start.19) | collective-permute-done | bytes 524320 | tf_op jit(solution)/shard_map/cond/branch_3_fun/ppermute | solution.py:23
  30.3 31.3 %collective-permute-done.18 = bf16[1,4,32,2048]{3,2,1,0:T(8,128)(2,1)} collective-permute-done((bf16[1,4,32,2048]{3,2,1,0:T(8,128)(2,1)S(1)}, bf16[1,4,32,2048]{3,2,1,0:T(8,128)(2,1)}, u32[]{:S(2)}, u32[]{:S(2)}) %collective-permute-start.18) | collective-permute-done | bytes 524320 | tf_op jit(solution)/shard_map/cond/branch_3_fun/ppermute | solution.py:23
  61.6 2.1 pick_1.1
  63.7 67.2 %conditional.4 = (bf16[512,1024]{1,0:T(8,128)(2,1)}, bf16[512,1024]{1,0:T(8,128)(2,1)}, bf16[2,32,2176]{2,1,0:T(8,128)(2,1)S(1)}, bf16[2,32,2176]{2,1,0:T(8,128)...) conditional(s32[]{:T(128)} %bitcast.14, ...), branch_computations={%region_7.8_spmd, %region_8.9_spmd, %region_9.10_spmd, %region_10.... | conditional | flops 1073741824 | bytes 15925496 | solution.py:386
  69.7 1.5 collective-permute-start.46
  71.2 9.0 %attend_0_1.9 = (bf16[2,32,2176]{2,1,0:T(8,128)(2,1)S(1)}, bf16[2,32,2176]{2,1,0:T(8,128)(2,1)S(1)}, bf16[2,32,2176]{2,1,0:T(8,128)(2,1)S(1)}, bf16[2,32,2176]{2,1,0:T(8,128)(2,1)S(1)}) custom-call(s32[51]{0:T(128)S(1)} %get-tuple-element.533.plan, bf16[1,4,32,2048]{3,2,1,0:T(8,128)(2,1)S(1)} %get-tuple-element.534.refs_0_, ...), custom_call_target="tpu_custom_call" | custom-call | flops 1073741824 | bytes 4194304 | tf_op jit(solution)/shard_map/cond/branch_2_fun/attend_0_1/pallas_call | solution.py:339
  80.4 3.0 collective-permute-start.48
  83.4 1.3 collective-permute-start.49
  84.7 9.6 %collective-permute-done.47 = bf16[2,32,2176]{2,1,0:T(8,128)(2,1)} collective-permute-done((bf16[2,32,2176]{2,1,0:T(8,128)(2,1)S(1)}, bf16[2,32,2176]{2,1,0:T(8,128)(2,1)}, u32[]{:S(2)}, u32[]{:S(2)}) %collective-permute-start.47) | collective-permute-done | bytes 278560 | tf_op jit(solution)/shard_map/cond/branch_2_fun/ppermute | solution.py:23
  94.3 8.6 %collective-permute-done.48 = bf16[2,32,2176]{2,1,0:T(8,128)(2,1)} collective-permute-done((bf16[2,32,2176]{2,1,0:T(8,128)(2,1)S(1)}, bf16[2,32,2176]{2,1,0:T(8,128)(2,1)}, u32[]{:S(2)}, u32[]{:S(2)}) %collective-permute-start.48) | collective-permute-done | bytes 278560 | tf_op jit(solution)/shard_map/cond/branch_2_fun/ppermute | solution.py:23
  103.0 14.5 %collective-permute-done.46 = bf16[512,1024]{1,0:T(8,128)(2,1)} collective-permute-done((bf16[512,1024]{1,0:T(8,128)(2,1)S(1)}, bf16[512,1024]{1,0:T(8,128)(2,1)}, u32[]{:S(2)}, u32[]{:S(2)}) %collective-permute-start.46) | collective-permute-done | bytes 1048608 | tf_op jit(solution)/shard_map/cond/branch_2_fun/ppermute | solution.py:23
  130.9 2.1 pick_2.1
  133.0 57.7 %conditional.5 = (bf16[512,1024]{1,0:T(8,128)(2,1)}, bf16[512,1024]{1,0:T(8,128)(2,1)}, bf16[1,32,2176]{2,1,0:T(8,128)(2,1)S(1)}, bf16[1,32,2176]{2,1,0:T(8,128)...) conditional(s32[]{:T(128)} %bitcast.16, ...), branch_computations={%region_14.15_spmd, %region_15.16_spmd, %region_16.17_spmd, %regio... | conditional | flops 536870912 | bytes 12157176 | solution.py:386
  141.8 1.8 collective-permute-start.95
  144.7 5.6 %attend_2.12 = (bf16[1,32,2176]{2,1,0:T(8,128)(2,1)S(1)}, bf16[1,32,2176]{2,1,0:T(8,128)(2,1)S(1)}, bf16[1,32,2176]{2,1,0:T(8,128)(2,1)S(1)}, bf16[1,32,2176]{2,1,0:T(8,128)(2,1)S(1)}) custom-call(s32[51]{0:T(128)S(1)} %get-tuple-element.713.plan, bf16[1,4,32,2048]{3,2,1,0:T(8,128)(2,1)S(1)} %get-tuple-element.714.refs_0_, ...), custom_call_target="tpu_custom_call" | custom-call | flops 536870912 | bytes 2097152 | tf_op jit(solution)/shard_map/cond/branch_5_fun/attend_2/pallas_call | solution.py:339
  150.4 3.0 collective-permute-start.98
  153.5 1.3 collective-permute-start.99
  154.8 3.0 collective-permute-done.97
  157.8 6.3 %collective-permute-done.98 = bf16[1,32,2176]{2,1,0:T(8,128)(2,1)} collective-permute-done((bf16[1,32,2176]{2,1,0:T(8,128)(2,1)S(1)}, bf16[1,32,2176]{2,1,0:T(8,128)(2,1)}, u32[]{:S(2)}, u32[]{:S(2)}) %collective-permute-start.98) | collective-permute-done | bytes 139296 | tf_op jit(solution)/shard_map/cond/branch_5_fun/ppermute | solution.py:23
  164.1 4.7 %collective-permute-done.95 = bf16[512,1024]{1,0:T(8,128)(2,1)} collective-permute-done((bf16[512,1024]{1,0:T(8,128)(2,1)S(1)}, bf16[512,1024]{1,0:T(8,128)(2,1)}, u32[]{:S(2)}, u32[]{:S(2)}) %collective-permute-start.95) | collective-permute-done | bytes 1048608 | tf_op jit(solution)/shard_map/cond/branch_5_fun/ppermute | solution.py:23
  168.8 21.6 %collective-permute-done.96 = bf16[512,1024]{1,0:T(8,128)(2,1)} collective-permute-done((bf16[512,1024]{1,0:T(8,128)(2,1)S(1)}, bf16[512,1024]{1,0:T(8,128)(2,1)}, u32[]{:S(2)}, u32[]{:S(2)}) %collective-permute-start.96) | collective-permute-done | bytes 1048608 | tf_op jit(solution)/shard_map/cond/branch_5_fun/ppermute | solution.py:23
  190.7 5.6 %attend_3.1 = (bf16[1,32,2176]{2,1,0:T(8,128)(2,1)S(1)}, bf16[1,32,2176]{2,1,0:T(8,128)(2,1)S(1)}, bf16[1,32,2176]{2,1,0:T(8,128)(2,1)S(1)}, bf16[1,32,2176]{2,1,0:T(8,128)(2,1)S(1)}) custom-call(s32[51]{0:T(128)S(1)} %get-tuple-element.784.plan, bf16[1,4,32,2048]{3,2,1,0:T(8,128)(2,1)S(1)} %copy-done, bf16[1,4,32,2048]{3,2,1,0:T(8,128)(2,1)} %get-tuple-element.791.refs_1_, ...), custom_call_target="tpu_custom_call" | custom-call | flops 536870912 | bytes 2097152 | tf_op jit(solution)/shard_map/attend_3/pallas_call | solution.py:339
  196.4 3.0 collective-permute-start.106
  200.8 255.8 %settle.1 = (bf16[1,4,512,1024]{3,2,1,0:T(8,128)(2,1)}, bf16[1,4,512,1024]{3,2,1,0:T(8,128)(2,1)}) custom-call(s32[51]{0:T(128)S(1)} %get-tuple-element.784.plan, bf16[1,4,512,1024]{3,2,1,0:T(8,128)(2,1)} %refs_0_.7, bf16[1,4,512,1024]{3,2,1,0:T(8,128)(2,1)} %refs_1_.5, bf16[512,1024]{1,0:T(8,128)(2,1)} %get-tuple-element.787.refs_2_.refs_8_, ...), custom_call_target="tpu_custom_call" | custom-call | bytes 16777216 | tf_op jit(solution)/shard_map/settle/pallas_call | solution.py:403
  456.7 4.6 combine.1
  (26 shorter events, 3.7 us)
Async XLA Ops:
  6.7 3.3 copy-start
  6.7 3.4 copy-start.1
  6.7 3.4 copy-start.2
  10.1 51.5 %collective-permute-start.15 = (bf16[512,1024]{1,0:T(8,128)(2,1)S(1)}, bf16[512,1024]{1,0:T(8,128)(2,1)}, u32[]{:S(2)}, u32[]{:S(2)}) collective-permute-start(bf16[512,1024]{1,0:T(8,128)(2,1)S(1)} %get-tuple-element.477), channel_id=1, source_target_pairs={{0,16},{4,20},{8,24},{12,28},{16,0},{20,4},{24,8},{28,12},{1,17},{... | collective-permute-start | bytes 3145736 | tf_op jit(solution)/shard_map/cond/branch_3_fun/ppermute | solution.py:23
  13.1 48.4 %collective-permute-start.16 = (bf16[512,1024]{1,0:T(8,128)(2,1)S(1)}, bf16[512,1024]{1,0:T(8,128)(2,1)}, u32[]{:S(2)}, u32[]{:S(2)}) collective-permute-start(bf16[512,1024]{1,0:T(8,128)(2,1)S(1)} %get-tuple-element.478), channel_id=1, source_target_pairs={{0,16},{4,20},{8,24},{12,28},{16,0},{20,4},{24,8},{28,12},{1,17},{... | collective-permute-start | bytes 3145736 | tf_op jit(solution)/shard_map/cond/branch_3_fun/ppermute | solution.py:23
  13.2 17.1 %collective-permute-start.19 = (bf16[1,4,32,2048]{3,2,1,0:T(8,128)(2,1)S(1)}, bf16[1,4,32,2048]{3,2,1,0:T(8,128)(2,1)}, u32[]{:S(2)}, u32[]{:S(2)}) collective-permute-start(bf16[1,4,32,2048]{3,2,1,0:T(8,128)(2,1)S(1)} %get-tuple-element.479), channel_id=1, source_target_pairs={{0,3},{1,2},{2,1},{3,0},{4,7},{5,6},{6,5},{7,4},{8,11},{9,10},{10,... | collective-permute-start | bytes 1572872 | tf_op jit(solution)/shard_map/cond/branch_3_fun/ppermute | solution.py:23
  17.2 44.3 %collective-permute-start.18 = (bf16[1,4,32,2048]{3,2,1,0:T(8,128)(2,1)S(1)}, bf16[1,4,32,2048]{3,2,1,0:T(8,128)(2,1)}, u32[]{:S(2)}, u32[]{:S(2)}) collective-permute-start(bf16[1,4,32,2048]{3,2,1,0:T(8,128)(2,1)S(1)} %get-tuple-element.479), channel_id=1, source_target_pairs={{0,2},{1,3},{2,0},{3,1},{4,6},{5,7},{6,4},{7,5},{8,10},{9,11},{10,... | collective-permute-start | bytes 1572872 | tf_op jit(solution)/shard_map/cond/branch_3_fun/ppermute | solution.py:23
  17.2 44.3 %collective-permute-start.17 = (bf16[1,4,32,2048]{3,2,1,0:T(8,128)(2,1)S(1)}, bf16[1,4,32,2048]{3,2,1,0:T(8,128)(2,1)}, u32[]{:S(2)}, u32[]{:S(2)}) collective-permute-start(bf16[1,4,32,2048]{3,2,1,0:T(8,128)(2,1)S(1)} %get-tuple-element.479), channel_id=1, source_target_pairs={{0,1},{1,0},{2,3},{3,2},{4,5},{5,4},{6,7},{7,6},{8,9},{9,8},{10,11... | collective-permute-start | bytes 1572872 | tf_op jit(solution)/shard_map/cond/branch_3_fun/ppermute | solution.py:23
  69.4 33.5 %collective-permute-start.45 = (bf16[512,1024]{1,0:T(8,128)(2,1)S(1)}, bf16[512,1024]{1,0:T(8,128)(2,1)}, u32[]{:S(2)}, u32[]{:S(2)}) collective-permute-start(bf16[512,1024]{1,0:T(8,128)(2,1)S(1)} %get-tuple-element.531), channel_id=1, source_target_pairs={{0,12},{4,8},{8,4},{12,0},{16,28},{20,24},{24,20},{28,16},{1,13},{... | collective-permute-start | bytes 3145736 | tf_op jit(solution)/shard_map/cond/branch_2_fun/ppermute | solution.py:23
  69.7 47.8 %collective-permute-start.46 = (bf16[512,1024]{1,0:T(8,128)(2,1)S(1)}, bf16[512,1024]{1,0:T(8,128)(2,1)}, u32[]{:S(2)}, u32[]{:S(2)}) collective-permute-start(bf16[512,1024]{1,0:T(8,128)(2,1)S(1)} %get-tuple-element.532), channel_id=1, source_target_pairs={{0,12},{4,8},{8,4},{12,0},{16,28},{20,24},{24,20},{28,16},{1,13},{... | collective-permute-start | bytes 3145736 | tf_op jit(solution)/shard_map/cond/branch_2_fun/ppermute | solution.py:23
  80.3 14.0 %collective-permute-start.47 = (bf16[2,32,2176]{2,1,0:T(8,128)(2,1)S(1)}, bf16[2,32,2176]{2,1,0:T(8,128)(2,1)}, u32[]{:S(2)}, u32[]{:S(2)}) collective-permute-start(bf16[2,32,2176]{2,1,0:T(8,128)(2,1)S(1)} %get-tuple-element.545), channel_id=1, source_target_pairs={{0,1},{1,0},{2,3},{3,2},{4,5},{5,4},{6,7},{7,6},{8,9},{9,8},{10,11... | collective-permute-start | bytes 835592 | tf_op jit(solution)/shard_map/cond/branch_2_fun/ppermute | solution.py:23
  80.4 22.6 %collective-permute-start.48 = (bf16[2,32,2176]{2,1,0:T(8,128)(2,1)S(1)}, bf16[2,32,2176]{2,1,0:T(8,128)(2,1)}, u32[]{:S(2)}, u32[]{:S(2)}) collective-permute-start(bf16[2,32,2176]{2,1,0:T(8,128)(2,1)S(1)} %get-tuple-element.546), channel_id=1, source_target_pairs={{0,2},{1,3},{2,0},{3,1},{4,6},{5,7},{6,4},{7,5},{8,10},{9,11},{10,... | collective-permute-start | bytes 835592 | tf_op jit(solution)/shard_map/cond/branch_2_fun/ppermute | solution.py:23
  83.4 19.6 %collective-permute-start.49 = (bf16[2,32,2176]{2,1,0:T(8,128)(2,1)S(1)}, bf16[2,32,2176]{2,1,0:T(8,128)(2,1)}, u32[]{:S(2)}, u32[]{:S(2)}) collective-permute-start(bf16[2,32,2176]{2,1,0:T(8,128)(2,1)S(1)} %get-tuple-element.547), channel_id=1, source_target_pairs={{0,3},{1,2},{2,1},{3,0},{4,7},{5,6},{6,5},{7,4},{8,11},{9,10},{10,... | collective-permute-start | bytes 835592 | tf_op jit(solution)/shard_map/cond/branch_2_fun/ppermute | solution.py:23
  141.8 27.1 %collective-permute-start.95 = (bf16[512,1024]{1,0:T(8,128)(2,1)S(1)}, bf16[512,1024]{1,0:T(8,128)(2,1)}, u32[]{:S(2)}, u32[]{:S(2)}) collective-permute-start(bf16[512,1024]{1,0:T(8,128)(2,1)S(1)} %get-tuple-element.711), channel_id=1, source_target_pairs={{0,24},{4,28},{8,16},{12,20},{16,8},{20,12},{24,0},{28,4},{1,25},{... | collective-permute-start | bytes 3145736 | tf_op jit(solution)/shard_map/cond/branch_5_fun/ppermute | solution.py:23
  143.6 46.9 %collective-permute-start.96 = (bf16[512,1024]{1,0:T(8,128)(2,1)S(1)}, bf16[512,1024]{1,0:T(8,128)(2,1)}, u32[]{:S(2)}, u32[]{:S(2)}) collective-permute-start(bf16[512,1024]{1,0:T(8,128)(2,1)S(1)} %get-tuple-element.712), channel_id=1, source_target_pairs={{0,24},{4,28},{8,16},{12,20},{16,8},{20,12},{24,0},{28,4},{1,25},{... | collective-permute-start | bytes 3145736 | tf_op jit(solution)/shard_map/cond/branch_5_fun/ppermute | solution.py:23
  150.4 7.5 %collective-permute-start.97 = (bf16[1,32,2176]{2,1,0:T(8,128)(2,1)S(1)}, bf16[1,32,2176]{2,1,0:T(8,128)(2,1)}, u32[]{:S(2)}, u32[]{:S(2)}) collective-permute-start(bf16[1,32,2176]{2,1,0:T(8,128)(2,1)S(1)} %get-tuple-element.727), channel_id=1, source_target_pairs={{0,1},{1,0},{2,3},{3,2},{4,5},{5,4},{6,7},{7,6},{8,9},{9,8},{10,11... | collective-permute-start | bytes 417800 | tf_op jit(solution)/shard_map/cond/branch_5_fun/ppermute | solution.py:23
  150.4 13.7 %collective-permute-start.98 = (bf16[1,32,2176]{2,1,0:T(8,128)(2,1)S(1)}, bf16[1,32,2176]{2,1,0:T(8,128)(2,1)}, u32[]{:S(2)}, u32[]{:S(2)}) collective-permute-start(bf16[1,32,2176]{2,1,0:T(8,128)(2,1)S(1)} %get-tuple-element.728), channel_id=1, source_target_pairs={{0,2},{1,3},{2,0},{3,1},{4,6},{5,7},{6,4},{7,5},{8,10},{9,11},{10,... | collective-permute-start | bytes 417800 | tf_op jit(solution)/shard_map/cond/branch_5_fun/ppermute | solution.py:23
  153.5 10.7 %collective-permute-start.99 = (bf16[1,32,2176]{2,1,0:T(8,128)(2,1)S(1)}, bf16[1,32,2176]{2,1,0:T(8,128)(2,1)}, u32[]{:S(2)}, u32[]{:S(2)}) collective-permute-start(bf16[1,32,2176]{2,1,0:T(8,128)(2,1)S(1)} %get-tuple-element.729), channel_id=1, source_target_pairs={{0,3},{1,2},{2,1},{3,0},{4,7},{5,6},{6,5},{7,4},{8,11},{9,10},{10,... | collective-permute-start | bytes 417800 | tf_op jit(solution)/shard_map/cond/branch_5_fun/ppermute | solution.py:23
  196.3 260.3 %collective-permute-start.105 = (bf16[1,32,2176]{2,1,0:T(8,128)(2,1)S(1)}, bf16[1,32,2176]{2,1,0:T(8,128)(2,1)S(1)}, u32[]{:S(2)}, u32[]{:S(2)}) collective-permute-start(bf16[1,32,2176]{2,1,0:T(8,128)(2,1)S(1)} %get-tuple-element.811), channel_id=1, source_target_pairs={{0,1},{1,0},{2,3},{3,2},{4,5},{5,4},{6,7},{7,6},{8,9},{9,8},{10,11... | collective-permute-start | bytes 417800 | tf_op jit(solution)/shard_map/ppermute | solution.py:23
  196.4 260.2 %collective-permute-start.106 = (bf16[1,32,2176]{2,1,0:T(8,128)(2,1)S(1)}, bf16[1,32,2176]{2,1,0:T(8,128)(2,1)S(1)}, u32[]{:S(2)}, u32[]{:S(2)}) collective-permute-start(bf16[1,32,2176]{2,1,0:T(8,128)(2,1)S(1)} %get-tuple-element.812), channel_id=1, source_target_pairs={{0,2},{1,3},{2,0},{3,1},{4,6},{5,7},{6,4},{7,5},{8,10},{9,11},{10,... | collective-permute-start | bytes 417800 | tf_op jit(solution)/shard_map/ppermute | solution.py:23
  199.5 257.2 %collective-permute-start.107 = (bf16[1,32,2176]{2,1,0:T(8,128)(2,1)S(1)}, bf16[1,32,2176]{2,1,0:T(8,128)(2,1)S(1)}, u32[]{:S(2)}, u32[]{:S(2)}) collective-permute-start(bf16[1,32,2176]{2,1,0:T(8,128)(2,1)S(1)} %get-tuple-element.813), channel_id=1, source_target_pairs={{0,3},{1,2},{2,1},{3,0},{4,7},{5,6},{6,5},{7,4},{8,11},{9,10},{10,... | collective-permute-start | bytes 417800 | tf_op jit(solution)/shard_map/ppermute | solution.py:23

commit v2 on v0

v2 whole, which is shorter than its diff:
```python
import functools
import math

import jax
import jax.numpy as jnp
from jax import lax
from jax.experimental import pallas as pl
from jax.experimental.pallas import tpu as pltpu
from jax.sharding import PartitionSpec as P

HD = 128
LANES = 128
MASKED = -1e30
FLOOR = -1e29
BF16 = jnp.bfloat16
F32 = jnp.float32
ANY = pl.BlockSpec(memory_space=pl.ANY)
SMEM = pl.BlockSpec(memory_space=pltpu.SMEM)
VMEM = pl.BlockSpec(memory_space=pltpu.VMEM)


def exchange(block, axis, mask):
    return lax.ppermute(block, axis, [(i, i ^ mask) for i in range(lax.axis_size(axis))])


class Layout:
    def __init__(self, requests, nblocks, matchings):
        self.nblocks = nblocks
        self.slot = 0
        self.last = requests
        self.count = 2 * requests
        self.perm = 3 * requests
        self.home = self.perm + requests * nblocks
        self.mover = self.home + requests * nblocks
        self.source = self.mover + matchings
        self.place = self.source + matchings
        self.size = self.place + 1


def plan_kernel(
    at, masks, movers, lists, lengths, keys, values, plan, key_out, value_out, sems
):
    matchings, nblocks, _ = lists.shape
    requests = lengths.shape[0]
    here = lax.axis_index("group")
    first = movers[0, here]
    copies = [
        pltpu.make_async_copy(keys.at[0, first], key_out, sems.at[0]),
        pltpu.make_async_copy(values.at[0, first], value_out, sems.at[1]),
    ]
    for copy in copies:
        copy.start()
    plan[at.place] = lax.axis_index("ctx")
    traced = []
    for slot in range(requests):
        group, where = here, jnp.int32(slot)
        last = jnp.int32(-1)
        blocks = [jnp.int32(b) for b in range(nblocks)]
        for step in reversed(range(matchings)):
            hit = movers[step, group] == where
            partner = group ^ masks[step]
            last = jnp.where(jnp.logical_and(hit, last < 0), step, last)
            moved = []
            for block in blocks:
                origin = block
                for j in range(nblocks):
                    origin = jnp.where(
                        lists[step, j, group] == block, lists[step, j, partner], origin
                    )
                moved.append(jnp.where(hit, origin, block))
            blocks = moved
            where = jnp.where(hit, movers[step, partner], where)
            group = jnp.where(hit, partner, group)
        traced.append((last, lengths[where, group], blocks))
    for slot in range(requests):
        last, count, blocks = traced[slot]
        rank = jnp.int32(0)
        for other in range(requests):
            if other != slot:
                ahead = traced[other][0] * requests + other < last * requests + slot
                rank = rank + ahead.astype(jnp.int32)
        plan[at.slot + rank] = jnp.int32(slot)
        plan[at.last + rank] = last
        plan[at.count + rank] = count
        for b in range(nblocks):
            plan[at.perm + rank * nblocks + b] = blocks[b]
            plan[at.home + rank * nblocks + blocks[b]] = jnp.int32(b)
    for step in range(matchings):
        mover = movers[step, here]
        source = jnp.int32(-1)
        for earlier in range(step):
            source = jnp.where(movers[earlier, here] == mover, earlier, source)
        plan[at.mover + step] = mover
        plan[at.source + step] = source
    for copy in copies:
        copy.wait()


def pick_kernel(at, step, choices, plan, *refs):
    sources, outs, sems = refs[: 2 * step + 2], refs[-1 - len(choices) : -1], refs[-1]
    mover, source, place = plan[at.mover + step], plan[at.source + step], plan[at.place]
    for code in range(-1, step):

        @pl.when(source == code)
        def _():
            for c, (out, (kinds, pieces)) in enumerate(zip(outs, choices)):
                for m, kind in enumerate(kinds):
                    view = sources[2 * code + 2 + kind]
                    view = view.at[0, mover] if code < 0 else view
                    if pieces is None:
                        pltpu.make_async_copy(view, out, sems.at[c]).start()
                        continue
                    wide = out.shape[2] // len(pieces)
                    for p, piece in enumerate(pieces):
                        begin = pl.multiple_of((place ^ piece) * wide, wide)
                        pltpu.make_async_copy(
                            view.at[:, pl.ds(begin, wide)],
                            out.at[m, :, pl.ds(p * wide, wide)],
                            sems.at[c],
                        ).start()

    for c, out in enumerate(outs):
        pltpu.make_async_copy(out, out, sems.at[c]).wait()


def stage(at, plan, position, newest, sources, bufs, sems):
    rows = bufs[0].shape[0] // at.nblocks
    slot, last = plan[at.slot + position], plan[at.last + position]
    for code in range(-1, newest + 1):

        @pl.when(last == code)
        def _():
            views = sources[2 * code + 2 : 2 * code + 4]
            views = [view.at[0, slot] if code < 0 else view for view in views]

            def block(b, carry):
                begin = pl.multiple_of(plan[at.perm + position * at.nblocks + b] * rows, rows)
                into = pl.ds(pl.multiple_of(b * rows, rows), rows)
                for n in range(2):
                    pltpu.make_async_copy(
                        views[n].at[pl.ds(begin, rows)], bufs[n].at[into], sems[n]
                    ).start()
                return carry

            lax.fori_loop(0, at.nblocks, block, 0)


def settle_kernel(at, ready, plan, *refs):
    sources, outs, buf, sems = refs[:-4], refs[-4:-2], refs[-2], refs[-1]
    for position, newest in enumerate(ready):
        bufs = [buf.at[n, position] for n in range(2)]
        stage(at, plan, position, newest, sources, bufs, [sems.at[n, position] for n in range(2)])
    for position in range(len(ready)):
        slot = plan[at.slot + position]
        for n in range(2):
            view, sem = buf.at[n, position], sems.at[n, position]
            pltpu.make_async_copy(view, view, sem).wait()
            pltpu.make_async_copy(view, outs[n].at[0, slot], sem).start()
    for position in range(len(ready)):
        slot = plan[at.slot + position]
        for n in range(2):
            view, sem = buf.at[n, position], sems.at[n, position]
            pltpu.make_async_copy(view, outs[n].at[0, slot], sem).wait()


class Heads:
    def __init__(self, width, tokens, own, features, segment):
        self.width = width
        self.tokens = tokens
        self.own = own
        self.shared = own * width * HD // features
        self.kv_own = own // self.shared
        self.wide = self.kv_own * HD
        self.segment = segment


def place_new(new, slot, buf, spans):
    segment, rows = buf.shape[0] - LANES, new.shape[1]
    buf[segment:, :] = jnp.zeros((LANES, buf.shape[1]), BF16)
    for cols, origin in spans:
        buf[segment : segment + rows, cols] = new[slot, :, origin]


def new_bias_of(size, place):
    fresh = size.tokens // size.width
    queries = size.shared * size.tokens
    token = lax.broadcasted_iota(jnp.int32, (queries, LANES), 0) % size.tokens
    column = lax.broadcasted_iota(jnp.int32, (queries, LANES), 1)
    allowed = jnp.logical_and(column < fresh, column + place * fresh <= token)
    return jnp.where(allowed, 0.0, MASKED).astype(F32)


def bias_of(at, size, plan, position, place):
    lane = lax.broadcasted_iota(jnp.int32, (1, LANES), 1)
    length = plan[at.count + position]
    rows = size.segment // at.nblocks
    biases = []
    for b in range(at.nblocks):
        home = plan[at.home + position * at.nblocks + b]
        limit = length - place * size.segment - home * rows
        for part in range(rows // LANES):
            biases.append(jnp.where(lane + part * LANES < limit, 0.0, MASKED).astype(F32))
    return jnp.concatenate(biases, axis=1)


def attend_owner(size, asked, keys, values, column, bias, new_bias, out, unroll=False):
    tokens, shared, segment = size.tokens, size.shared, size.segment
    scale = math.log2(math.e) / HD**0.5
    stat_lane = lax.broadcasted_iota(jnp.int32, (tokens, LANES), 1)

    def head(j, stats):
        tops, totals = stats
        cols = pl.ds(pl.multiple_of(column + j * HD, HD), HD)
        spans = [
            pl.ds(pl.multiple_of((j * shared + s) * HD, HD), HD) for s in range(shared)
        ]
        scores = lax.dot_general(
            jnp.concatenate([asked[:, span] for span in spans], axis=0),
            keys[:, cols],
            (((1,), (1,)), ((), ())),
            preferred_element_type=F32,
        )
        older = scores[:, :segment] * scale + bias
        newer = scores[:, segment:] * scale + new_bias
        top = jnp.maximum(
            jnp.max(older, axis=1, keepdims=True), jnp.max(newer, axis=1, keepdims=True)
        )
        top = jnp.maximum(top, FLOOR)
        older = jnp.exp2(older - top)
        newer = jnp.exp2(newer - top)
        total = jnp.sum(older, axis=1, keepdims=True) + jnp.sum(newer, axis=1, keepdims=True)
        weights = jnp.concatenate([older.astype(BF16), newer.astype(BF16)], axis=1)
        summed = jnp.dot(weights, values[:, cols], preferred_element_type=F32).astype(BF16)
        for s, span in enumerate(spans):
            part = slice(s * tokens, (s + 1) * tokens)
            out[:, span] = summed[part]
            chosen = stat_lane == j * shared + s
            tops = jnp.where(chosen, top[part], tops)
            totals = jnp.where(chosen, total[part], totals)
        return tops, totals

    stats = (jnp.zeros((tokens, LANES), F32), jnp.zeros((tokens, LANES), F32))
    stats = lax.fori_loop(0, size.kv_own, head, stats, unroll=unroll)
    out[:, size.own * HD :] = pack_stats(*stats, size.own).astype(BF16)


def attend_kernel(at, size, first, newest, pieces, kinds, plan, *refs):
    count, some = len(newest), len(pieces)
    q_refs, (new_k, new_v), refs = refs[:some], refs[some : some + 2], refs[some + 2 :]
    outs, (kbuf, vbuf, qbuf, obuf, sems) = refs[-5 - some : -5], refs[-5:]
    sources = refs[: -5 - some]
    partial = kinds is not None
    place = plan[at.place]

    def start(view, buf, sem):
        pltpu.make_async_copy(view, buf.at[pl.ds(0, size.segment)], sem).start()

    for n in range(count):
        slot, last = plan[at.slot + first + n], plan[at.last + first + n]
        bufs = (kbuf.at[n], vbuf.at[n])
        if partial:
            for held, ref in zip(kinds, sources):
                for m, kind in enumerate(held):
                    start(ref.at[m], bufs[kind], sems.at[kind, n])
        else:
            for code in range(-1, newest[n] + 1):

                @pl.when(last == code)
                def _():
                    for m in range(2):
                        view = sources[2 * code + 2 + m]
                        start(view.at[0, slot] if code < 0 else view, bufs[m], sems.at[m, n])

        for p in range(some):
            pltpu.make_async_copy(q_refs[p].at[0, slot], qbuf.at[n, p], sems.at[2, n]).start()

    for n in range(count):
        slot = plan[at.slot + first + n]
        spans = [(slice(None), slice(None))]
        if partial:
            spans = [own_columns(size, place, p, piece) for p, piece in enumerate(pieces)]
        place_new(new_k, slot, kbuf.at[n], spans)
        place_new(new_v, slot, vbuf.at[n], spans)

    new_bias = new_bias_of(size, place)

    def request(n, carry):
        bias = bias_of(at, size, plan, first + n, place)
        for m, buf in enumerate((kbuf, vbuf)):
            view = buf.at[n, pl.ds(0, size.segment)]
            pltpu.make_async_copy(view, view, sems.at[m, n]).wait()
        pltpu.make_async_copy(qbuf.at[n], qbuf.at[n], sems.at[2, n]).wait()

        def owner(p, carry):
            column = p * size.wide if partial else (place ^ (p + pieces[0])) * size.wide
            attend_owner(
                size,
                qbuf.at[n, p],
                kbuf.at[n],
                vbuf.at[n],
                column,
                bias,
                new_bias,
                obuf.at[p, n],
            )
            return carry

        return lax.fori_loop(0, some, owner, carry)

    lax.fori_loop(0, count, request, 0)
    copies = [pltpu.make_async_copy(obuf.at[p], outs[p], sems.at[3, p]) for p in range(some)]
    for copy in copies:
        copy.start()
    for copy in copies:
        copy.wait()


def own_columns(size, place, p, piece):
    begin = pl.multiple_of((place ^ piece) * size.wide, size.wide)
    return pl.ds(p * size.wide, size.wide), pl.ds(begin, size.wide)


def split(value, parts):
    result = []
    for _ in range(parts):
        result.append(value.astype(BF16).astype(F32))
        value = value - result[-1]
    return result


def pack_stats(tops, totals, own):
    packed = jnp.zeros_like(tops)
    for n, part in enumerate(split(tops, 3) + split(totals, 2)):
        packed = packed + (pltpu.roll(part, n * own, 1) if n else part)
    return packed


def unpack_stats(packed, own):
    parts = [pltpu.roll(packed, LANES - n * own, 1) if n else packed for n in range(5)]
    return (parts[0] + parts[1]) + parts[2], parts[3] + parts[4]


def combined(pieces, heads, out):
    stats = [unpack_stats(piece[:, heads * HD :].astype(F32), heads) for piece in pieces]
    peak = functools.reduce(jnp.maximum, [top for top, _ in stats])
    factors = [jnp.exp2(top - peak) for top, _ in stats]
    denom = sum(total * factor for (_, total), factor in zip(stats, factors))
    shares = [factor / denom for factor in factors]
    for h in range(heads):
        cols = slice(h * HD, (h + 1) * HD)
        out[:, cols] = sum(
            piece[:, cols].astype(F32) * share[:, h : h + 1] for piece, share in zip(pieces, shares)
        ).astype(BF16)


def finish_kernel(at, size, parcels, lots, settled, ready, plan, *refs):
    count = sum(lots)
    some = len(parcels)
    arrived, refs = refs[:some], refs[some:]
    sources, refs = refs[: 2 * len(parcels_before(ready))], refs[2 * len(parcels_before(ready)) :]
    query, new_k, new_v = refs[:3]
    pieces, refs = refs[3:-13], refs[-11:]
    attended, after = refs[0], refs[1:3]
    kbuf, vbuf, qbuf, pbuf, full, sems, out_sems, in_sems = refs[3:]
    place, slot = plan[at.place], plan[at.slot + count]
    copies = [
        pltpu.make_async_copy(view, buf.at[pl.ds(0, size.segment)], in_sems.at[m])
        for m, (view, buf) in enumerate(zip(own_parcel(parcels, arrived), (kbuf, vbuf)))
    ]
    copies.append(pltpu.make_async_copy(query.at[0, slot], qbuf, in_sems.at[2]))
    for copy in copies:
        copy.start()
    before = 0
    for lot, each in enumerate([*lots, 1]):
        for i in range(size.width):
            if lot < len(lots) or i:
                piece = pieces[lot * size.width + i - lot // len(lots)]
                into = pbuf.at[i, pl.ds(before, each)]
                pltpu.make_async_copy(piece, into, in_sems.at[3]).start()
        before += each
    for position in range(settled, count):
        bufs = [full.at[n, position - settled] for n in range(2)]
        marks = [sems.at[n, position - settled] for n in range(2)]
        stage(at, plan, position, ready[position], sources, bufs, marks)
    rows = size.segment // at.nblocks

    def block(b, carry):
        begin = pl.multiple_of(plan[at.perm + count * at.nblocks + b] * rows, rows)
        into = pl.ds(pl.multiple_of(b * rows, rows), rows)
        for (kinds, parcel), ref in zip(parcels, arrived):
            for m, n in enumerate(kinds):
                for p, piece in enumerate(parcel):
                    cols, whole = own_columns(size, place, p, piece)
                    pltpu.make_async_copy(
                        ref.at[m, pl.ds(begin, rows), cols],
                        full.at[n, count - settled, into, whole],
                        sems.at[n, count - settled],
                    ).start()
        return carry

    lax.fori_loop(0, at.nblocks, block, 0)
    spans = [own_columns(size, place, 0, 0)]
    place_new(new_k, slot, kbuf, spans)
    place_new(new_v, slot, vbuf, spans)
    bias = bias_of(at, size, plan, count, place)
    new_bias = new_bias_of(size, place)
    for copy in copies:
        copy.wait()
    attend_owner(size, qbuf, kbuf, vbuf, 0, bias, new_bias, pbuf.at[0, count], True)
    for position in range(settled, count + 1):
        there = plan[at.slot + position]
        for n in range(2):
            view, sem = full.at[n, position - settled], sems.at[n, position - settled]
            pltpu.make_async_copy(view, view, sem).wait()
            pltpu.make_async_copy(
                view, after[n].at[0, there], out_sems.at[n, position - settled]
            ).start()
    theirs = (pbuf.at[0, pl.ds(0, count)], pbuf.at[pl.ds(1, size.width - 1)])
    for view in theirs:
        pltpu.make_async_copy(view, view, in_sems.at[3]).wait()

    def request(n, carry):
        parts = [pbuf.at[i, n] for i in range(size.width)]
        combined(parts, size.own, attended.at[0, plan[at.slot + n]])
        return carry

    lax.fori_loop(0, count + 1, request, 0)
    for position in range(settled, count + 1):
        there = plan[at.slot + position]
        for n in range(2):
            view = full.at[n, position - settled]
            pltpu.make_async_copy(
                view, after[n].at[0, there], out_sems.at[n, position - settled]
            ).wait()


def parcels_before(ready):
    return range(-1, max(ready))


def own_parcel(parcels, arrived):
    for n in range(2):
        for (kinds, parcel), ref in zip(parcels, arrived):
            if parcel == (0,) and n in kinds:
                yield ref.at[kinds.index(n)]


def shards(
    query, cache_keys, cache_values, new_keys, new_values, masks, movers, block_lists, lengths
):
    groups = lax.axis_size("group")
    width = lax.axis_size("ctx")
    _, requests, segment, features = cache_keys.shape
    tokens = query.shape[2]
    matchings, _, nblocks = block_lists.shape
    own = query.shape[3] // HD
    size = Heads(width, tokens, own, features, segment)
    at = Layout(requests, nblocks, matchings)
    ready = [max(-1, n - (requests - matchings)) for n in range(requests)]
    caches = (cache_keys, cache_values)
    big = pltpu.CompilerParams(vmem_limit_bytes=40 * 1024 * 1024)
    result = jax.ShapeDtypeStruct((tokens, own * HD + LANES), BF16)
    everyone = tuple(range(width))
    far, near = everyone[(width + 1) // 2 :], everyone[1 : (width + 1) // 2]
    parcels = [((0,), far), ((1,), far), ((0, 1), near), ((0, 1), (0,))]

    request = jax.ShapeDtypeStruct((segment, features), BF16)
    plan, *moving = pl.pallas_call(
        functools.partial(plan_kernel, at),
        out_shape=(jax.ShapeDtypeStruct((at.size,), jnp.int32), request, request),
        in_specs=[SMEM] * 4 + [ANY] * 2,
        out_specs=(SMEM, VMEM, VMEM),
        scratch_shapes=[pltpu.SemaphoreType.DMA((2,))],
        name="plan",
    )(masks, movers, block_lists.transpose(0, 2, 1), lengths.T, *caches)

    def lasting(microseconds):
        return pl.CostEstimate(
            flops=0, bytes_accessed=int(microseconds * 3.7e6), transcendentals=0
        )

    def pick(step, choices, sources, after=()):
        shapes = [
            (len(kinds), segment, len(pieces) * size.wide) if pieces else (segment, features)
            for kinds, pieces in choices
        ]
        wanted = {kind for kinds, _ in choices for kind in kinds}
        used = [
            sources[2 * n + (kind if kind in wanted else 1 - kind)]
            for n in range(step + 1)
            for kind in range(2)
        ]
        return pl.pallas_call(
            functools.partial(pick_kernel, at, step, choices),
            out_shape=[jax.ShapeDtypeStruct(shape, BF16) for shape in shapes],
            in_specs=[SMEM] + [ANY] * (len(used) + len(after)),
            out_specs=[VMEM] * len(choices),
            scratch_shapes=[pltpu.SemaphoreType.DMA((len(choices),))],
            cost_estimate=lasting(2.5),
            name=f"pick_{step}",
        )(plan, *used, *after)

    def attend(first, count, pieces, asked, fresh, sources, kinds=None, after=()):
        newest = ready[first : first + count]
        if kinds is None:
            sources = sources[: 2 * (max(newest) + 2)]
        held = sources[0].shape[-1]
        some = len(pieces)
        return pl.pallas_call(
            functools.partial(attend_kernel, at, size, first, newest, pieces, kinds),
            out_shape=[jax.ShapeDtypeStruct((count, *result.shape), BF16)] * some,
            in_specs=[SMEM] + [ANY] * some + [VMEM] * 2 + [ANY] * (len(sources) + len(after)),
            out_specs=[ANY] * some,
            scratch_shapes=[
                pltpu.VMEM((count, segment + LANES, held), BF16),
                pltpu.VMEM((count, segment + LANES, held), BF16),
                pltpu.VMEM((count, some, tokens, own * HD), BF16),
                pltpu.VMEM((some, count, *result.shape), BF16),
                pltpu.SemaphoreType.DMA((4, max(some, count))),
            ],
            compiler_params=big,
            cost_estimate=lasting(1 + 1.5 * some * count),
            name=f"attend_{first}_{count}_{some}",
        )(plan, *[asked[piece] for piece in pieces], *fresh, *sources, *after)

    def send_home(pieces, results):
        return [exchange(part, "ctx", piece) if piece else part for piece, part in zip(pieces, results)]

    def settle(positions, sources):
        count = len(positions)
        newest = [ready[n] for n in positions]
        used = sources[: 2 * (max(newest) + 2)]
        return pl.pallas_call(
            functools.partial(settle_kernel, at, newest),
            out_shape=[jax.ShapeDtypeStruct(cache_keys.shape, BF16)] * 2,
            in_specs=[SMEM] + [ANY] * len(used),
            out_specs=[ANY] * 2,
            scratch_shapes=[
                pltpu.VMEM((2, count, segment, features), BF16),
                pltpu.SemaphoreType.DMA((2, count)),
            ],
            compiler_params=big,
            cost_estimate=lasting(2 * count),
            name="settle",
        )(plan, *used)

    def pad_new():
        extra = -new_keys.shape[2] % 16
        return [jnp.pad(new[0], ((0, 0), (0, extra), (0, 0))) for new in (new_keys, new_values)]

    def choices(step):
        return parcels if step == matchings - 1 else [((0,), None), ((1,), None)]

    def prepare(step, sources):
        return pick(step, choices(step)[:1], sources)[0]

    def first_branch(mask):
        arrived = [exchange(block, "group", mask) for block in moving]
        asked = [query] + [exchange(query, "ctx", piece) for piece in everyone[1:]]
        return arrived, prepare(1, [*caches, *arrived]), asked, pad_new()

    def middle_branch(step, positions, prepared, asked, fresh, sources, mask):
        moving = [prepared, *pick(step, choices(step)[1:], sources)]
        arrived = [exchange(block, "group", mask) for block in moving]
        done = send_home(
            everyone, attend(positions[0], len(positions), everyone, asked, fresh, sources)
        )
        after = settle(positions, sources) if step == 1 else []
        return arrived, prepare(step + 1, sources + arrived), done, after

    def last_branch(step, first, prepared, asked, fresh, sources, mask):
        second = pick(step, parcels[1:2], sources)
        moving = [prepared, *second, *pick(step, parcels[2:], sources, second)]
        arrived = [exchange(block, "group", mask) for block in moving]
        done = send_home(everyone, attend(first, 1, everyone, asked, fresh, sources))
        most = attend(
            requests - 1, 1, far, asked, fresh, arrived[:2], [(0,), (1,)], done[:1]
        )
        parts = dict(zip(far, send_home(far, most)))
        if near:
            rest = attend(
                requests - 1, 1, near, asked, fresh, arrived[2:3], [(0, 1)], most[:1]
            )
            parts.update(zip(near, send_home(near, rest)))
        return arrived, done, [parts[piece] for piece in everyone[1:]]

    indices = masks - 1

    def switch(step, branch, *given):
        return lax.switch(
            indices[step],
            [functools.partial(branch, *given, mask) for mask in range(1, groups)],
        )

    arrived, prepared, asked, fresh = switch(0, first_branch)
    sources = [*caches, *arrived]
    lots, done, after = [], [], None
    for step in range(1, matchings - 1):
        first = sum(lots)
        positions = range(first, ready.index(step - 1) + 1)
        arrived, prepared, part, settled = switch(
            step, middle_branch, step, positions, prepared, asked, fresh, sources
        )
        after = after or settled
        sources = sources + arrived
        lots.append(len(positions))
        done += part
    arrived, part, pieces = switch(
        matchings - 1, last_branch, matchings - 1, sum(lots), prepared, asked, fresh, sources
    )
    lots.append(1)
    pieces = [*done, *part, *pieces]
    ahead = 1 + len(arrived) + len(sources) + 3 + len(pieces)
    left = requests - lots[0]
    return pl.pallas_call(
        functools.partial(finish_kernel, at, size, parcels, lots, lots[0], ready),
        out_shape=[
            jax.ShapeDtypeStruct(array.shape, BF16) for array in (query, cache_keys, cache_values)
        ],
        in_specs=[SMEM]
        + [ANY] * (len(arrived) + len(sources) + 1)
        + [VMEM] * 2
        + [ANY] * (len(pieces) + 2),
        out_specs=[VMEM, ANY, ANY],
        scratch_shapes=[
            pltpu.VMEM((segment + LANES, size.wide), BF16),
            pltpu.VMEM((segment + LANES, size.wide), BF16),
            pltpu.VMEM((tokens, own * HD), BF16),
            pltpu.VMEM((width, requests, *result.shape), BF16),
            pltpu.VMEM((2, left, segment, features), BF16),
            pltpu.SemaphoreType.DMA((2, left)),
            pltpu.SemaphoreType.DMA((2, left)),
            pltpu.SemaphoreType.DMA((4,)),
        ],
        input_output_aliases={ahead: 1, ahead + 1: 2},
        compiler_params=big,
        name="finish",
    )(plan, *arrived, *sources, query, *fresh, *pieces, *after)


def solution(mesh):
    placed = (
        P("group", None, None, "ctx"),
        P("group", None, "ctx", None),
        P("group", None, "ctx", None),
        P("group", None, "ctx", None),
        P("group", None, "ctx", None),
        P(),
        P(),
        P(),
        P(),
    )
    return jax.shard_map(
        shards,
        mesh=mesh,
        in_specs=placed,
        out_specs=(
            P("group", None, None, "ctx"),
            P("group", None, "ctx", None),
            P("group", None, "ctx", None),
        ),
        check_vma=False,
    )
```

time: 576 us -> 169 us (0.29)
  waiting for transfers between devices: 348 us -> 82.6 us
  local copies, waits for them, and re-layouts: 91.6 us -> 0.63 us
  other arithmetic: 56.6 us -> 0.66 us
  Pallas kernels: 0 us -> 53.2 us
  between operations: 25.7 us -> 2.86 us
  blocking collectives: 21 us -> 0 us
  matrix products: 19.6 us -> 0 us
  starting transfers between devices: 11.1 us -> 28.8 us
    ppermute x9 -> x20, waiting for transfers between devices: 268 us -> 82.6 us  [exchange(): lax.ppermute(block, axis, [(i, i ^ mask) for i in range(lax.axis_size(axi...]
    reduce_scatter x2 -> x0, waiting for transfers between devices: 80.1 us -> none  [the longest x1 76 us: shards(): lax.psum_scatter(scaled, 'ctx', scatter_dimension=2, tiled=True)]
    pallas_call x0 -> x12, Pallas kernels: none -> 53.2 us  [the longest x4 28.6 us: attend(): pl.pallas_call(functools.partial(attend_kernel, at, size, first, newest,...]
    select_n x19 -> x0, other arithmetic: 32.7 us -> none  [the longest x9 25.4 us: route_blocks(): current = jnp.where(flag, swapped, current)]
    dynamic_slice x25 -> x0, local copies, waits for them, and re-layouts: 28.6 us -> none  [the longest x16 20 us: shards(): lax.map(partial_attention, (gathered, keys, values, new_keys[0], new_valu...]
    pmax x1 -> x0, blocking collectives: 21 us -> none  [shards(): peak = lax.pmax(top, 'ctx')]
    dot_general x16 -> x0, matrix products: 19.6 us -> none  [the longest x4 6.15 us: partial_attention(): jnp.einsum('tkgd,skd->kgts', heads_q, fresh_keys.reshape(local_new, kv_he...]
    ppermute x9 -> x20, starting transfers between devices: 10.8 us -> 28.8 us  [exchange(): lax.ppermute(block, axis, [(i, i ^ mask) for i in range(lax.axis_size(axi...]
  transfers between devices with their start and end apart: 12 -> 20, of which waited for: 11 -> 12; matrix products, arithmetic and copies ran while one was open for 7% -> 0% of each run, Pallas kernels for 0% -> 24%
where the time goes in v2:
time: 169 us
  waiting for transfers between devices  82.6 us (49%)
  Pallas kernels  53.2 us (31%)
  starting transfers between devices  28.8 us (17%)
  between operations  2.86 us (2%)
    ppermute x20, waiting for transfers between devices, exchange(): lax.ppermute(block, axis, [(i, i ^ mask) for i in range(lax.axis_size(axi...  82.6 us
    ppermute x20, starting transfers between devices, exchange(): lax.ppermute(block, axis, [(i, i ^ mask) for i in range(lax.axis_size(axi...  28.8 us
    pallas_call x4, Pallas kernels, attend(): pl.pallas_call(functools.partial(attend_kernel, at, size, first, newest,...  28.6 us
    pallas_call x5, Pallas kernels, pick(): pl.pallas_call(functools.partial(pick_kernel, at, step, choices), out_sha...  11.3 us
    pallas_call x1, Pallas kernels, shards(): pl.pallas_call(functools.partial(finish_kernel, at, size, parcels, lots,...  6.67 us
    pallas_call x1, Pallas kernels, shards(): pl.pallas_call(functools.partial(plan_kernel, at), out_shape=(jax.ShapeDt...  3.6 us
  transfers between devices with their start and end apart: 20, of which 12 were waited for; matrix products, arithmetic and copies ran while one was open for 0% of the time, Pallas kernels for 24%

profile of v2, /device:TPU:0, one launch (start us, length us, event | category | flops | bytes accessed | tf_op | source)
XLA Modules:
  0.0 168.9 jit_solution(17006278630727644386)
XLA Ops:
  3.9 3.6 %plan.1 = (s32[51]{0:T(128)S(1)}, bf16[512,1024]{1,0:T(8,128)(2,1)S(1)}, bf16[512,1024]{1,0:T(8,128)(2,1)}) custom-call(s32[3]{0:T(128)} %masks.1, s32[3,8]{1,0:T(4,128)} %movers.1, s32[3,4,8]{2,1,0:T(4,128)} %bitcast.33, s32[4,8]{1,0:T(4,128)} %bitcast.34, bf16[1,4,512,1024]{3,2,1,0:T(8,128)(2,1)} %refs_4_.1, bf16[1,4,512,1024]{3,2,1,0:T(8,128)(2,1)} %refs_5_.1), custom_call_target="tpu_custom_call" | custom-call | tf_op jit(solution)/shard_map/plan/pallas_call | solution.py:468
  7.5 51.9 %conditional.3 = (bf16[512,1024]{1,0:T(8,128)(2,1)}, bf16[512,1024]{1,0:T(8,128)(2,1)}, bf16[512,1024]{1,0:T(8,128)(2,1)S(1)}, bf16[1,4,32,2048]{3,2,1,0:T(8,128...) conditional(s32[]{:T(128)} %bitcast.18, ...), branch_computations={%region_0.1_spmd, %region_1.2_spmd, %region_2.3_spmd, %region_3.4_... | conditional | bytes 24323548 | solution.py:590
  7.5 2.4 %collective-permute-start.10 = (bf16[512,1024]{1,0:T(8,128)(2,1)S(1)}, bf16[512,1024]{1,0:T(8,128)(2,1)}, u32[]{:S(2)}, u32[]{:S(2)}) collective-permute-start(bf16[512,1024]{1,0:T(8,128)(2,1)S(1)} %get-tuple-element.476), channel_id=1, source_target_pairs={{0,12},{4,8},{8,4},{12,0},{16,28},{20,24},{24,20},{28,16},{1,13},{... | collective-permute-start | bytes 3145736 | tf_op jit(solution)/shard_map/cond/branch_2_fun/ppermute | solution.py:23
  10.1 4.3 %collective-permute-start.14 = (bf16[1,4,32,2048]{3,2,1,0:T(8,128)(2,1)S(1)}, bf16[1,4,32,2048]{3,2,1,0:T(8,128)(2,1)}, u32[]{:S(2)}, u32[]{:S(2)}) collective-permute-start(bf16[1,4,32,2048]{3,2,1,0:T(8,128)(2,1)S(1)} %get-tuple-element.480), channel_id=1, source_target_pairs={{0,3},{1,2},{2,1},{3,0},{4,7},{5,6},{6,5},{7,4},{8,11},{9,10},{10,... | collective-permute-start | bytes 1572872 | tf_op jit(solution)/shard_map/cond/branch_2_fun/ppermute | solution.py:23
  15.0 18.5 %collective-permute-done.10.refs_2_.refs_3_ = bf16[512,1024]{1,0:T(8,128)(2,1)} collective-permute-done((bf16[512,1024]{1,0:T(8,128)(2,1)S(1)}, bf16[512,1024]{1,0:T(8,128)(2,1)}, u32[]{:S(2)}, u32[]{:S(2)}) %collective-permute-start.10) | collective-permute-done | bytes 1048608 | tf_op jit(solution)/shard_map/cond/branch_2_fun/ppermute | solution.py:23
  33.5 1.8 %pick_1.16 = bf16[512,1024]{1,0:T(8,128)(2,1)S(1)} custom-call(s32[51]{0:T(128)S(1)} %get-tuple-element.478.plan, bf16[1,4,512,1024]{3,2,1,0:T(8,128)(2,1)} %get-tuple-element.479.refs_0_.refs_1_, bf16[1,4,512,1024]{3,2,1,0:T(8,128)(2,1)} %get-tuple-element.479.refs_0_.refs_1_, bf16[512,1024]{1,0:T(8,128)(2,1)} %collective-permute-done.10.refs_2_.refs_3_, ...), custom_call_target="tpu_custom_call" | custom-call | bytes 9250000 | tf_op jit(solution)/shard_map/cond/branch_2_fun/pick_1/pallas_call | solution.py:493
  35.3 24.1 %collective-permute-done.13 = bf16[1,4,32,2048]{3,2,1,0:T(8,128)(2,1)} collective-permute-done((bf16[1,4,32,2048]{3,2,1,0:T(8,128)(2,1)S(1)}, bf16[1,4,32,2048]{3,2,1,0:T(8,128)(2,1)}, u32[]{:S(2)}, u32[]{:S(2)}) %collective-permute-start.13) | collective-permute-done | bytes 524320 | tf_op jit(solution)/shard_map/cond/branch_2_fun/ppermute | solution.py:23
  59.4 48.0 %conditional.4 = (bf16[512,1024]{1,0:T(8,128)(2,1)}, bf16[512,1024]{1,0:T(8,128)(2,1)}, bf16[1,512,512]{2,1,0:T(8,128)(2,1)S(1)}, bf16[2,32,2176]{2,1,0:T(8,128)...) conditional(s32[]{:T(128)} %bitcast.17, ...), branch_computations={%region_7.8_spmd, %region_8.9_spmd, %region_9.10_spmd, %region_10.... | conditional | bytes 126685712 | solution.py:590
  59.6 2.8 %pick_1.23 = bf16[512,1024]{1,0:T(8,128)(2,1)} custom-call(s32[51]{0:T(128)S(1)} %get-tuple-element.548.plan, bf16[1,4,512,1024]{3,2,1,0:T(8,128)(2,1)} %get-tuple-element.549.refs_0_.refs_1_.refs_7_, bf16[1,4,512,1024]{3,2,1,0:T(8,128)(2,1)} %get-tuple-element.549.refs_0_.refs_1_.refs_7_, bf16[512,1024]{1,0:T(8,128)(2,1)} %get-tuple-element.550.refs_2_.refs_3_.refs_9_, ...), custom_call_target="tpu_custom_call" | custom-call | bytes 9250000 | tf_op jit(solution)/shard_map/cond/branch_2_fun/pick_1/pallas_call | solution.py:493
  62.5 1.7 collective-permute-start.46
  64.1 12.9 %attend_0_2_4.9 = (bf16[2,32,2176]{2,1,0:T(8,128)(2,1)S(1)}, bf16[2,32,2176]{2,1,0:T(8,128)(2,1)S(1)}, bf16[2,32,2176]{2,1,0:T(8,128)(2,1)S(1)}, bf16[2,32,2176]{2,1,0:T(8,128)(2,1)S(1)}) custom-call(s32[51]{0:T(128)S(1)} %get-tuple-element.548.plan, bf16[1,4,32,2048]{3,2,1,0:T(8,128)(2,1)S(1)} %get-tuple-element.553.refs_0_, ...), custom_call_target="tpu_custom_call" | custom-call | bytes 48100000 | tf_op jit(solution)/shard_map/cond/branch_2_fun/attend_0_2_4/pallas_call | solution.py:509
  77.1 3.0 %collective-permute-start.48 = (bf16[2,32,2176]{2,1,0:T(8,128)(2,1)S(1)}, bf16[2,32,2176]{2,1,0:T(8,128)(2,1)}, u32[]{:S(2)}, u32[]{:S(2)}) collective-permute-start(bf16[2,32,2176]{2,1,0:T(8,128)(2,1)S(1)} %get-tuple-element.561), channel_id=1, source_target_pairs={{0,2},{1,3},{2,0},{3,1},{4,6},{5,7},{6,4},{7,5},{8,10},{9,11},{10,... | collective-permute-start | bytes 835592 | tf_op jit(solution)/shard_map/cond/branch_2_fun/ppermute | solution.py:23
  81.4 3.0 %settle.9 = (bf16[1,4,512,1024]{3,2,1,0:T(8,128)(2,1)}, bf16[1,4,512,1024]{3,2,1,0:T(8,128)(2,1)}) custom-call(s32[51]{0:T(128)S(1)} %get-tuple-element.548.plan, bf16[1,4,512,1024]{3,2,1,0:T(8,128)(2,1)S(1)} %copy-done.2, bf16[1,4,512,1024]{3,2,1,0:T(8,128)(2,1)S(1)} %copy-done.9, bf16[512,1024]{1,0:T(8,128)(2,1)} %get-tuple-element.552.refs_2_.refs_3_.refs_8_, ...), custom_call_target="tpu_custom_call" | custom-call | bytes 14800000 | tf_op jit(solution)/shard_map/cond/branch_2_fun/settle/pallas_call | solution.py:533
  86.6 4.2 %collective-permute-done.47 = bf16[2,32,2176]{2,1,0:T(8,128)(2,1)} collective-permute-done((bf16[2,32,2176]{2,1,0:T(8,128)(2,1)S(1)}, bf16[2,32,2176]{2,1,0:T(8,128)(2,1)}, u32[]{:S(2)}, u32[]{:S(2)}) %collective-permute-start.47) | collective-permute-done | bytes 278560 | tf_op jit(solution)/shard_map/cond/branch_2_fun/ppermute | solution.py:23
  90.8 8.8 %collective-permute-done.48 = bf16[2,32,2176]{2,1,0:T(8,128)(2,1)} collective-permute-done((bf16[2,32,2176]{2,1,0:T(8,128)(2,1)S(1)}, bf16[2,32,2176]{2,1,0:T(8,128)(2,1)}, u32[]{:S(2)}, u32[]{:S(2)}) %collective-permute-start.48) | collective-permute-done | bytes 278560 | tf_op jit(solution)/shard_map/cond/branch_2_fun/ppermute | solution.py:23
  99.7 7.8 %collective-permute-done.46 = bf16[512,1024]{1,0:T(8,128)(2,1)} collective-permute-done((bf16[512,1024]{1,0:T(8,128)(2,1)}, bf16[512,1024]{1,0:T(8,128)(2,1)}, u32[]{:S(2)}, u32[]{:S(2)}) %collective-permute-start.46) | collective-permute-done | bytes 1048608 | tf_op jit(solution)/shard_map/cond/branch_2_fun/ppermute | solution.py:23
  107.4 54.6 %conditional.5 = (bf16[1,512,512]{2,1,0:T(8,128)(2,1)}, bf16[1,512,512]{2,1,0:T(8,128)(2,1)}, bf16[2,512,256]{2,1,0:T(8,128)(2,1)}, bf16[2,512,256]{2,1,0:T(8,12...) conditional(s32[]{:T(128)} %bitcast.16, ...), branch_computations={%region_14.15_spmd, %region_15.16_spmd, %region_16.17_spmd, %regio... | conditional | bytes 80181432 | solution.py:590
  107.4 2.4 %pick_2.38.refs_6_ = bf16[1,512,512]{2,1,0:T(8,128)(2,1)} custom-call(s32[51]{0:T(128)S(1)} %get-tuple-element.748.plan, bf16[1,4,512,1024]{3,2,1,0:T(8,128)(2,1)} %get-tuple-element.749.refs_0_.refs_1_.refs_7_, bf16[1,4,512,1024]{3,2,1,0:T(8,128)(2,1)} %get-tuple-element.749.refs_0_.refs_1_.refs_7_, ...), custom_call_target="tpu_custom_call" | custom-call | bytes 9250000 | tf_op jit(solution)/shard_map/cond/branch_5_fun/pick_2/pallas_call | solution.py:493
  109.8 1.8 %collective-permute-start.121 = (bf16[1,512,512]{2,1,0:T(8,128)(2,1)}, bf16[1,512,512]{2,1,0:T(8,128)(2,1)}, u32[]{:S(2)}, u32[]{:S(2)}) collective-permute-start(bf16[1,512,512]{2,1,0:T(8,128)(2,1)} %pick_2.38.refs_6_), channel_id=1, source_target_pairs={{0,24},{4,28},{8,16},{12,20},{16,8},{20,12},{24,0},{28,4},{1,25},{... | collective-permute-start | bytes 1572872 | tf_op jit(solution)/shard_map/cond/branch_5_fun/ppermute | solution.py:23
  112.8 2.8 %pick_2.39 = (bf16[2,512,256]{2,1,0:T(8,128)(2,1)}, bf16[2,512,256]{2,1,0:T(8,128)(2,1)}) custom-call(s32[51]{0:T(128)S(1)} %get-tuple-element.748.plan, bf16[1,4,512,1024]{3,2,1,0:T(8,128)(2,1)} %get-tuple-element.752.refs_0_.refs_6_, bf16[1,4,512,1024]{3,2,1,0:T(8,128)(2,1)} %get-tuple-element.749.refs_0_.refs_1_.refs_7_, ...), custom_call_target="tpu_custom_call" | custom-call | bytes 9250000 | tf_op jit(solution)/shard_map/cond/branch_5_fun/pick_2/pallas_call | solution.py:493
  115.6 1.8 %collective-permute-start.122 = (bf16[2,512,256]{2,1,0:T(8,128)(2,1)}, bf16[2,512,256]{2,1,0:T(8,128)(2,1)}, u32[]{:S(2)}, u32[]{:S(2)}) collective-permute-start(bf16[2,512,256]{2,1,0:T(8,128)(2,1)} %get-tuple-element.755), channel_id=1, source_target_pairs={{0,24},{4,28},{8,16},{12,20},{16,8},{20,12},{24,0},{28,4},{1,25},{... | collective-permute-start | bytes 1572872 | tf_op jit(solution)/shard_map/cond/branch_5_fun/ppermute | solution.py:23
  118.6 8.0 %attend_2_1_4.12 = (bf16[1,32,2176]{2,1,0:T(8,128)(2,1)}, bf16[1,32,2176]{2,1,0:T(8,128)(2,1)S(1)}, bf16[1,32,2176]{2,1,0:T(8,128)(2,1)S(1)}, bf16[1,32,2176]{2,1,0:T(8,128)(2,1)S(1)}) custom-call(s32[51]{0:T(128)S(1)} %get-tuple-element.748.plan, bf16[1,4,32,2048]{3,2,1,0:T(8,128)(2,1)S(1)} %get-tuple-element.757.refs_0_, ...), custom_call_target="tpu_custom_call" | custom-call | bytes 25900000 | tf_op jit(solution)/shard_map/cond/branch_5_fun/attend_2_1_4/pallas_call | solution.py:509
  126.7 3.0 %collective-permute-start.125 = (bf16[1,32,2176]{2,1,0:T(8,128)(2,1)S(1)}, bf16[1,32,2176]{2,1,0:T(8,128)(2,1)}, u32[]{:S(2)}, u32[]{:S(2)}) collective-permute-start(bf16[1,32,2176]{2,1,0:T(8,128)(2,1)S(1)} %get-tuple-element.765), channel_id=1, source_target_pairs={{0,2},{1,3},{2,0},{3,1},{4,6},{5,7},{6,4},{7,5},{8,10},{9,11},{10,... | collective-permute-start | bytes 417800 | tf_op jit(solution)/shard_map/cond/branch_5_fun/ppermute | solution.py:23
  129.7 7.4 %collective-permute-done.120.refs_4_ = bf16[1,512,512]{2,1,0:T(8,128)(2,1)} collective-permute-done((bf16[1,512,512]{2,1,0:T(8,128)(2,1)S(1)}, bf16[1,512,512]{2,1,0:T(8,128)(2,1)}, u32[]{:S(2)}, u32[]{:S(2)}) %collective-permute-start.120) | collective-permute-done | bytes 524320 | tf_op jit(solution)/shard_map/cond/branch_5_fun/ppermute | solution.py:23
  137.1 2.5 %collective-permute-start.126 = (bf16[1,32,2176]{2,1,0:T(8,128)(2,1)S(1)}, bf16[1,32,2176]{2,1,0:T(8,128)(2,1)}, u32[]{:S(2)}, u32[]{:S(2)}) collective-permute-start(bf16[1,32,2176]{2,1,0:T(8,128)(2,1)S(1)} %get-tuple-element.766), channel_id=1, source_target_pairs={{0,3},{1,2},{2,1},{3,0},{4,7},{5,6},{6,5},{7,4},{8,11},{9,10},{10,... | collective-permute-start | bytes 417800 | tf_op jit(solution)/shard_map/cond/branch_5_fun/ppermute | solution.py:23
  139.6 4.7 %attend_3_1_2.12 = (bf16[1,32,2176]{2,1,0:T(8,128)(2,1)S(1)}, bf16[1,32,2176]{2,1,0:T(8,128)(2,1)S(1)}) custom-call(s32[51]{0:T(128)S(1)} %get-tuple-element.748.plan, bf16[1,4,32,2048]{3,2,1,0:T(8,128)(2,1)} %get-tuple-element.759.refs_2_.refs_0_, bf16[1,4,32,2048]{3,2,1,0:T(8,128)(2,1)} %get-tuple-element.760.refs_3_.refs_1_, ...), custom_call_target="tpu_custom_call" | custom-call | bytes 14800000 | tf_op jit(solution)/shard_map/cond/branch_5_fun/attend_3_1_2/pallas_call | solution.py:509
  144.3 4.1 %collective-permute-done.122.refs_3_ = bf16[2,512,256]{2,1,0:T(8,128)(2,1)} collective-permute-done((bf16[2,512,256]{2,1,0:T(8,128)(2,1)}, bf16[2,512,256]{2,1,0:T(8,128)(2,1)}, u32[]{:S(2)}, u32[]{:S(2)}) %collective-permute-start.122) | collective-permute-done | bytes 524320 | tf_op jit(solution)/shard_map/cond/branch_5_fun/ppermute | solution.py:23
  148.4 3.0 %attend_3_1_1.12 = bf16[1,32,2176]{2,1,0:T(8,128)(2,1)S(1)} custom-call(s32[51]{0:T(128)S(1)} %get-tuple-element.748.plan, bf16[1,4,32,2048]{3,2,1,0:T(8,128)(2,1)} %get-tuple-element.758.refs_1_.refs_0_, bf16[4,16,1024]{2,1,0:T(8,128)(2,1)S(1)} %get-tuple-element.761.refs_4_.refs_2_.refs_1_, ...), custom_call_target="tpu_custom_call" | custom-call | bytes 9250000 | tf_op jit(solution)/shard_map/cond/branch_5_fun/attend_3_1_1/pallas_call | solution.py:509
  151.4 2.5 %collective-permute-start.129 = (bf16[1,32,2176]{2,1,0:T(8,128)(2,1)S(1)}, bf16[1,32,2176]{2,1,0:T(8,128)(2,1)}, u32[]{:S(2)}, u32[]{:S(2)}) collective-permute-start(bf16[1,32,2176]{2,1,0:T(8,128)(2,1)S(1)} %get-tuple-element.768), channel_id=1, source_target_pairs={{0,3},{1,2},{2,1},{3,0},{4,7},{5,6},{6,5},{7,4},{8,11},{9,10},{10,... | collective-permute-start | bytes 417800 | tf_op jit(solution)/shard_map/cond/branch_5_fun/ppermute | solution.py:23
  155.0 3.7 %collective-permute-done.123 = bf16[2,512,256]{2,1,0:T(8,128)(2,1)} collective-permute-done((bf16[2,512,256]{2,1,0:T(8,128)(2,1)}, bf16[2,512,256]{2,1,0:T(8,128)(2,1)}, u32[]{:S(2)}, u32[]{:S(2)}) %collective-permute-start.123) | collective-permute-done | bytes 524320 | tf_op jit(solution)/shard_map/cond/branch_5_fun/ppermute | solution.py:23
  160.1 1.9 %collective-permute-done.127 = bf16[1,32,2176]{2,1,0:T(8,128)(2,1)} collective-permute-done((bf16[1,32,2176]{2,1,0:T(8,128)(2,1)S(1)}, bf16[1,32,2176]{2,1,0:T(8,128)(2,1)}, u32[]{:S(2)}, u32[]{:S(2)}) %collective-permute-start.127) | collective-permute-done | bytes 139296 | tf_op jit(solution)/shard_map/cond/branch_5_fun/ppermute | solution.py:23
  162.0 6.7 %finish.1 = (bf16[1,4,32,2048]{3,2,1,0:T(8,128)(2,1)}, bf16[1,4,512,1024]{3,2,1,0:T(8,128)(2,1)}, bf16[1,4,512,1024]{3,2,1,0:T(8,128)(2,1)}) custom-call(s32[51]{0:T(128)S(1)} %get-tuple-element.825.plan, bf16[1,512,512]{2,1,0:T(8,128)(2,1)} %get-tuple-element.839.refs_0_, ...), custom_call_target="tpu_custom_call", output_to_operand_aliasing={{1}: (25, {}), {2}: (26, {})} | custom-call | tf_op jit(solution)/shard_map/finish/pallas_call | solution.py:615
  (37 shorter events, 10.7 us)
Async XLA Ops:
  3.8 3.6 %copy-start.14 = (bf16[1,4,32,2048]{3,2,1,0:T(8,128)(2,1)S(1)}, bf16[1,4,32,2048]{3,2,1,0:T(8,128)(2,1)}, u32[]{:S(2)}) copy-start(bf16[1,4,32,2048]{3,2,1,0:T(8,128)(2,1)} %refs_10_.1) | copy-start | bytes 1572868
  3.8 3.6 %copy-start.15 = (bf16[1,4,8,1024]{3,2,1,0:T(8,128)(2,1)S(1)}, bf16[1,4,8,1024]{3,2,1,0:T(8,128)(2,1)}, u32[]{:S(2)}) copy-start(bf16[1,4,8,1024]{3,2,1,0:T(8,128)(2,1)} %param.33) | copy-start | bytes 196612
  3.9 3.6 %copy-start.16 = (bf16[1,4,8,1024]{3,2,1,0:T(8,128)(2,1)S(1)}, bf16[1,4,8,1024]{3,2,1,0:T(8,128)(2,1)}, u32[]{:S(2)}) copy-start(bf16[1,4,8,1024]{3,2,1,0:T(8,128)(2,1)} %param.34) | copy-start | bytes 196612
  7.5 26.0 %collective-permute-start.10 = (bf16[512,1024]{1,0:T(8,128)(2,1)S(1)}, bf16[512,1024]{1,0:T(8,128)(2,1)}, u32[]{:S(2)}, u32[]{:S(2)}) collective-permute-start(bf16[512,1024]{1,0:T(8,128)(2,1)S(1)} %get-tuple-element.476), channel_id=1, source_target_pairs={{0,12},{4,8},{8,4},{12,0},{16,28},{20,24},{24,20},{28,16},{1,13},{... | collective-permute-start | bytes 3145736 | tf_op jit(solution)/shard_map/cond/branch_2_fun/ppermute | solution.py:23
  10.0 49.4 %collective-permute-start.11 = (bf16[512,1024]{1,0:T(8,128)(2,1)}, bf16[512,1024]{1,0:T(8,128)(2,1)}, u32[]{:S(2)}, u32[]{:S(2)}) collective-permute-start(bf16[512,1024]{1,0:T(8,128)(2,1)} %get-tuple-element.477), channel_id=1, source_target_pairs={{0,12},{4,8},{8,4},{12,0},{16,28},{20,24},{24,20},{28,16},{1,13},{... | collective-permute-start | bytes 3145736 | tf_op jit(solution)/shard_map/cond/branch_2_fun/ppermute | solution.py:23
  10.1 25.3 %collective-permute-start.14 = (bf16[1,4,32,2048]{3,2,1,0:T(8,128)(2,1)S(1)}, bf16[1,4,32,2048]{3,2,1,0:T(8,128)(2,1)}, u32[]{:S(2)}, u32[]{:S(2)}) collective-permute-start(bf16[1,4,32,2048]{3,2,1,0:T(8,128)(2,1)S(1)} %get-tuple-element.480), channel_id=1, source_target_pairs={{0,3},{1,2},{2,1},{3,0},{4,7},{5,6},{6,5},{7,4},{8,11},{9,10},{10,... | collective-permute-start | bytes 1572872 | tf_op jit(solution)/shard_map/cond/branch_2_fun/ppermute | solution.py:23
  14.4 45.0 %collective-permute-start.13 = (bf16[1,4,32,2048]{3,2,1,0:T(8,128)(2,1)S(1)}, bf16[1,4,32,2048]{3,2,1,0:T(8,128)(2,1)}, u32[]{:S(2)}, u32[]{:S(2)}) collective-permute-start(bf16[1,4,32,2048]{3,2,1,0:T(8,128)(2,1)S(1)} %get-tuple-element.480), channel_id=1, source_target_pairs={{0,2},{1,3},{2,0},{3,1},{4,6},{5,7},{6,4},{7,5},{8,10},{9,11},{10,... | collective-permute-start | bytes 1572872 | tf_op jit(solution)/shard_map/cond/branch_2_fun/ppermute | solution.py:23
  14.4 45.0 %collective-permute-start.12 = (bf16[1,4,32,2048]{3,2,1,0:T(8,128)(2,1)S(1)}, bf16[1,4,32,2048]{3,2,1,0:T(8,128)(2,1)}, u32[]{:S(2)}, u32[]{:S(2)}) collective-permute-start(bf16[1,4,32,2048]{3,2,1,0:T(8,128)(2,1)S(1)} %get-tuple-element.480), channel_id=1, source_target_pairs={{0,1},{1,0},{2,3},{3,2},{4,5},{5,4},{6,7},{7,6},{8,9},{9,8},{10,11... | collective-permute-start | bytes 1572872 | tf_op jit(solution)/shard_map/cond/branch_2_fun/ppermute | solution.py:23
  59.4 25.6 %collective-permute-start.45 = (bf16[512,1024]{1,0:T(8,128)(2,1)S(1)}, bf16[512,1024]{1,0:T(8,128)(2,1)}, u32[]{:S(2)}, u32[]{:S(2)}) collective-permute-start(bf16[512,1024]{1,0:T(8,128)(2,1)S(1)} %get-tuple-element.547), channel_id=1, source_target_pairs={{0,12},{4,8},{8,4},{12,0},{16,28},{20,24},{24,20},{28,16},{1,13},{... | collective-permute-start | bytes 3145736 | tf_op jit(solution)/shard_map/cond/branch_2_fun/ppermute | solution.py:23
  62.5 45.0 %collective-permute-start.46 = (bf16[512,1024]{1,0:T(8,128)(2,1)}, bf16[512,1024]{1,0:T(8,128)(2,1)}, u32[]{:S(2)}, u32[]{:S(2)}) collective-permute-start(bf16[512,1024]{1,0:T(8,128)(2,1)} %pick_1.23), channel_id=1, source_target_pairs={{0,12},{4,8},{8,4},{12,0},{16,28},{20,24},{24,20},{28,16},{1,13},{... | collective-permute-start | bytes 3145736 | tf_op jit(solution)/shard_map/cond/branch_2_fun/ppermute | solution.py:23
  64.1 17.3 %copy-start.2 = (bf16[1,4,512,1024]{3,2,1,0:T(8,128)(2,1)S(1)}, bf16[1,4,512,1024]{3,2,1,0:T(8,128)(2,1)}, u32[]{:S(2)}) copy-start(bf16[1,4,512,1024]{3,2,1,0:T(8,128)(2,1)} %get-tuple-element.551.refs_0_.refs_1_.refs_6_) | copy-start | bytes 12582916 | tf_op jit(solution)/shard_map/cond
  64.1 17.3 %copy-start.9 = (bf16[1,4,512,1024]{3,2,1,0:T(8,128)(2,1)S(1)}, bf16[1,4,512,1024]{3,2,1,0:T(8,128)(2,1)}, u32[]{:S(2)}) copy-start(bf16[1,4,512,1024]{3,2,1,0:T(8,128)(2,1)} %get-tuple-element.549.refs_0_.refs_1_.refs_7_) | copy-start | bytes 12582916 | tf_op jit(solution)/shard_map/cond
  77.0 13.8 %collective-permute-start.47 = (bf16[2,32,2176]{2,1,0:T(8,128)(2,1)S(1)}, bf16[2,32,2176]{2,1,0:T(8,128)(2,1)}, u32[]{:S(2)}, u32[]{:S(2)}) collective-permute-start(bf16[2,32,2176]{2,1,0:T(8,128)(2,1)S(1)} %get-tuple-element.560), channel_id=1, source_target_pairs={{0,1},{1,0},{2,3},{3,2},{4,5},{5,4},{6,7},{7,6},{8,9},{9,8},{10,11... | collective-permute-start | bytes 835592 | tf_op jit(solution)/shard_map/cond/branch_2_fun/ppermute | solution.py:23
  77.1 22.6 %collective-permute-start.48 = (bf16[2,32,2176]{2,1,0:T(8,128)(2,1)S(1)}, bf16[2,32,2176]{2,1,0:T(8,128)(2,1)}, u32[]{:S(2)}, u32[]{:S(2)}) collective-permute-start(bf16[2,32,2176]{2,1,0:T(8,128)(2,1)S(1)} %get-tuple-element.561), channel_id=1, source_target_pairs={{0,2},{1,3},{2,0},{3,1},{4,6},{5,7},{6,4},{7,5},{8,10},{9,11},{10,... | collective-permute-start | bytes 835592 | tf_op jit(solution)/shard_map/cond/branch_2_fun/ppermute | solution.py:23
  80.1 19.6 %collective-permute-start.49 = (bf16[2,32,2176]{2,1,0:T(8,128)(2,1)S(1)}, bf16[2,32,2176]{2,1,0:T(8,128)(2,1)}, u32[]{:S(2)}, u32[]{:S(2)}) collective-permute-start(bf16[2,32,2176]{2,1,0:T(8,128)(2,1)S(1)} %get-tuple-element.562), channel_id=1, source_target_pairs={{0,3},{1,2},{2,1},{3,0},{4,7},{5,6},{6,5},{7,4},{8,11},{9,10},{10,... | collective-permute-start | bytes 835592 | tf_op jit(solution)/shard_map/cond/branch_2_fun/ppermute | solution.py:23
  109.8 16.9 %collective-permute-start.121 = (bf16[1,512,512]{2,1,0:T(8,128)(2,1)}, bf16[1,512,512]{2,1,0:T(8,128)(2,1)}, u32[]{:S(2)}, u32[]{:S(2)}) collective-permute-start(bf16[1,512,512]{2,1,0:T(8,128)(2,1)} %pick_2.38.refs_6_), channel_id=1, source_target_pairs={{0,24},{4,28},{8,16},{12,20},{16,8},{20,12},{24,0},{28,4},{1,25},{... | collective-permute-start | bytes 1572872 | tf_op jit(solution)/shard_map/cond/branch_5_fun/ppermute | solution.py:23
  111.6 25.5 %collective-permute-start.120 = (bf16[1,512,512]{2,1,0:T(8,128)(2,1)S(1)}, bf16[1,512,512]{2,1,0:T(8,128)(2,1)}, u32[]{:S(2)}, u32[]{:S(2)}) collective-permute-start(bf16[1,512,512]{2,1,0:T(8,128)(2,1)S(1)} %get-tuple-element.747), channel_id=1, source_target_pairs={{0,24},{4,28},{8,16},{12,20},{16,8},{20,12},{24,0},{28,4},{1,25},{... | collective-permute-start | bytes 1572872 | tf_op jit(solution)/shard_map/cond/branch_5_fun/ppermute | solution.py:23
  115.6 32.8 %collective-permute-start.122 = (bf16[2,512,256]{2,1,0:T(8,128)(2,1)}, bf16[2,512,256]{2,1,0:T(8,128)(2,1)}, u32[]{:S(2)}, u32[]{:S(2)}) collective-permute-start(bf16[2,512,256]{2,1,0:T(8,128)(2,1)} %get-tuple-element.755), channel_id=1, source_target_pairs={{0,24},{4,28},{8,16},{12,20},{16,8},{20,12},{24,0},{28,4},{1,25},{... | collective-permute-start | bytes 1572872 | tf_op jit(solution)/shard_map/cond/branch_5_fun/ppermute | solution.py:23
  117.4 41.3 %collective-permute-start.123 = (bf16[2,512,256]{2,1,0:T(8,128)(2,1)}, bf16[2,512,256]{2,1,0:T(8,128)(2,1)}, u32[]{:S(2)}, u32[]{:S(2)}) collective-permute-start(bf16[2,512,256]{2,1,0:T(8,128)(2,1)} %get-tuple-element.756), channel_id=1, source_target_pairs={{0,24},{4,28},{8,16},{12,20},{16,8},{20,12},{24,0},{28,4},{1,25},{... | collective-permute-start | bytes 1572872 | tf_op jit(solution)/shard_map/cond/branch_5_fun/ppermute | solution.py:23
  126.6 24.8 %collective-permute-start.124 = (bf16[1,32,2176]{2,1,0:T(8,128)(2,1)S(1)}, bf16[1,32,2176]{2,1,0:T(8,128)(2,1)}, u32[]{:S(2)}, u32[]{:S(2)}) collective-permute-start(bf16[1,32,2176]{2,1,0:T(8,128)(2,1)S(1)} %get-tuple-element.764), channel_id=1, source_target_pairs={{0,1},{1,0},{2,3},{3,2},{4,5},{5,4},{6,7},{7,6},{8,9},{9,8},{10,11... | collective-permute-start | bytes 417800 | tf_op jit(solution)/shard_map/cond/branch_5_fun/ppermute | solution.py:23
  126.7 27.2 %collective-permute-start.125 = (bf16[1,32,2176]{2,1,0:T(8,128)(2,1)S(1)}, bf16[1,32,2176]{2,1,0:T(8,128)(2,1)}, u32[]{:S(2)}, u32[]{:S(2)}) collective-permute-start(bf16[1,32,2176]{2,1,0:T(8,128)(2,1)S(1)} %get-tuple-element.765), channel_id=1, source_target_pairs={{0,2},{1,3},{2,0},{3,1},{4,6},{5,7},{6,4},{7,5},{8,10},{9,11},{10,... | collective-permute-start | bytes 417800 | tf_op jit(solution)/shard_map/cond/branch_5_fun/ppermute | solution.py:23
  137.1 17.9 %collective-permute-start.126 = (bf16[1,32,2176]{2,1,0:T(8,128)(2,1)S(1)}, bf16[1,32,2176]{2,1,0:T(8,128)(2,1)}, u32[]{:S(2)}, u32[]{:S(2)}) collective-permute-start(bf16[1,32,2176]{2,1,0:T(8,128)(2,1)S(1)} %get-tuple-element.766), channel_id=1, source_target_pairs={{0,3},{1,2},{2,1},{3,0},{4,7},{5,6},{6,5},{7,4},{8,11},{9,10},{10,... | collective-permute-start | bytes 417800 | tf_op jit(solution)/shard_map/cond/branch_5_fun/ppermute | solution.py:23
  148.4 11.8 %collective-permute-start.128 = (bf16[1,32,2176]{2,1,0:T(8,128)(2,1)S(1)}, bf16[1,32,2176]{2,1,0:T(8,128)(2,1)}, u32[]{:S(2)}, u32[]{:S(2)}) collective-permute-start(bf16[1,32,2176]{2,1,0:T(8,128)(2,1)S(1)} %get-tuple-element.767.refs_4_), channel_id=1, source_target_pairs={{0,2},{1,3},{2,0},{3,1},{4,6},{5,7},{6,4},{7,5},{8,10},{9,11},{10,... | collective-permute-start | bytes 417800 | tf_op jit(solution)/shard_map/cond/branch_5_fun/ppermute | solution.py:23
  151.4 7.6 %collective-permute-start.129 = (bf16[1,32,2176]{2,1,0:T(8,128)(2,1)S(1)}, bf16[1,32,2176]{2,1,0:T(8,128)(2,1)}, u32[]{:S(2)}, u32[]{:S(2)}) collective-permute-start(bf16[1,32,2176]{2,1,0:T(8,128)(2,1)S(1)} %get-tuple-element.768), channel_id=1, source_target_pairs={{0,3},{1,2},{2,1},{3,0},{4,7},{5,6},{6,5},{7,4},{8,11},{9,10},{10,... | collective-permute-start | bytes 417800 | tf_op jit(solution)/shard_map/cond/branch_5_fun/ppermute | solution.py:23
  154.0 8.1 %collective-permute-start.127 = (bf16[1,32,2176]{2,1,0:T(8,128)(2,1)S(1)}, bf16[1,32,2176]{2,1,0:T(8,128)(2,1)}, u32[]{:S(2)}, u32[]{:S(2)}) collective-permute-start(bf16[1,32,2176]{2,1,0:T(8,128)(2,1)S(1)} %attend_3_1_1.12), channel_id=1, source_target_pairs={{0,1},{1,0},{2,3},{3,2},{4,5},{5,4},{6,7},{7,6},{8,9},{9,8},{10,11... | collective-permute-start | bytes 417800 | tf_op jit(solution)/shard_map/cond/branch_5_fun/ppermute | solution.py:23

commit v3 on v2

--- a/solution.py
+++ b/solution.py
@@ -37,20 +37,51 @@
         self.size = self.place + 1
 
 
+def copy_pieces(views, out, sem, place, first):
+    wide = views[0].shape[1] // lax.axis_size("ctx")
+
+    def piece(p, carry):
+        begin = pl.multiple_of((place ^ (first + p)) * wide, wide)
+        into = pl.ds(pl.multiple_of(p * wide, wide), wide)
+        for m, view in enumerate(views):
+            pltpu.make_async_copy(view.at[:, pl.ds(begin, wide)], out.at[m, :, into], sem).start()
+        return carry
+
+    lax.fori_loop(0, out.shape[2] // wide, piece, 0)
+
+
+def place_pieces(parcel, bufs, sems, place, first, rows=None, into=None):
+    rows = pl.ds(0, parcel.shape[1]) if rows is None else rows
+    into = rows if into is None else into
+    wide = bufs[0].shape[1] // lax.axis_size("ctx")
+
+    def piece(p, carry):
+        begin = pl.multiple_of((place ^ (first + p)) * wide, wide)
+        origin = pl.ds(pl.multiple_of(p * wide, wide), wide)
+        for m, buf in enumerate(bufs):
+            pltpu.make_async_copy(
+                parcel.at[m, rows, origin], buf.at[into, pl.ds(begin, wide)], sems[m]
+            ).start()
+        return carry
+
+    lax.fori_loop(0, parcel.shape[2] // wide, piece, 0)
+
+
 def plan_kernel(
-    at, masks, movers, lists, lengths, keys, values, plan, key_out, value_out, sems
+    at, parcels, masks, movers, lists, lengths, keys, values, plan, *refs
 ):
+    some = len(parcels)
+    indices, outs, sems = refs[: -1 - some], refs[-1 - some : -1], refs[-1]
     matchings, nblocks, _ = lists.shape
     requests = lengths.shape[0]
     here = lax.axis_index("group")
-    first = movers[0, here]
-    copies = [
-        pltpu.make_async_copy(keys.at[0, first], key_out, sems.at[0]),
-        pltpu.make_async_copy(values.at[0, first], value_out, sems.at[1]),
-    ]
-    for copy in copies:
-        copy.start()
-    plan[at.place] = lax.axis_index("ctx")
+    place = lax.axis_index("ctx")
+    views = [keys.at[0, movers[0, here]], values.at[0, movers[0, here]]]
+    for c, (out, pieces) in enumerate(zip(outs, parcels)):
+        copy_pieces(views, out, sems.at[c], place, pieces[0])
+    for step, index in enumerate(indices):
+        index[0] = masks[step] - 1
+    plan[at.place] = place
     traced = []
     for slot in range(requests):
         group, where = here, jnp.int32(slot)
@@ -92,32 +123,28 @@
             source = jnp.where(movers[earlier, here] == mover, earlier, source)
         plan[at.mover + step] = mover
         plan[at.source + step] = source
-    for copy in copies:
-        copy.wait()
+    for c, out in enumerate(outs):
+        pltpu.make_async_copy(out, out, sems.at[c]).wait()
 
 
 def pick_kernel(at, step, choices, plan, *refs):
     sources, outs, sems = refs[: 2 * step + 2], refs[-1 - len(choices) : -1], refs[-1]
     mover, source, place = plan[at.mover + step], plan[at.source + step], plan[at.place]
+    half = lax.axis_size("ctx") // 2
     for code in range(-1, step):
+        pair = sources[2 * code + 2 : 2 * code + 4]
 
         @pl.when(source == code)
         def _():
-            for c, (out, (kinds, pieces)) in enumerate(zip(outs, choices)):
-                for m, kind in enumerate(kinds):
-                    view = sources[2 * code + 2 + kind]
-                    view = view.at[0, mover] if code < 0 else view
-                    if pieces is None:
-                        pltpu.make_async_copy(view, out, sems.at[c]).start()
-                        continue
-                    wide = out.shape[2] // len(pieces)
-                    for p, piece in enumerate(pieces):
-                        begin = pl.multiple_of((place ^ piece) * wide, wide)
-                        pltpu.make_async_copy(
-                            view.at[:, pl.ds(begin, wide)],
-                            out.at[m, :, pl.ds(p * wide, wide)],
-                            sems.at[c],
-                        ).start()
+            for c, (out, pieces) in enumerate(zip(outs, choices)):
+                if code < 0:
+                    views = [view.at[0, mover] for view in pair]
+                    copy_pieces(views, out, sems.at[c], place, pieces[0])
+                else:
+                    far = pieces[0] >= half
+                    begin = (pieces[0] - half * far) * (out.shape[2] // len(pieces))
+                    view = pair[0 if far else 1].at[:, :, pl.ds(begin, out.shape[2])]
+                    pltpu.make_async_copy(view, out, sems.at[c]).start()
 
     for c, out in enumerate(outs):
         pltpu.make_async_copy(out, out, sems.at[c]).wait()
@@ -125,21 +152,25 @@
 
 def stage(at, plan, position, newest, sources, bufs, sems):
     rows = bufs[0].shape[0] // at.nblocks
-    slot, last = plan[at.slot + position], plan[at.last + position]
+    slot, last, place = plan[at.slot + position], plan[at.last + position], plan[at.place]
+    half = lax.axis_size("ctx") // 2
     for code in range(-1, newest + 1):
 
         @pl.when(last == code)
         def _():
-            views = sources[2 * code + 2 : 2 * code + 4]
-            views = [view.at[0, slot] if code < 0 else view for view in views]
+            pair = sources[2 * code + 2 : 2 * code + 4]
 
             def block(b, carry):
                 begin = pl.multiple_of(plan[at.perm + position * at.nblocks + b] * rows, rows)
                 into = pl.ds(pl.multiple_of(b * rows, rows), rows)
-                for n in range(2):
-                    pltpu.make_async_copy(
-                        views[n].at[pl.ds(begin, rows)], bufs[n].at[into], sems[n]
-                    ).start()
+                if code < 0:
+                    for n in range(2):
+                        pltpu.make_async_copy(
+                            pair[n].at[0, slot, pl.ds(begin, rows)], bufs[n].at[into], sems[n]
+                        ).start()
+                else:
+                    for parcel, first in zip(pair, (half, 0)):
+                        place_pieces(parcel, bufs, sems, place, first, pl.ds(begin, rows), into)
                 return carry
 
             lax.fori_loop(0, at.nblocks, block, 0)
@@ -244,32 +275,33 @@
     out[:, size.own * HD :] = pack_stats(*stats, size.own).astype(BF16)
 
 
-def attend_kernel(at, size, first, newest, pieces, kinds, plan, *refs):
+def attend_kernel(at, size, first, newest, pieces, partial, plan, *refs):
     count, some = len(newest), len(pieces)
     q_refs, (new_k, new_v), refs = refs[:some], refs[some : some + 2], refs[some + 2 :]
     outs, (kbuf, vbuf, qbuf, obuf, sems) = refs[-5 - some : -5], refs[-5:]
     sources = refs[: -5 - some]
-    partial = kinds is not None
     place = plan[at.place]
-
-    def start(view, buf, sem):
-        pltpu.make_async_copy(view, buf.at[pl.ds(0, size.segment)], sem).start()
+    half = size.width // 2
 
     for n in range(count):
         slot, last = plan[at.slot + first + n], plan[at.last + first + n]
-        bufs = (kbuf.at[n], vbuf.at[n])
+        bufs = [buf.at[n, pl.ds(0, size.segment)] for buf in (kbuf, vbuf)]
+        marks = [sems.at[m, n] for m in range(2)]
         if partial:
-            for held, ref in zip(kinds, sources):
-                for m, kind in enumerate(held):
-                    start(ref.at[m], bufs[kind], sems.at[kind, n])
+            for m in range(2):
+                pltpu.make_async_copy(sources[0].at[m], bufs[m], marks[m]).start()
         else:
             for code in range(-1, newest[n] + 1):
 
                 @pl.when(last == code)
                 def _():
-                    for m in range(2):
-                        view = sources[2 * code + 2 + m]
-                        start(view.at[0, slot] if code < 0 else view, bufs[m], sems.at[m, n])
+                    pair = sources[2 * code + 2 : 2 * code + 4]
+                    if code < 0:
+                        for m in range(2):
+                            pltpu.make_async_copy(pair[m].at[0, slot], bufs[m], marks[m]).start()
+                    else:
+                        for parcel, begin in zip(pair, (half, 0)):
+                            place_pieces(parcel, bufs, marks, place, begin)
 
         for p in range(some):
             pltpu.make_async_copy(q_refs[p].at[0, slot], qbuf.at[n, p], sems.at[2, n]).start()
@@ -359,13 +391,13 @@
     arrived, refs = refs[:some], refs[some:]
     sources, refs = refs[: 2 * len(parcels_before(ready))], refs[2 * len(parcels_before(ready)) :]
     query, new_k, new_v = refs[:3]
-    pieces, refs = refs[3:-13], refs[-11:]
+    pieces, refs = refs[3:-14], refs[-12:]
     attended, after = refs[0], refs[1:3]
-    kbuf, vbuf, qbuf, pbuf, full, sems, out_sems, in_sems = refs[3:]
+    kbuf, vbuf, qbuf, pbuf, mixed, full, sems, out_sems, in_sems = refs[3:]
     place, slot = plan[at.place], plan[at.slot + count]
     copies = [
-        pltpu.make_async_copy(view, buf.at[pl.ds(0, size.segment)], in_sems.at[m])
-        for m, (view, buf) in enumerate(zip(own_parcel(parcels, arrived), (kbuf, vbuf)))
+        pltpu.make_async_copy(arrived[-1].at[m], buf.at[pl.ds(0, size.segment)], in_sems.at[m])
+        for m, buf in enumerate((kbuf, vbuf))
     ]
     copies.append(pltpu.make_async_copy(query.at[0, slot], qbuf, in_sems.at[2]))
     for copy in copies:
@@ -383,19 +415,14 @@
         marks = [sems.at[n, position - settled] for n in range(2)]
         stage(at, plan, position, ready[position], sources, bufs, marks)
     rows = size.segment // at.nblocks
+    bufs = [full.at[n, count - settled] for n in range(2)]
+    marks = [sems.at[n, count - settled] for n in range(2)]
 
     def block(b, carry):
         begin = pl.multiple_of(plan[at.perm + count * at.nblocks + b] * rows, rows)
         into = pl.ds(pl.multiple_of(b * rows, rows), rows)
-        for (kinds, parcel), ref in zip(parcels, arrived):
-            for m, n in enumerate(kinds):
-                for p, piece in enumerate(parcel):
-                    cols, whole = own_columns(size, place, p, piece)
-                    pltpu.make_async_copy(
-                        ref.at[m, pl.ds(begin, rows), cols],
-                        full.at[n, count - settled, into, whole],
-                        sems.at[n, count - settled],
-                    ).start()
+        for parcel, ref in zip(parcels, arrived):
+            place_pieces(ref, bufs, marks, place, parcel[0], pl.ds(begin, rows), into)
         return carry
 
     lax.fori_loop(0, at.nblocks, block, 0)
@@ -404,9 +431,18 @@
     place_new(new_v, slot, vbuf, spans)
     bias = bias_of(at, size, plan, count, place)
     new_bias = new_bias_of(size, place)
-    for copy in copies:
-        copy.wait()
-    attend_owner(size, qbuf, kbuf, vbuf, 0, bias, new_bias, pbuf.at[0, count], True)
+    theirs = (pbuf.at[0, pl.ds(0, count)], pbuf.at[pl.ds(1, size.width - 1)])
+    for view in theirs:
+        pltpu.make_async_copy(view, view, in_sems.at[3]).wait()
+
+    def request(n, carry):
+        parts = [pbuf.at[i, n] for i in range(size.width)]
+        combined(parts, size.own, mixed.at[n])
+        there = attended.at[0, plan[at.slot + n]]
+        pltpu.make_async_copy(mixed.at[n], there, in_sems.at[4]).start()
+        return carry
+
+    lax.fori_loop(0, count, request, 0)
     for position in range(settled, count + 1):
         there = plan[at.slot + position]
         for n in range(2):
@@ -415,16 +451,10 @@
             pltpu.make_async_copy(
                 view, after[n].at[0, there], out_sems.at[n, position - settled]
             ).start()
-    theirs = (pbuf.at[0, pl.ds(0, count)], pbuf.at[pl.ds(1, size.width - 1)])
-    for view in theirs:
-        pltpu.make_async_copy(view, view, in_sems.at[3]).wait()
-
-    def request(n, carry):
-        parts = [pbuf.at[i, n] for i in range(size.width)]
-        combined(parts, size.own, attended.at[0, plan[at.slot + n]])
-        return carry
-
-    lax.fori_loop(0, count + 1, request, 0)
+    for copy in copies:
+        copy.wait()
+    attend_owner(size, qbuf, kbuf, vbuf, 0, bias, new_bias, pbuf.at[0, count], True)
+    lax.fori_loop(count, count + 1, request, 0)
     for position in range(settled, count + 1):
         there = plan[at.slot + position]
         for n in range(2):
@@ -432,17 +462,11 @@
             pltpu.make_async_copy(
                 view, after[n].at[0, there], out_sems.at[n, position - settled]
             ).wait()
+    pltpu.make_async_copy(mixed, mixed, in_sems.at[4]).wait()
 
 
 def parcels_before(ready):
     return range(-1, max(ready))
-
-
-def own_parcel(parcels, arrived):
-    for n in range(2):
-        for (kinds, parcel), ref in zip(parcels, arrived):
-            if parcel == (0,) and n in kinds:
-                yield ref.at[kinds.index(n)]
 
 
 def shards(
@@ -461,18 +485,25 @@
     big = pltpu.CompilerParams(vmem_limit_bytes=40 * 1024 * 1024)
     result = jax.ShapeDtypeStruct((tokens, own * HD + LANES), BF16)
     everyone = tuple(range(width))
-    far, near = everyone[(width + 1) // 2 :], everyone[1 : (width + 1) // 2]
-    parcels = [((0,), far), ((1,), far), ((0, 1), near), ((0, 1), (0,))]
-
-    request = jax.ShapeDtypeStruct((segment, features), BF16)
-    plan, *moving = pl.pallas_call(
-        functools.partial(plan_kernel, at),
-        out_shape=(jax.ShapeDtypeStruct((at.size,), jnp.int32), request, request),
+    halves = [part for part in (everyone[width // 2 :], everyone[: width // 2]) if part]
+    parcels = [part for part in (halves[0], everyone[1 : width // 2], (0,)) if part]
+
+    def held(pieces):
+        return jax.ShapeDtypeStruct((2, segment, len(pieces) * size.wide), BF16)
+
+    plan, *scalars = pl.pallas_call(
+        functools.partial(plan_kernel, at, halves),
+        out_shape=(
+            jax.ShapeDtypeStruct((at.size,), jnp.int32),
+            *[jax.ShapeDtypeStruct((1,), jnp.int32)] * matchings,
+            *map(held, halves),
+        ),
         in_specs=[SMEM] * 4 + [ANY] * 2,
-        out_specs=(SMEM, VMEM, VMEM),
-        scratch_shapes=[pltpu.SemaphoreType.DMA((2,))],
+        out_specs=(SMEM, *[SMEM] * matchings, *[VMEM] * len(halves)),
+        scratch_shapes=[pltpu.SemaphoreType.DMA((len(halves),))],
         name="plan",
     )(masks, movers, block_lists.transpose(0, 2, 1), lengths.T, *caches)
+    indices, initial = scalars[:matchings], scalars[matchings:]
 
     def lasting(microseconds):
         return pl.CostEstimate(
@@ -480,34 +511,24 @@
         )
 
     def pick(step, choices, sources, after=()):
-        shapes = [
-            (len(kinds), segment, len(pieces) * size.wide) if pieces else (segment, features)
-            for kinds, pieces in choices
-        ]
-        wanted = {kind for kinds, _ in choices for kind in kinds}
-        used = [
-            sources[2 * n + (kind if kind in wanted else 1 - kind)]
-            for n in range(step + 1)
-            for kind in range(2)
-        ]
         return pl.pallas_call(
             functools.partial(pick_kernel, at, step, choices),
-            out_shape=[jax.ShapeDtypeStruct(shape, BF16) for shape in shapes],
-            in_specs=[SMEM] + [ANY] * (len(used) + len(after)),
+            out_shape=list(map(held, choices)),
+            in_specs=[SMEM] + [ANY] * (len(sources) + len(after)),
             out_specs=[VMEM] * len(choices),
             scratch_shapes=[pltpu.SemaphoreType.DMA((len(choices),))],
             cost_estimate=lasting(2.5),
             name=f"pick_{step}",
-        )(plan, *used, *after)
-
-    def attend(first, count, pieces, asked, fresh, sources, kinds=None, after=()):
+        )(plan, *sources, *after)
+
+    def attend(first, count, pieces, asked, fresh, sources, partial=False, after=()):
         newest = ready[first : first + count]
-        if kinds is None:
+        if not partial:
             sources = sources[: 2 * (max(newest) + 2)]
-        held = sources[0].shape[-1]
         some = len(pieces)
+        held = some * size.wide if partial else features
         return pl.pallas_call(
-            functools.partial(attend_kernel, at, size, first, newest, pieces, kinds),
+            functools.partial(attend_kernel, at, size, first, newest, pieces, partial),
             out_shape=[jax.ShapeDtypeStruct((count, *result.shape), BF16)] * some,
             in_specs=[SMEM] + [ANY] * some + [VMEM] * 2 + [ANY] * (len(sources) + len(after)),
             out_specs=[ANY] * some,
@@ -548,51 +569,44 @@
         extra = -new_keys.shape[2] % 16
         return [jnp.pad(new[0], ((0, 0), (0, extra), (0, 0))) for new in (new_keys, new_values)]
 
-    def choices(step):
-        return parcels if step == matchings - 1 else [((0,), None), ((1,), None)]
-
-    def prepare(step, sources):
-        return pick(step, choices(step)[:1], sources)[0]
+    def prepare(step, sources, arrived):
+        return pick(step, halves[:1], [*sources, arrived[0], arrived[0]])[0]
 
     def first_branch(mask):
-        arrived = [exchange(block, "group", mask) for block in moving]
-        asked = [query] + [exchange(query, "ctx", piece) for piece in everyone[1:]]
-        return arrived, prepare(1, [*caches, *arrived]), asked, pad_new()
+        arrived = [exchange(block, "group", mask) for block in initial]
+        asked = [query] + [exchange(query, "ctx", piece) for piece in everyone[1:-1]]
+        return arrived, prepare(1, caches, arrived), asked, pad_new()
 
     def middle_branch(step, positions, prepared, asked, fresh, sources, mask):
-        moving = [prepared, *pick(step, choices(step)[1:], sources)]
+        moving = [prepared, *pick(step, halves[1:], sources)]
         arrived = [exchange(block, "group", mask) for block in moving]
         done = send_home(
             everyone, attend(positions[0], len(positions), everyone, asked, fresh, sources)
         )
         after = settle(positions, sources) if step == 1 else []
-        return arrived, prepare(step + 1, sources + arrived), done, after
+        return arrived, prepare(step + 1, sources, arrived), done, after
 
     def last_branch(step, first, prepared, asked, fresh, sources, mask):
-        second = pick(step, parcels[1:2], sources)
-        moving = [prepared, *second, *pick(step, parcels[2:], sources, second)]
+        whole = attend(first, 1, everyone, asked, fresh, sources)
+        moving = [prepared, *pick(step, parcels[1:], sources, whole[:1])]
         arrived = [exchange(block, "group", mask) for block in moving]
-        done = send_home(everyone, attend(first, 1, everyone, asked, fresh, sources))
-        most = attend(
-            requests - 1, 1, far, asked, fresh, arrived[:2], [(0,), (1,)], done[:1]
-        )
-        parts = dict(zip(far, send_home(far, most)))
-        if near:
-            rest = attend(
-                requests - 1, 1, near, asked, fresh, arrived[2:3], [(0, 1)], most[:1]
-            )
-            parts.update(zip(near, send_home(near, rest)))
+        done = send_home(everyone, whole)
+        parts, after = {}, done[:1]
+        for parcel, block in zip(parcels[:-1], arrived):
+            part = attend(requests - 1, 1, parcel, asked, fresh, [block], True, after)
+            parts.update(zip(parcel, send_home(parcel, part)))
+            after = [*part[:1], *done[1:]]
         return arrived, done, [parts[piece] for piece in everyone[1:]]
-
-    indices = masks - 1
 
     def switch(step, branch, *given):
         return lax.switch(
-            indices[step],
+            indices[step].reshape(()),
             [functools.partial(branch, *given, mask) for mask in range(1, groups)],
         )
 
+    ahead = exchange(query, "ctx", width - 1)
     arrived, prepared, asked, fresh = switch(0, first_branch)
+    asked = [*asked, ahead]
     sources = [*caches, *arrived]
     lots, done, after = [], [], None
     for step in range(1, matchings - 1):
@@ -621,16 +635,17 @@
         + [ANY] * (len(arrived) + len(sources) + 1)
         + [VMEM] * 2
         + [ANY] * (len(pieces) + 2),
-        out_specs=[VMEM, ANY, ANY],
+        out_specs=[ANY] * 3,
         scratch_shapes=[
             pltpu.VMEM((segment + LANES, size.wide), BF16),
             pltpu.VMEM((segment + LANES, size.wide), BF16),
             pltpu.VMEM((tokens, own * HD), BF16),
             pltpu.VMEM((width, requests, *result.shape), BF16),
+            pltpu.VMEM((requests, tokens, own * HD), BF16),
             pltpu.VMEM((2, left, segment, features), BF16),
             pltpu.SemaphoreType.DMA((2, left)),
             pltpu.SemaphoreType.DMA((2, left)),
-            pltpu.SemaphoreType.DMA((4,)),
+            pltpu.SemaphoreType.DMA((5,)),
         ],
         input_output_aliases={ahead: 1, ahead + 1: 2},
         compiler_params=big,

time: 169 us -> 164 us (0.970)
  starting transfers between devices: 28.8 us -> 23.5 us
  waiting for transfers between devices: 82.6 us -> 86.4 us
  Pallas kernels: 53.2 us -> 50 us
    ppermute x20 -> x19, starting transfers between devices: 28.8 us -> 23.5 us  [exchange(): lax.ppermute(block, axis, [(i, i ^ mask) for i in range(lax.axis_size(axi...]
    ppermute x20 -> x19, waiting for transfers between devices: 82.6 us -> 86.4 us  [exchange(): lax.ppermute(block, axis, [(i, i ^ mask) for i in range(lax.axis_size(axi...]
    pallas_call x5 -> x4, Pallas kernels: 11.3 us -> 9.05 us  [pick(): pl.pallas_call(functools.partial(pick_kernel, at, step, choices), out_sha...]
  transfers between devices with their start and end apart: 20 -> 19, of which waited for: 12 -> 11; matrix products, arithmetic and copies ran while one was open for 0% -> 0% of each run, Pallas kernels for 24% -> 27%
where the time goes in v3:
time: 164 us; the launch traced here: 163 us
  waiting for transfers between devices  86.4 us (53%)
  Pallas kernels  50 us (30%)
  starting transfers between devices  23.5 us (14%)
  between operations  2.86 us (2%)
    ppermute x19, waiting for transfers between devices, exchange(): lax.ppermute(block, axis, [(i, i ^ mask) for i in range(lax.axis_size(axi...  86.4 us
    pallas_call x4, Pallas kernels, attend(): pl.pallas_call(functools.partial(attend_kernel, at, size, first, newest,...  28.5 us
    ppermute x19, starting transfers between devices, exchange(): lax.ppermute(block, axis, [(i, i ^ mask) for i in range(lax.axis_size(axi...  23.5 us
    pallas_call x4, Pallas kernels, pick(): pl.pallas_call(functools.partial(pick_kernel, at, step, choices), out_sha...  9.05 us
    pallas_call x1, Pallas kernels, shards(): pl.pallas_call(functools.partial(finish_kernel, at, size, parcels, lots,...  5.95 us
    pallas_call x1, Pallas kernels, shards(): pl.pallas_call(functools.partial(plan_kernel, at, halves), out_shape=(jax...  3.52 us
  transfers between devices with their start and end apart: 19, of which 11 were waited for; matrix products, arithmetic and copies ran while one was open for 0% of the time, Pallas kernels for 27%

profile of v3, /device:TPU:0, one launch (start us, length us, event | category | flops | bytes accessed | tf_op | source)
XLA Modules:
  0.0 163.0 jit_solution(10105070213859398969)
XLA Ops:
  0.6 5.1 %collective-permute-start.126 = (bf16[1,4,32,2048]{3,2,1,0:T(8,128)(2,1)}, bf16[1,4,32,2048]{3,2,1,0:T(8,128)(2,1)S(1)}, u32[]{:S(2)}, u32[]{:S(2)}) collective-permute-start(bf16[1,4,32,2048]{3,2,1,0:T(8,128)(2,1)} %refs_9_.1), channel_id=1, source_target_pairs={{0,3},{1,2},{2,1},{3,0},{4,7},{5,6},{6,5},{7,4},{8,11},{9,10},{10,... | collective-permute-start | bytes 1572872 | tf_op jit(solution)/shard_map/ppermute | solution.py:23
  5.8 3.5 %plan.1 = (s32[51]{0:T(128)S(1)}, s32[1]{0:T(128)}, s32[1]{0:T(128)}, s32[1]{0:T(128)}, bf16[2,512,512]{2,1,0:T(8,128)(2,1)S(1)}, /*index=5*/bf16[2,512,512]{2,1,0:T(8,128)(2,1)}) custom-call(s32[3]{0:T(128)} %masks.1, s32[3,8]{1,0:T(4,128)} %movers.1, s32[3,4,8]{2,1,0:T(4,128)} %bitcast.33, s32[4,8]{1,0:T(4,128)} %bitcast.34, ...), custom_call_target="tpu_custom_call" | custom-call | tf_op jit(solution)/shard_map/plan/pallas_call | solution.py:494
  11.3 48.9 %conditional.3 = (bf16[2,512,512]{2,1,0:T(8,128)(2,1)}, bf16[2,512,512]{2,1,0:T(8,128)(2,1)}, bf16[2,512,512]{2,1,0:T(8,128)(2,1)S(1)}, bf16[1,4,32,2048]{3,2,1,...) conditional(s32[]{:T(128)} %bitcast.18, ...), branch_computations={%region_0.1_spmd, %region_1.2_spmd, %region_2.3_spmd, %region_3.4_... | conditional | bytes 22226348 | solution.py:602
  11.3 1.7 %collective-permute-start.24 = (bf16[2,512,512]{2,1,0:T(8,128)(2,1)S(1)}, bf16[2,512,512]{2,1,0:T(8,128)(2,1)}, u32[]{:S(2)}, u32[]{:S(2)}) collective-permute-start(bf16[2,512,512]{2,1,0:T(8,128)(2,1)S(1)} %get-tuple-element.524), channel_id=1, source_target_pairs={{0,28},{4,24},{8,20},{12,16},{16,12},{20,8},{24,4},{28,0},{1,29},{... | collective-permute-start | bytes 3145736 | tf_op jit(solution)/shard_map/cond/branch_6_fun/ppermute | solution.py:23
  13.0 1.0 collective-permute-start.25
  14.7 23.1 %collective-permute-done.24.refs_2_.refs_3_ = bf16[2,512,512]{2,1,0:T(8,128)(2,1)} collective-permute-done((bf16[2,512,512]{2,1,0:T(8,128)(2,1)S(1)}, bf16[2,512,512]{2,1,0:T(8,128)(2,1)}, u32[]{:S(2)}, u32[]{:S(2)}) %collective-permute-start.24) | collective-permute-done | bytes 1048608 | tf_op jit(solution)/shard_map/cond/branch_6_fun/ppermute | solution.py:23
  37.8 1.8 %pick_1.20 = bf16[2,512,512]{2,1,0:T(8,128)(2,1)S(1)} custom-call(s32[51]{0:T(128)S(1)} %get-tuple-element.526.plan, bf16[1,4,512,1024]{3,2,1,0:T(8,128)(2,1)} %get-tuple-element.527.refs_0_, bf16[1,4,512,1024]{3,2,1,0:T(8,128)(2,1)} %get-tuple-element.528.refs_1_, bf16[2,512,512]{2,1,0:T(8,128)(2,1)} %collective-permute-done.24.refs_2_.refs_3_, ...), custom_call_target="tpu_custom_call" | custom-call | bytes 9250000 | tf_op jit(solution)/shard_map/cond/branch_6_fun/pick_1/pallas_call | solution.py:514
  39.5 11.3 %collective-permute-done.27 = bf16[1,4,32,2048]{3,2,1,0:T(8,128)(2,1)} collective-permute-done((bf16[1,4,32,2048]{3,2,1,0:T(8,128)(2,1)S(1)}, bf16[1,4,32,2048]{3,2,1,0:T(8,128)(2,1)}, u32[]{:S(2)}, u32[]{:S(2)}) %collective-permute-start.27) | collective-permute-done | bytes 524320 | tf_op jit(solution)/shard_map/cond/branch_6_fun/ppermute | solution.py:23
  50.8 9.4 %collective-permute-done.25 = bf16[2,512,512]{2,1,0:T(8,128)(2,1)} collective-permute-done((bf16[2,512,512]{2,1,0:T(8,128)(2,1)}, bf16[2,512,512]{2,1,0:T(8,128)(2,1)}, u32[]{:S(2)}, u32[]{:S(2)}) %collective-permute-start.25) | collective-permute-done | bytes 1048608 | tf_op jit(solution)/shard_map/cond/branch_6_fun/ppermute | solution.py:23
  60.2 47.7 %conditional.4 = (bf16[2,512,512]{2,1,0:T(8,128)(2,1)}, bf16[2,512,512]{2,1,0:T(8,128)(2,1)}, bf16[2,512,512]{2,1,0:T(8,128)(2,1)S(1)}, bf16[2,32,2176]{2,1,0:T(...) conditional(s32[]{:T(128)} %bitcast.17, ...), branch_computations={%region_7.8_spmd, %region_8.9_spmd, %region_9.10_spmd, %region_10.... | conditional | bytes 126685712 | solution.py:602
  61.0 2.8 %pick_1.23 = bf16[2,512,512]{2,1,0:T(8,128)(2,1)} custom-call(s32[51]{0:T(128)S(1)} %get-tuple-element.569.plan, bf16[1,4,512,1024]{3,2,1,0:T(8,128)(2,1)} %get-tuple-element.570.refs_0_.refs_6_, bf16[1,4,512,1024]{3,2,1,0:T(8,128)(2,1)} %get-tuple-element.571.refs_1_.refs_7_, bf16[2,512,512]{2,1,0:T(8,128)(2,1)} %get-tuple-element.572.refs_2_.refs_8_, ...), custom_call_target="tpu_custom_call" | custom-call | bytes 9250000 | tf_op jit(solution)/shard_map/cond/branch_2_fun/pick_1/pallas_call | solution.py:514
  63.8 1.1 collective-permute-start.39
  64.9 12.8 %attend_0_2_4.9 = (bf16[2,32,2176]{2,1,0:T(8,128)(2,1)S(1)}, bf16[2,32,2176]{2,1,0:T(8,128)(2,1)S(1)}, bf16[2,32,2176]{2,1,0:T(8,128)(2,1)S(1)}, bf16[2,32,2176]{2,1,0:T(8,128)(2,1)S(1)}) custom-call(s32[51]{0:T(128)S(1)} %get-tuple-element.569.plan, bf16[1,4,32,2048]{3,2,1,0:T(8,128)(2,1)S(1)} %get-tuple-element.574.refs_0_, ...), custom_call_target="tpu_custom_call" | custom-call | bytes 48100000 | tf_op jit(solution)/shard_map/cond/branch_2_fun/attend_0_2_4/pallas_call | solution.py:530
  78.1 4.0 %collective-permute-start.42 = (bf16[2,32,2176]{2,1,0:T(8,128)(2,1)S(1)}, bf16[2,32,2176]{2,1,0:T(8,128)(2,1)}, u32[]{:S(2)}, u32[]{:S(2)}) collective-permute-start(bf16[2,32,2176]{2,1,0:T(8,128)(2,1)S(1)} %get-tuple-element.583), channel_id=1, source_target_pairs={{0,3},{1,2},{2,1},{3,0},{4,7},{5,6},{6,5},{7,4},{8,11},{9,10},{10,... | collective-permute-start | bytes 835592 | tf_op jit(solution)/shard_map/cond/branch_2_fun/ppermute | solution.py:23
  82.2 3.0 %settle.9 = (bf16[1,4,512,1024]{3,2,1,0:T(8,128)(2,1)}, bf16[1,4,512,1024]{3,2,1,0:T(8,128)(2,1)}) custom-call(s32[51]{0:T(128)S(1)} %get-tuple-element.569.plan, bf16[1,4,512,1024]{3,2,1,0:T(8,128)(2,1)S(1)} %copy-done.2, bf16[1,4,512,1024]{3,2,1,0:T(8,128)(2,1)S(1)} %copy-done.9, bf16[2,512,512]{2,1,0:T(8,128)(2,1)} %get-tuple-element.572.refs_2_.refs_8_, ...), custom_call_target="tpu_custom_call" | custom-call | bytes 14800000 | tf_op jit(solution)/shard_map/cond/branch_2_fun/settle/pallas_call | solution.py:554
  85.5 1.8 %pick_2.16 = bf16[2,512,512]{2,1,0:T(8,128)(2,1)S(1)} custom-call(s32[51]{0:T(128)S(1)} %get-tuple-element.569.plan, bf16[1,4,512,1024]{3,2,1,0:T(8,128)(2,1)} %get-tuple-element.570.refs_0_.refs_6_, bf16[1,4,512,1024]{3,2,1,0:T(8,128)(2,1)} %get-tuple-element.571.refs_1_.refs_7_, bf16[2,512,512]{2,1,0:T(8,128)(2,1)} %get-tuple-element.572.refs_2_.refs_8_, ...), custom_call_target="tpu_custom_call" | custom-call | bytes 9250000 | tf_op jit(solution)/shard_map/cond/branch_2_fun/pick_2/pallas_call | solution.py:514
  87.3 3.1 %collective-permute-done.40 = bf16[2,32,2176]{2,1,0:T(8,128)(2,1)} collective-permute-done((bf16[2,32,2176]{2,1,0:T(8,128)(2,1)S(1)}, bf16[2,32,2176]{2,1,0:T(8,128)(2,1)}, u32[]{:S(2)}, u32[]{:S(2)}) %collective-permute-start.40) | collective-permute-done | bytes 278560 | tf_op jit(solution)/shard_map/cond/branch_2_fun/ppermute | solution.py:23
  90.4 9.9 %collective-permute-done.41 = bf16[2,32,2176]{2,1,0:T(8,128)(2,1)} collective-permute-done((bf16[2,32,2176]{2,1,0:T(8,128)(2,1)S(1)}, bf16[2,32,2176]{2,1,0:T(8,128)(2,1)}, u32[]{:S(2)}, u32[]{:S(2)}) %collective-permute-start.41) | collective-permute-done | bytes 278560 | tf_op jit(solution)/shard_map/cond/branch_2_fun/ppermute | solution.py:23
  100.3 7.6 %collective-permute-done.39 = bf16[2,512,512]{2,1,0:T(8,128)(2,1)} collective-permute-done((bf16[2,512,512]{2,1,0:T(8,128)(2,1)}, bf16[2,512,512]{2,1,0:T(8,128)(2,1)}, u32[]{:S(2)}, u32[]{:S(2)}) %collective-permute-start.39) | collective-permute-done | bytes 1048608 | tf_op jit(solution)/shard_map/cond/branch_2_fun/ppermute | solution.py:23
  108.0 48.9 %conditional.5 = (bf16[2,512,512]{2,1,0:T(8,128)(2,1)}, bf16[2,512,256]{2,1,0:T(8,128)(2,1)}, bf16[2,512,256]{2,1,0:T(8,128)(2,1)}, bf16[1,32,2176]{2,1,0:T(8,12...) conditional(s32[]{:T(128)} %bitcast.16, ...), branch_computations={%region_14.15_spmd, %region_15.16_spmd, %region_16.17_spmd, %regio... | conditional | bytes 70931384 | solution.py:602
  108.0 1.6 collective-permute-start.72
  109.6 8.0 %attend_2_1_4.8 = (bf16[1,32,2176]{2,1,0:T(8,128)(2,1)}, bf16[1,32,2176]{2,1,0:T(8,128)(2,1)S(1)}, bf16[1,32,2176]{2,1,0:T(8,128)(2,1)S(1)}, bf16[1,32,2176]{2,1,0:T(8,128)(2,1)S(1)}) custom-call(s32[51]{0:T(128)S(1)} %get-tuple-element.681.plan, bf16[1,4,32,2048]{3,2,1,0:T(8,128)(2,1)S(1)} %get-tuple-element.688.refs_0_, ...), custom_call_target="tpu_custom_call" | custom-call | bytes 25900000 | tf_op jit(solution)/shard_map/cond/branch_1_fun/attend_2_1_4/pallas_call | solution.py:530
  117.6 2.7 %pick_2.22 = (bf16[2,512,256]{2,1,0:T(8,128)(2,1)}, bf16[2,512,256]{2,1,0:T(8,128)(2,1)}) custom-call(s32[51]{0:T(128)S(1)} %get-tuple-element.681.plan, bf16[1,4,512,1024]{3,2,1,0:T(8,128)(2,1)} %get-tuple-element.682.refs_6_.refs_0_, bf16[1,4,512,1024]{3,2,1,0:T(8,128)(2,1)} %get-tuple-element.683.refs_7_.refs_1_, ...), custom_call_target="tpu_custom_call" | custom-call | bytes 9250000 | tf_op jit(solution)/shard_map/cond/branch_1_fun/pick_2/pallas_call | solution.py:514
  120.9 1.6 collective-permute-start.74
  123.3 10.8 %collective-permute-done.72.refs_4_ = bf16[2,512,512]{2,1,0:T(8,128)(2,1)} collective-permute-done((bf16[2,512,512]{2,1,0:T(8,128)(2,1)S(1)}, bf16[2,512,512]{2,1,0:T(8,128)(2,1)}, u32[]{:S(2)}, u32[]{:S(2)}) %collective-permute-start.72) | collective-permute-done | bytes 1048608 | tf_op jit(solution)/shard_map/cond/branch_1_fun/ppermute | solution.py:23
  134.1 4.6 %attend_3_1_2.8 = (bf16[1,32,2176]{2,1,0:T(8,128)(2,1)S(1)}, bf16[1,32,2176]{2,1,0:T(8,128)(2,1)S(1)}) custom-call(s32[51]{0:T(128)S(1)} %get-tuple-element.681.plan, bf16[1,4,32,2048]{3,2,1,0:T(8,128)(2,1)} %get-tuple-element.690.refs_2_.refs_0_, bf16[1,4,32,2048]{3,2,1,0:T(8,128)(2,1)S(1)} %get-tuple-element.691.refs_3_.refs_1_, ...), custom_call_target="tpu_custom_call" | custom-call | bytes 14800000 | tf_op jit(solution)/shard_map/cond/branch_1_fun/attend_3_1_2/pallas_call | solution.py:530
  138.8 3.9 %collective-permute-start.80 = (bf16[1,32,2176]{2,1,0:T(8,128)(2,1)S(1)}, bf16[1,32,2176]{2,1,0:T(8,128)(2,1)}, u32[]{:S(2)}, u32[]{:S(2)}) collective-permute-start(bf16[1,32,2176]{2,1,0:T(8,128)(2,1)S(1)} %get-tuple-element.701), channel_id=1, source_target_pairs={{0,3},{1,2},{2,1},{3,0},{4,7},{5,6},{6,5},{7,4},{8,11},{9,10},{10,... | collective-permute-start | bytes 417800 | tf_op jit(solution)/shard_map/cond/branch_1_fun/ppermute | solution.py:23
  142.7 2.7 %collective-permute-done.73.refs_3_ = bf16[2,512,256]{2,1,0:T(8,128)(2,1)} collective-permute-done((bf16[2,512,256]{2,1,0:T(8,128)(2,1)}, bf16[2,512,256]{2,1,0:T(8,128)(2,1)}, u32[]{:S(2)}, u32[]{:S(2)}) %collective-permute-start.73) | collective-permute-done | bytes 524320 | tf_op jit(solution)/shard_map/cond/branch_1_fun/ppermute | solution.py:23
  145.3 3.0 %attend_3_1_1.8 = bf16[1,32,2176]{2,1,0:T(8,128)(2,1)S(1)} custom-call(s32[51]{0:T(128)S(1)} %get-tuple-element.681.plan, bf16[1,4,32,2048]{3,2,1,0:T(8,128)(2,1)} %get-tuple-element.689.refs_1_.refs_0_, bf16[4,16,1024]{2,1,0:T(8,128)(2,1)S(1)} %get-tuple-element.692.refs_4_.refs_2_.refs_1_, ...), custom_call_target="tpu_custom_call" | custom-call | bytes 9250000 | tf_op jit(solution)/shard_map/cond/branch_1_fun/attend_3_1_1/pallas_call | solution.py:530
  148.8 7.0 %collective-permute-done.74 = bf16[2,512,256]{2,1,0:T(8,128)(2,1)} collective-permute-done((bf16[2,512,256]{2,1,0:T(8,128)(2,1)}, bf16[2,512,256]{2,1,0:T(8,128)(2,1)}, u32[]{:S(2)}, u32[]{:S(2)}) %collective-permute-start.74) | collective-permute-done | bytes 524320 | tf_op jit(solution)/shard_map/cond/branch_1_fun/ppermute | solution.py:23
  155.7 1.1 collective-permute-done.79
  156.8 5.9 %finish.1 = (bf16[1,4,32,2048]{3,2,1,0:T(8,128)(2,1)}, bf16[1,4,512,1024]{3,2,1,0:T(8,128)(2,1)}, bf16[1,4,512,1024]{3,2,1,0:T(8,128)(2,1)}) custom-call(s32[51]{0:T(128)S(1)} %get-tuple-element.847.plan, bf16[2,512,512]{2,1,0:T(8,128)(2,1)} %get-tuple-element.863.refs_0_, ...), custom_call_target="tpu_custom_call", output_to_operand_aliasing={{1}: (24, {}), {2}: (25, {})} | custom-call | tf_op jit(solution)/shard_map/finish/pallas_call | solution.py:629
  (32 shorter events, 4.0 us)
Async XLA Ops:
  0.6 59.6 %collective-permute-start.126 = (bf16[1,4,32,2048]{3,2,1,0:T(8,128)(2,1)}, bf16[1,4,32,2048]{3,2,1,0:T(8,128)(2,1)S(1)}, u32[]{:S(2)}, u32[]{:S(2)}) collective-permute-start(bf16[1,4,32,2048]{3,2,1,0:T(8,128)(2,1)} %refs_9_.1), channel_id=1, source_target_pairs={{0,3},{1,2},{2,1},{3,0},{4,7},{5,6},{6,5},{7,4},{8,11},{9,10},{10,... | collective-permute-start | bytes 1572872 | tf_op jit(solution)/shard_map/ppermute | solution.py:23
  5.7 5.5 %copy-start.14 = (bf16[1,4,32,2048]{3,2,1,0:T(8,128)(2,1)S(1)}, bf16[1,4,32,2048]{3,2,1,0:T(8,128)(2,1)}, u32[]{:S(2)}) copy-start(bf16[1,4,32,2048]{3,2,1,0:T(8,128)(2,1)} %refs_9_.1) | copy-start | bytes 1572868
  5.7 5.5 %copy-start.15 = (bf16[1,4,8,1024]{3,2,1,0:T(8,128)(2,1)S(1)}, bf16[1,4,8,1024]{3,2,1,0:T(8,128)(2,1)}, u32[]{:S(2)}) copy-start(bf16[1,4,8,1024]{3,2,1,0:T(8,128)(2,1)} %param.33) | copy-start | bytes 196612
  5.8 5.5 %copy-start.16 = (bf16[1,4,8,1024]{3,2,1,0:T(8,128)(2,1)S(1)}, bf16[1,4,8,1024]{3,2,1,0:T(8,128)(2,1)}, u32[]{:S(2)}) copy-start(bf16[1,4,8,1024]{3,2,1,0:T(8,128)(2,1)} %param.34) | copy-start | bytes 196612
  11.3 26.4 %collective-permute-start.24 = (bf16[2,512,512]{2,1,0:T(8,128)(2,1)S(1)}, bf16[2,512,512]{2,1,0:T(8,128)(2,1)}, u32[]{:S(2)}, u32[]{:S(2)}) collective-permute-start(bf16[2,512,512]{2,1,0:T(8,128)(2,1)S(1)} %get-tuple-element.524), channel_id=1, source_target_pairs={{0,28},{4,24},{8,20},{12,16},{16,12},{20,8},{24,4},{28,0},{1,29},{... | collective-permute-start | bytes 3145736 | tf_op jit(solution)/shard_map/cond/branch_6_fun/ppermute | solution.py:23
  13.0 47.2 %collective-permute-start.25 = (bf16[2,512,512]{2,1,0:T(8,128)(2,1)}, bf16[2,512,512]{2,1,0:T(8,128)(2,1)}, u32[]{:S(2)}, u32[]{:S(2)}) collective-permute-start(bf16[2,512,512]{2,1,0:T(8,128)(2,1)} %get-tuple-element.525), channel_id=1, source_target_pairs={{0,28},{4,24},{8,20},{12,16},{16,12},{20,8},{24,4},{28,0},{1,29},{... | collective-permute-start | bytes 3145736 | tf_op jit(solution)/shard_map/cond/branch_6_fun/ppermute | solution.py:23
  14.1 36.8 %collective-permute-start.27 = (bf16[1,4,32,2048]{3,2,1,0:T(8,128)(2,1)S(1)}, bf16[1,4,32,2048]{3,2,1,0:T(8,128)(2,1)}, u32[]{:S(2)}, u32[]{:S(2)}) collective-permute-start(bf16[1,4,32,2048]{3,2,1,0:T(8,128)(2,1)S(1)} %get-tuple-element.529), channel_id=1, source_target_pairs={{0,2},{1,3},{2,0},{3,1},{4,6},{5,7},{6,4},{7,5},{8,10},{9,11},{10,... | collective-permute-start | bytes 1572872 | tf_op jit(solution)/shard_map/cond/branch_6_fun/ppermute | solution.py:23
  14.1 36.8 %collective-permute-start.26 = (bf16[1,4,32,2048]{3,2,1,0:T(8,128)(2,1)S(1)}, bf16[1,4,32,2048]{3,2,1,0:T(8,128)(2,1)}, u32[]{:S(2)}, u32[]{:S(2)}) collective-permute-start(bf16[1,4,32,2048]{3,2,1,0:T(8,128)(2,1)S(1)} %get-tuple-element.529), channel_id=1, source_target_pairs={{0,1},{1,0},{2,3},{3,2},{4,5},{5,4},{6,7},{7,6},{8,9},{9,8},{10,11... | collective-permute-start | bytes 1572872 | tf_op jit(solution)/shard_map/cond/branch_6_fun/ppermute | solution.py:23
  60.2 25.3 %collective-permute-start.38 = (bf16[2,512,512]{2,1,0:T(8,128)(2,1)S(1)}, bf16[2,512,512]{2,1,0:T(8,128)(2,1)}, u32[]{:S(2)}, u32[]{:S(2)}) collective-permute-start(bf16[2,512,512]{2,1,0:T(8,128)(2,1)S(1)} %get-tuple-element.568), channel_id=1, source_target_pairs={{0,12},{4,8},{8,4},{12,0},{16,28},{20,24},{24,20},{28,16},{1,13},{... | collective-permute-start | bytes 3145736 | tf_op jit(solution)/shard_map/cond/branch_2_fun/ppermute | solution.py:23
  63.8 44.2 %collective-permute-start.39 = (bf16[2,512,512]{2,1,0:T(8,128)(2,1)}, bf16[2,512,512]{2,1,0:T(8,128)(2,1)}, u32[]{:S(2)}, u32[]{:S(2)}) collective-permute-start(bf16[2,512,512]{2,1,0:T(8,128)(2,1)} %pick_1.23), channel_id=1, source_target_pairs={{0,12},{4,8},{8,4},{12,0},{16,28},{20,24},{24,20},{28,16},{1,13},{... | collective-permute-start | bytes 3145736 | tf_op jit(solution)/shard_map/cond/branch_2_fun/ppermute | solution.py:23
  64.9 17.3 %copy-start.2 = (bf16[1,4,512,1024]{3,2,1,0:T(8,128)(2,1)S(1)}, bf16[1,4,512,1024]{3,2,1,0:T(8,128)(2,1)}, u32[]{:S(2)}) copy-start(bf16[1,4,512,1024]{3,2,1,0:T(8,128)(2,1)} %get-tuple-element.570.refs_0_.refs_6_) | copy-start | bytes 12582916 | tf_op jit(solution)/shard_map/cond
  64.9 17.3 %copy-start.9 = (bf16[1,4,512,1024]{3,2,1,0:T(8,128)(2,1)S(1)}, bf16[1,4,512,1024]{3,2,1,0:T(8,128)(2,1)}, u32[]{:S(2)}) copy-start(bf16[1,4,512,1024]{3,2,1,0:T(8,128)(2,1)} %get-tuple-element.571.refs_1_.refs_7_) | copy-start | bytes 12582916 | tf_op jit(solution)/shard_map/cond
  77.7 12.7 %collective-permute-start.40 = (bf16[2,32,2176]{2,1,0:T(8,128)(2,1)S(1)}, bf16[2,32,2176]{2,1,0:T(8,128)(2,1)}, u32[]{:S(2)}, u32[]{:S(2)}) collective-permute-start(bf16[2,32,2176]{2,1,0:T(8,128)(2,1)S(1)} %get-tuple-element.581), channel_id=1, source_target_pairs={{0,1},{1,0},{2,3},{3,2},{4,5},{5,4},{6,7},{7,6},{8,9},{9,8},{10,11... | collective-permute-start | bytes 835592 | tf_op jit(solution)/shard_map/cond/branch_2_fun/ppermute | solution.py:23
  77.8 22.6 %collective-permute-start.41 = (bf16[2,32,2176]{2,1,0:T(8,128)(2,1)S(1)}, bf16[2,32,2176]{2,1,0:T(8,128)(2,1)}, u32[]{:S(2)}, u32[]{:S(2)}) collective-permute-start(bf16[2,32,2176]{2,1,0:T(8,128)(2,1)S(1)} %get-tuple-element.582), channel_id=1, source_target_pairs={{0,2},{1,3},{2,0},{3,1},{4,6},{5,7},{6,4},{7,5},{8,10},{9,11},{10,... | collective-permute-start | bytes 835592 | tf_op jit(solution)/shard_map/cond/branch_2_fun/ppermute | solution.py:23
  78.1 22.2 %collective-permute-start.42 = (bf16[2,32,2176]{2,1,0:T(8,128)(2,1)S(1)}, bf16[2,32,2176]{2,1,0:T(8,128)(2,1)}, u32[]{:S(2)}, u32[]{:S(2)}) collective-permute-start(bf16[2,32,2176]{2,1,0:T(8,128)(2,1)S(1)} %get-tuple-element.583), channel_id=1, source_target_pairs={{0,3},{1,2},{2,1},{3,0},{4,7},{5,6},{6,5},{7,4},{8,11},{9,10},{10,... | collective-permute-start | bytes 835592 | tf_op jit(solution)/shard_map/cond/branch_2_fun/ppermute | solution.py:23
  108.0 26.1 %collective-permute-start.72 = (bf16[2,512,512]{2,1,0:T(8,128)(2,1)S(1)}, bf16[2,512,512]{2,1,0:T(8,128)(2,1)}, u32[]{:S(2)}, u32[]{:S(2)}) collective-permute-start(bf16[2,512,512]{2,1,0:T(8,128)(2,1)S(1)} %get-tuple-element.680), channel_id=1, source_target_pairs={{0,8},{4,12},{8,0},{12,4},{16,24},{20,28},{24,16},{28,20},{1,9},{5... | collective-permute-start | bytes 3145736 | tf_op jit(solution)/shard_map/cond/branch_1_fun/ppermute | solution.py:23
  120.4 25.0 %collective-permute-start.73 = (bf16[2,512,256]{2,1,0:T(8,128)(2,1)}, bf16[2,512,256]{2,1,0:T(8,128)(2,1)}, u32[]{:S(2)}, u32[]{:S(2)}) collective-permute-start(bf16[2,512,256]{2,1,0:T(8,128)(2,1)} %get-tuple-element.695), channel_id=1, source_target_pairs={{0,8},{4,12},{8,0},{12,4},{16,24},{20,28},{24,16},{28,20},{1,9},{5... | collective-permute-start | bytes 1572872 | tf_op jit(solution)/shard_map/cond/branch_1_fun/ppermute | solution.py:23
  120.9 34.9 %collective-permute-start.74 = (bf16[2,512,256]{2,1,0:T(8,128)(2,1)}, bf16[2,512,256]{2,1,0:T(8,128)(2,1)}, u32[]{:S(2)}, u32[]{:S(2)}) collective-permute-start(bf16[2,512,256]{2,1,0:T(8,128)(2,1)} %get-tuple-element.696), channel_id=1, source_target_pairs={{0,8},{4,12},{8,0},{12,4},{16,24},{20,28},{24,16},{28,20},{1,9},{5... | collective-permute-start | bytes 1572872 | tf_op jit(solution)/shard_map/cond/branch_1_fun/ppermute | solution.py:23
  122.5 16.3 %collective-permute-start.75 = (bf16[1,32,2176]{2,1,0:T(8,128)(2,1)S(1)}, bf16[1,32,2176]{2,1,0:T(8,128)(2,1)}, u32[]{:S(2)}, u32[]{:S(2)}) collective-permute-start(bf16[1,32,2176]{2,1,0:T(8,128)(2,1)S(1)} %get-tuple-element.697), channel_id=1, source_target_pairs={{0,1},{1,0},{2,3},{3,2},{4,5},{5,4},{6,7},{7,6},{8,9},{9,8},{10,11... | collective-permute-start | bytes 417800 | tf_op jit(solution)/shard_map/cond/branch_1_fun/ppermute | solution.py:23
  122.5 20.2 %collective-permute-start.76 = (bf16[1,32,2176]{2,1,0:T(8,128)(2,1)S(1)}, bf16[1,32,2176]{2,1,0:T(8,128)(2,1)}, u32[]{:S(2)}, u32[]{:S(2)}) collective-permute-start(bf16[1,32,2176]{2,1,0:T(8,128)(2,1)S(1)} %get-tuple-element.698), channel_id=1, source_target_pairs={{0,2},{1,3},{2,0},{3,1},{4,6},{5,7},{6,4},{7,5},{8,10},{9,11},{10,... | collective-permute-start | bytes 417800 | tf_op jit(solution)/shard_map/cond/branch_1_fun/ppermute | solution.py:23
  134.1 8.6 %collective-permute-start.77 = (bf16[1,32,2176]{2,1,0:T(8,128)(2,1)S(1)}, bf16[1,32,2176]{2,1,0:T(8,128)(2,1)}, u32[]{:S(2)}, u32[]{:S(2)}) collective-permute-start(bf16[1,32,2176]{2,1,0:T(8,128)(2,1)S(1)} %get-tuple-element.699), channel_id=1, source_target_pairs={{0,3},{1,2},{2,1},{3,0},{4,7},{5,6},{6,5},{7,4},{8,11},{9,10},{10,... | collective-permute-start | bytes 417800 | tf_op jit(solution)/shard_map/cond/branch_1_fun/ppermute | solution.py:23
  138.8 17.0 %collective-permute-start.80 = (bf16[1,32,2176]{2,1,0:T(8,128)(2,1)S(1)}, bf16[1,32,2176]{2,1,0:T(8,128)(2,1)}, u32[]{:S(2)}, u32[]{:S(2)}) collective-permute-start(bf16[1,32,2176]{2,1,0:T(8,128)(2,1)S(1)} %get-tuple-element.701), channel_id=1, source_target_pairs={{0,3},{1,2},{2,1},{3,0},{4,7},{5,6},{6,5},{7,4},{8,11},{9,10},{10,... | collective-permute-start | bytes 417800 | tf_op jit(solution)/shard_map/cond/branch_1_fun/ppermute | solution.py:23
  148.4 7.4 %collective-permute-start.78 = (bf16[1,32,2176]{2,1,0:T(8,128)(2,1)S(1)}, bf16[1,32,2176]{2,1,0:T(8,128)(2,1)}, u32[]{:S(2)}, u32[]{:S(2)}) collective-permute-start(bf16[1,32,2176]{2,1,0:T(8,128)(2,1)S(1)} %attend_3_1_1.8), channel_id=1, source_target_pairs={{0,1},{1,0},{2,3},{3,2},{4,5},{5,4},{6,7},{7,6},{8,9},{9,8},{10,11... | collective-permute-start | bytes 417800 | tf_op jit(solution)/shard_map/cond/branch_1_fun/ppermute | solution.py:23
  148.5 8.4 %collective-permute-start.79 = (bf16[1,32,2176]{2,1,0:T(8,128)(2,1)S(1)}, bf16[1,32,2176]{2,1,0:T(8,128)(2,1)}, u32[]{:S(2)}, u32[]{:S(2)}) collective-permute-start(bf16[1,32,2176]{2,1,0:T(8,128)(2,1)S(1)} %get-tuple-element.700.refs_4_), channel_id=1, source_target_pairs={{0,2},{1,3},{2,0},{3,1},{4,6},{5,7},{6,4},{7,5},{8,10},{9,11},{10,... | collective-permute-start | bytes 417800 | tf_op jit(solution)/shard_map/cond/branch_1_fun/ppermute | solution.py:23

commit v4 on v3

--- a/solution.py
+++ b/solution.py
@@ -10,6 +10,8 @@
 
 HD = 128
 LANES = 128
+PARTS = 5
+STATS = 16
 MASKED = -1e30
 FLOOR = -1e29
 BF16 = jnp.bfloat16
@@ -206,80 +208,76 @@
 
 
 def place_new(new, slot, buf, spans):
-    segment, rows = buf.shape[0] - LANES, new.shape[1]
-    buf[segment:, :] = jnp.zeros((LANES, buf.shape[1]), BF16)
+    rows = new.shape[1]
     for cols, origin in spans:
-        buf[segment : segment + rows, cols] = new[slot, :, origin]
-
-
-def new_bias_of(size, place):
+        buf[buf.shape[0] - rows :, cols] = new[slot, :, origin]
+
+
+def place_new_bias(size, place, bias):
     fresh = size.tokens // size.width
-    queries = size.shared * size.tokens
-    token = lax.broadcasted_iota(jnp.int32, (queries, LANES), 0) % size.tokens
-    column = lax.broadcasted_iota(jnp.int32, (queries, LANES), 1)
-    allowed = jnp.logical_and(column < fresh, column + place * fresh <= token)
-    return jnp.where(allowed, 0.0, MASKED).astype(F32)
-
-
-def bias_of(at, size, plan, position, place):
-    lane = lax.broadcasted_iota(jnp.int32, (1, LANES), 1)
+    shape = bias[size.segment :].shape
+    row = lax.broadcasted_iota(jnp.int32, shape, 0)
+    token = lax.broadcasted_iota(jnp.int32, shape, 1) % size.tokens
+    allowed = jnp.logical_and(row < fresh, row + place * fresh <= token)
+    bias[size.segment :] = jnp.where(allowed, 0.0, MASKED).astype(F32)
+
+
+def place_bias(at, size, plan, position, place, bias):
+    rows = size.segment // at.nblocks
     length = plan[at.count + position]
-    rows = size.segment // at.nblocks
-    biases = []
-    for b in range(at.nblocks):
-        home = plan[at.home + position * at.nblocks + b]
-        limit = length - place * size.segment - home * rows
-        for part in range(rows // LANES):
-            biases.append(jnp.where(lane + part * LANES < limit, 0.0, MASKED).astype(F32))
-    return jnp.concatenate(biases, axis=1)
-
-
-def attend_owner(size, asked, keys, values, column, bias, new_bias, out, unroll=False):
-    tokens, shared, segment = size.tokens, size.shared, size.segment
+    row = lax.broadcasted_iota(jnp.int32, (rows, bias.shape[1]), 0)
+
+    def block(b, carry):
+        limit = length - place * size.segment - plan[at.home + position * at.nblocks + b] * rows
+        into = pl.ds(pl.multiple_of(b * rows, rows), rows)
+        bias[into] = jnp.where(row < limit, 0.0, MASKED).astype(F32)
+        return carry
+
+    lax.fori_loop(0, at.nblocks, block, 0)
+
+
+def attend_owner(size, asked, keys, values, column, bias, out, unroll=False):
+    tokens, shared = size.tokens, size.shared
     scale = math.log2(math.e) / HD**0.5
-    stat_lane = lax.broadcasted_iota(jnp.int32, (tokens, LANES), 1)
+    stat_row = lax.broadcasted_iota(jnp.int32, (STATS, shared * tokens), 0)
 
     def head(j, stats):
-        tops, totals = stats
         cols = pl.ds(pl.multiple_of(column + j * HD, HD), HD)
         spans = [
             pl.ds(pl.multiple_of((j * shared + s) * HD, HD), HD) for s in range(shared)
         ]
         scores = lax.dot_general(
+            keys[:, cols],
             jnp.concatenate([asked[:, span] for span in spans], axis=0),
-            keys[:, cols],
             (((1,), (1,)), ((), ())),
             preferred_element_type=F32,
         )
-        older = scores[:, :segment] * scale + bias
-        newer = scores[:, segment:] * scale + new_bias
-        top = jnp.maximum(
-            jnp.max(older, axis=1, keepdims=True), jnp.max(newer, axis=1, keepdims=True)
+        scores = scores * scale + bias[...]
+        top = jnp.maximum(jnp.max(scores, axis=0, keepdims=True), FLOOR)
+        weights = jnp.exp2(scores - top)
+        total = jnp.sum(weights, axis=0, keepdims=True)
+        summed = lax.dot_general(
+            values[:, cols],
+            weights.astype(BF16),
+            (((0,), (0,)), ((), ())),
+            preferred_element_type=F32,
         )
-        top = jnp.maximum(top, FLOOR)
-        older = jnp.exp2(older - top)
-        newer = jnp.exp2(newer - top)
-        total = jnp.sum(older, axis=1, keepdims=True) + jnp.sum(newer, axis=1, keepdims=True)
-        weights = jnp.concatenate([older.astype(BF16), newer.astype(BF16)], axis=1)
-        summed = jnp.dot(weights, values[:, cols], preferred_element_type=F32).astype(BF16)
-        for s, span in enumerate(spans):
-            part = slice(s * tokens, (s + 1) * tokens)
-            out[:, span] = summed[part]
-            chosen = stat_lane == j * shared + s
-            tops = jnp.where(chosen, top[part], tops)
-            totals = jnp.where(chosen, total[part], totals)
-        return tops, totals
-
-    stats = (jnp.zeros((tokens, LANES), F32), jnp.zeros((tokens, LANES), F32))
+        out[pl.ds(pl.multiple_of(j * HD, HD), HD)] = summed.astype(BF16)
+        for n, part in enumerate(split(top, 3) + split(total, 2)):
+            stats = jnp.where(stat_row == j * PARTS + n, part, stats)
+        return stats
+
+    stats = jnp.zeros(stat_row.shape, F32)
     stats = lax.fori_loop(0, size.kv_own, head, stats, unroll=unroll)
-    out[:, size.own * HD :] = pack_stats(*stats, size.own).astype(BF16)
-
-
-def attend_kernel(at, size, first, newest, pieces, partial, plan, *refs):
+    out[size.wide :] = stats.astype(BF16)
+
+
+def attend_kernel(at, size, first, newest, pieces, partial, cuts, plan, *refs):
     count, some = len(newest), len(pieces)
     q_refs, (new_k, new_v), refs = refs[:some], refs[some : some + 2], refs[some + 2 :]
-    outs, (kbuf, vbuf, qbuf, obuf, sems) = refs[-5 - some : -5], refs[-5:]
-    sources = refs[: -5 - some]
+    total = some * len(cuts)
+    outs, (kbuf, vbuf, qbuf, obuf, bias, sems) = refs[-6 - total : -6], refs[-6:]
+    sources = refs[: -6 - total]
     place = plan[at.place]
     half = size.width // 2
 
@@ -314,10 +312,10 @@
         place_new(new_k, slot, kbuf.at[n], spans)
         place_new(new_v, slot, vbuf.at[n], spans)
 
-    new_bias = new_bias_of(size, place)
+    place_new_bias(size, place, bias)
 
     def request(n, carry):
-        bias = bias_of(at, size, plan, first + n, place)
+        place_bias(at, size, plan, first + n, place, bias)
         for m, buf in enumerate((kbuf, vbuf)):
             view = buf.at[n, pl.ds(0, size.segment)]
             pltpu.make_async_copy(view, view, sems.at[m, n]).wait()
@@ -332,7 +330,6 @@
                 vbuf.at[n],
                 column,
                 bias,
-                new_bias,
                 obuf.at[p, n],
             )
             return carry
@@ -340,7 +337,11 @@
         return lax.fori_loop(0, some, owner, carry)
 
     lax.fori_loop(0, count, request, 0)
-    copies = [pltpu.make_async_copy(obuf.at[p], outs[p], sems.at[3, p]) for p in range(some)]
+    copies = []
+    for n, out in enumerate(outs):
+        p, cut = divmod(n, len(cuts))
+        view = obuf.at[p, :, pl.ds(sum(cuts[:cut]), cuts[cut])]
+        copies.append(pltpu.make_async_copy(view, out, sems.at[3, n]))
     for copy in copies:
         copy.start()
     for copy in copies:
@@ -360,29 +361,23 @@
     return result
 
 
-def pack_stats(tops, totals, own):
-    packed = jnp.zeros_like(tops)
-    for n, part in enumerate(split(tops, 3) + split(totals, 2)):
-        packed = packed + (pltpu.roll(part, n * own, 1) if n else part)
-    return packed
-
-
-def unpack_stats(packed, own):
-    parts = [pltpu.roll(packed, LANES - n * own, 1) if n else packed for n in range(5)]
-    return (parts[0] + parts[1]) + parts[2], parts[3] + parts[4]
-
-
-def combined(pieces, heads, out):
-    stats = [unpack_stats(piece[:, heads * HD :].astype(F32), heads) for piece in pieces]
-    peak = functools.reduce(jnp.maximum, [top for top, _ in stats])
-    factors = [jnp.exp2(top - peak) for top, _ in stats]
-    denom = sum(total * factor for (_, total), factor in zip(stats, factors))
-    shares = [factor / denom for factor in factors]
-    for h in range(heads):
-        cols = slice(h * HD, (h + 1) * HD)
-        out[:, cols] = sum(
-            piece[:, cols].astype(F32) * share[:, h : h + 1] for piece, share in zip(pieces, shares)
-        ).astype(BF16)
+def combined(size, pieces, out):
+    tokens = size.tokens
+    stats = [piece[size.wide :].astype(F32) for piece in pieces]
+    for j in range(size.kv_own):
+        rows = [[stat[n : n + 1] for n in range(j * PARTS, (j + 1) * PARTS)] for stat in stats]
+        tops = [row[0] + row[1] + row[2] for row in rows]
+        peak = functools.reduce(jnp.maximum, tops)
+        factors = [jnp.exp2(top - peak) for top in tops]
+        denom = sum((row[3] + row[4]) * factor for row, factor in zip(rows, factors))
+        mixed = sum(
+            piece[j * HD : (j + 1) * HD].astype(F32) * (factor / denom)
+            for piece, factor in zip(pieces, factors)
+        )
+        mixed = mixed.T.astype(BF16)
+        for s in range(size.shared):
+            cols = slice((j * size.shared + s) * HD, (j * size.shared + s + 1) * HD)
+            out[:, cols] = mixed[s * tokens : (s + 1) * tokens]
 
 
 def finish_kernel(at, size, parcels, lots, settled, ready, plan, *refs):
@@ -391,9 +386,9 @@
     arrived, refs = refs[:some], refs[some:]
     sources, refs = refs[: 2 * len(parcels_before(ready))], refs[2 * len(parcels_before(ready)) :]
     query, new_k, new_v = refs[:3]
-    pieces, refs = refs[3:-14], refs[-12:]
+    pieces, refs = refs[3:-15], refs[-13:]
     attended, after = refs[0], refs[1:3]
-    kbuf, vbuf, qbuf, pbuf, mixed, full, sems, out_sems, in_sems = refs[3:]
+    kbuf, vbuf, qbuf, pbuf, bias, mixed, full, sems, out_sems, in_sems = refs[3:]
     place, slot = plan[at.place], plan[at.slot + count]
     copies = [
         pltpu.make_async_copy(arrived[-1].at[m], buf.at[pl.ds(0, size.segment)], in_sems.at[m])
@@ -402,13 +397,16 @@
     copies.append(pltpu.make_async_copy(query.at[0, slot], qbuf, in_sems.at[2]))
     for copy in copies:
         copy.start()
+    pieces = iter(pieces)
     before = 0
     for lot, each in enumerate([*lots, 1]):
         for i in range(size.width):
-            if lot < len(lots) or i:
-                piece = pieces[lot * size.width + i - lot // len(lots)]
-                into = pbuf.at[i, pl.ds(before, each)]
+            row = 0
+            while row < pbuf.shape[2] and (lot < len(lots) or i):
+                piece = next(pieces)
+                into = pbuf.at[i, pl.ds(before, each), pl.ds(row, piece.shape[1])]
                 pltpu.make_async_copy(piece, into, in_sems.at[3]).start()
+                row += piece.shape[1]
         before += each
     for position in range(settled, count):
         bufs = [full.at[n, position - settled] for n in range(2)]
@@ -429,15 +427,15 @@
     spans = [own_columns(size, place, 0, 0)]
     place_new(new_k, slot, kbuf, spans)
     place_new(new_v, slot, vbuf, spans)
-    bias = bias_of(at, size, plan, count, place)
-    new_bias = new_bias_of(size, place)
+    place_bias(at, size, plan, count, place, bias)
+    place_new_bias(size, place, bias)
     theirs = (pbuf.at[0, pl.ds(0, count)], pbuf.at[pl.ds(1, size.width - 1)])
     for view in theirs:
         pltpu.make_async_copy(view, view, in_sems.at[3]).wait()
 
     def request(n, carry):
         parts = [pbuf.at[i, n] for i in range(size.width)]
-        combined(parts, size.own, mixed.at[n])
+        combined(size, parts, mixed.at[n])
         there = attended.at[0, plan[at.slot + n]]
         pltpu.make_async_copy(mixed.at[n], there, in_sems.at[4]).start()
         return carry
@@ -453,7 +451,7 @@
             ).start()
     for copy in copies:
         copy.wait()
-    attend_owner(size, qbuf, kbuf, vbuf, 0, bias, new_bias, pbuf.at[0, count], True)
+    attend_owner(size, qbuf, kbuf, vbuf, 0, bias, pbuf.at[0, count], True)
     lax.fori_loop(count, count + 1, request, 0)
     for position in range(settled, count + 1):
         there = plan[at.slot + position]
@@ -483,10 +481,14 @@
     ready = [max(-1, n - (requests - matchings)) for n in range(requests)]
     caches = (cache_keys, cache_values)
     big = pltpu.CompilerParams(vmem_limit_bytes=40 * 1024 * 1024)
-    result = jax.ShapeDtypeStruct((tokens, own * HD + LANES), BF16)
+    queries = size.shared * tokens
+    result = jax.ShapeDtypeStruct((size.wide + STATS, queries), BF16)
+    behind = -(-new_keys.shape[2] // 16) * 16
+    scores = pltpu.VMEM((segment + behind, queries), F32)
     everyone = tuple(range(width))
     halves = [part for part in (everyone[width // 2 :], everyone[: width // 2]) if part]
-    parcels = [part for part in (halves[0], everyone[1 : width // 2], (0,)) if part]
+    near = everyone[1 : width // 2]
+    parcels = [part for part in (halves[0], near, (0,)) if part]
 
     def held(pieces):
         return jax.ShapeDtypeStruct((2, segment, len(pieces) * size.wide), BF16)
@@ -521,23 +523,27 @@
             name=f"pick_{step}",
         )(plan, *sources, *after)
 
-    def attend(first, count, pieces, asked, fresh, sources, partial=False, after=()):
+    def attend(first, count, pieces, asked, fresh, sources, partial=False, after=(), cuts=None):
         newest = ready[first : first + count]
         if not partial:
             sources = sources[: 2 * (max(newest) + 2)]
         some = len(pieces)
         held = some * size.wide if partial else features
+        cuts = cuts or [result.shape[0]]
         return pl.pallas_call(
-            functools.partial(attend_kernel, at, size, first, newest, pieces, partial),
-            out_shape=[jax.ShapeDtypeStruct((count, *result.shape), BF16)] * some,
+            functools.partial(attend_kernel, at, size, first, newest, pieces, partial, cuts),
+            out_shape=[
+                jax.ShapeDtypeStruct((count, rows, queries), BF16) for _ in pieces for rows in cuts
+            ],
             in_specs=[SMEM] + [ANY] * some + [VMEM] * 2 + [ANY] * (len(sources) + len(after)),
-            out_specs=[ANY] * some,
+            out_specs=[ANY] * (some * len(cuts)),
             scratch_shapes=[
-                pltpu.VMEM((count, segment + LANES, held), BF16),
-                pltpu.VMEM((count, segment + LANES, held), BF16),
+                pltpu.VMEM((count, segment + behind, held), BF16),
+                pltpu.VMEM((count, segment + behind, held), BF16),
                 pltpu.VMEM((count, some, tokens, own * HD), BF16),
                 pltpu.VMEM((some, count, *result.shape), BF16),
-                pltpu.SemaphoreType.DMA((4, max(some, count))),
+                scores,
+                pltpu.SemaphoreType.DMA((4, max(some * len(cuts), count))),
             ],
             compiler_params=big,
             cost_estimate=lasting(1 + 1.5 * some * count),
@@ -566,7 +572,7 @@
         )(plan, *used)
 
     def pad_new():
-        extra = -new_keys.shape[2] % 16
+        extra = behind - new_keys.shape[2]
         return [jnp.pad(new[0], ((0, 0), (0, extra), (0, 0))) for new in (new_keys, new_values)]
 
     def prepare(step, sources, arrived):
@@ -593,10 +599,15 @@
         done = send_home(everyone, whole)
         parts, after = {}, done[:1]
         for parcel, block in zip(parcels[:-1], arrived):
-            part = attend(requests - 1, 1, parcel, asked, fresh, [block], True, after)
-            parts.update(zip(parcel, send_home(parcel, part)))
+            cuts = [size.wide // 2, result.shape[0] - size.wide // 2] if parcel == near else None
+            part = attend(requests - 1, 1, parcel, asked, fresh, [block], True, after, cuts)
+            each = len(part) // len(parcel)
+            for n, piece in enumerate(parcel):
+                parts[piece] = [
+                    exchange(array, "ctx", piece) for array in part[n * each : (n + 1) * each]
+                ]
             after = [*part[:1], *done[1:]]
-        return arrived, done, [parts[piece] for piece in everyone[1:]]
+        return arrived, done, [array for piece in everyone[1:] for array in parts[piece]]
 
     def switch(step, branch, *given):
         return lax.switch(
@@ -637,10 +648,11 @@
         + [ANY] * (len(pieces) + 2),
         out_specs=[ANY] * 3,
         scratch_shapes=[
-            pltpu.VMEM((segment + LANES, size.wide), BF16),
-            pltpu.VMEM((segment + LANES, size.wide), BF16),
+            pltpu.VMEM((segment + behind, size.wide), BF16),
+            pltpu.VMEM((segment + behind, size.wide), BF16),
             pltpu.VMEM((tokens, own * HD), BF16),
             pltpu.VMEM((width, requests, *result.shape), BF16),
+            scores,
             pltpu.VMEM((requests, tokens, own * HD), BF16),
             pltpu.VMEM((2, left, segment, features), BF16),
             pltpu.SemaphoreType.DMA((2, left)),

time: 164 us -> 160 us (0.976); the launches traced: 163 us -> 157 us
  waiting for transfers between devices: 86.4 us -> 78 us
    ppermute x19 -> x20, waiting for transfers between devices: 86.4 us -> 78 us  [exchange(): lax.ppermute(block, axis, [(i, i ^ mask) for i in range(lax.axis_size(axi...]
    ppermute x19 -> x20, starting transfers between devices: 23.5 us -> 24.9 us  [exchange(): lax.ppermute(block, axis, [(i, i ^ mask) for i in range(lax.axis_size(axi...]
  transfers between devices with their start and end apart: 19 -> 20, of which waited for: 11 -> 10; matrix products, arithmetic and copies ran while one was open for 0% -> 0% of each run, Pallas kernels for 27% -> 29%
where the time goes in v4:
time: 160 us; the launch traced here: 157 us
  waiting for transfers between devices  78 us (49%)
  Pallas kernels  50.8 us (32%)
  starting transfers between devices  24.9 us (16%)
  between operations  2.83 us (2%)
    ppermute x20, waiting for transfers between devices, exchange(): lax.ppermute(block, axis, [(i, i ^ mask) for i in range(lax.axis_size(axi...  78 us
    pallas_call x4, Pallas kernels, attend(): pl.pallas_call(functools.partial(attend_kernel, at, size, first, newest,...  27.9 us
    ppermute x20, starting transfers between devices, exchange(): lax.ppermute(block, axis, [(i, i ^ mask) for i in range(lax.axis_size(axi...  24.9 us
    pallas_call x4, Pallas kernels, pick(): pl.pallas_call(functools.partial(pick_kernel, at, step, choices), out_sha...  8.99 us
    pallas_call x1, Pallas kernels, shards(): pl.pallas_call(functools.partial(finish_kernel, at, size, parcels, lots,...  5.94 us
    pallas_call x1, Pallas kernels, settle(): pl.pallas_call(functools.partial(settle_kernel, at, newest), out_shape=[j...  4.42 us
    pallas_call x1, Pallas kernels, shards(): pl.pallas_call(functools.partial(plan_kernel, at, halves), out_shape=(jax...  3.52 us
  transfers between devices with their start and end apart: 20, of which 10 were waited for; matrix products, arithmetic and copies ran while one was open for 0% of the time, Pallas kernels for 29%

profile of v4, /device:TPU:0, one launch (start us, length us, event | category | flops | bytes accessed | tf_op | source)
XLA Modules:
  0.0 156.8 jit_solution(10991224006142970142)
XLA Ops:
  0.6 5.1 %collective-permute-start.133 = (bf16[1,4,32,2048]{3,2,1,0:T(8,128)(2,1)}, bf16[1,4,32,2048]{3,2,1,0:T(8,128)(2,1)S(1)}, u32[]{:S(2)}, u32[]{:S(2)}) collective-permute-start(bf16[1,4,32,2048]{3,2,1,0:T(8,128)(2,1)} %refs_9_.1), channel_id=1, source_target_pairs={{0,3},{1,2},{2,1},{3,0},{4,7},{5,6},{6,5},{7,4},{8,11},{9,10},{10,... | collective-permute-start | bytes 1572872 | tf_op jit(solution)/shard_map/ppermute | solution.py:25
  5.8 3.5 %plan.1 = (s32[51]{0:T(128)S(1)}, s32[1]{0:T(128)}, s32[1]{0:T(128)}, s32[1]{0:T(128)}, bf16[2,512,512]{2,1,0:T(8,128)(2,1)S(1)}, /*index=5*/bf16[2,512,512]{2,1,0:T(8,128)(2,1)}) custom-call(s32[3]{0:T(128)} %masks.1, s32[3,8]{1,0:T(4,128)} %movers.1, s32[3,4,8]{2,1,0:T(4,128)} %bitcast.33, s32[4,8]{1,0:T(4,128)} %bitcast.34, ...), custom_call_target="tpu_custom_call" | custom-call | tf_op jit(solution)/shard_map/plan/pallas_call | solution.py:496
  11.3 47.3 %conditional.3 = (bf16[2,512,512]{2,1,0:T(8,128)(2,1)}, bf16[2,512,512]{2,1,0:T(8,128)(2,1)}, bf16[2,512,512]{2,1,0:T(8,128)(2,1)S(1)}, bf16[1,4,32,2048]{3,2,1,...) conditional(s32[]{:T(128)} %bitcast.18, ...), branch_computations={%region_0.1_spmd, %region_1.2_spmd, %region_2.3_spmd, %region_3.4_... | conditional | bytes 22226348 | solution.py:613
  11.3 1.6 %collective-permute-start.12 = (bf16[2,512,512]{2,1,0:T(8,128)(2,1)S(1)}, bf16[2,512,512]{2,1,0:T(8,128)(2,1)}, u32[]{:S(2)}, u32[]{:S(2)}) collective-permute-start(bf16[2,512,512]{2,1,0:T(8,128)(2,1)S(1)} %get-tuple-element.500), channel_id=1, source_target_pairs={{0,16},{4,20},{8,24},{12,28},{16,0},{20,4},{24,8},{28,12},{1,17},{... | collective-permute-start | bytes 3145736 | tf_op jit(solution)/shard_map/cond/branch_3_fun/ppermute | solution.py:25
  14.1 23.5 %collective-permute-done.12.refs_2_.refs_3_ = bf16[2,512,512]{2,1,0:T(8,128)(2,1)} collective-permute-done((bf16[2,512,512]{2,1,0:T(8,128)(2,1)S(1)}, bf16[2,512,512]{2,1,0:T(8,128)(2,1)}, u32[]{:S(2)}, u32[]{:S(2)}) %collective-permute-start.12) | collective-permute-done | bytes 1048608 | tf_op jit(solution)/shard_map/cond/branch_3_fun/ppermute | solution.py:25
  37.6 1.8 %pick_1.17 = bf16[2,512,512]{2,1,0:T(8,128)(2,1)S(1)} custom-call(s32[51]{0:T(128)S(1)} %get-tuple-element.502.plan, bf16[1,4,512,1024]{3,2,1,0:T(8,128)(2,1)} %get-tuple-element.503.refs_0_, bf16[1,4,512,1024]{3,2,1,0:T(8,128)(2,1)} %get-tuple-element.504.refs_1_, bf16[2,512,512]{2,1,0:T(8,128)(2,1)} %collective-permute-done.12.refs_2_.refs_3_, ...), custom_call_target="tpu_custom_call" | custom-call | bytes 9250000 | tf_op jit(solution)/shard_map/cond/branch_3_fun/pick_1/pallas_call | solution.py:516
  39.4 11.5 %collective-permute-done.15 = bf16[1,4,32,2048]{3,2,1,0:T(8,128)(2,1)} collective-permute-done((bf16[1,4,32,2048]{3,2,1,0:T(8,128)(2,1)S(1)}, bf16[1,4,32,2048]{3,2,1,0:T(8,128)(2,1)}, u32[]{:S(2)}, u32[]{:S(2)}) %collective-permute-start.15) | collective-permute-done | bytes 524320 | tf_op jit(solution)/shard_map/cond/branch_3_fun/ppermute | solution.py:25
  50.8 7.7 %collective-permute-done.13 = bf16[2,512,512]{2,1,0:T(8,128)(2,1)} collective-permute-done((bf16[2,512,512]{2,1,0:T(8,128)(2,1)}, bf16[2,512,512]{2,1,0:T(8,128)(2,1)}, u32[]{:S(2)}, u32[]{:S(2)}) %collective-permute-start.13) | collective-permute-done | bytes 1048608 | tf_op jit(solution)/shard_map/cond/branch_3_fun/ppermute | solution.py:25
  58.6 46.3 %conditional.4 = (bf16[2,512,512]{2,1,0:T(8,128)(2,1)}, bf16[2,512,512]{2,1,0:T(8,128)(2,1)}, bf16[2,512,512]{2,1,0:T(8,128)(2,1)S(1)}, bf16[2,272,256]{2,1,0:T(...) conditional(s32[]{:T(128)} %bitcast.17, ...), branch_computations={%region_7.8_spmd, %region_8.9_spmd, %region_9.10_spmd, %region_10.... | conditional | bytes 126685712 | solution.py:613
  58.6 1.5 collective-permute-start.33
  60.1 2.7 %pick_1.22 = bf16[2,512,512]{2,1,0:T(8,128)(2,1)} custom-call(s32[51]{0:T(128)S(1)} %get-tuple-element.551.plan, bf16[1,4,512,1024]{3,2,1,0:T(8,128)(2,1)} %get-tuple-element.552.refs_0_.refs_6_, bf16[1,4,512,1024]{3,2,1,0:T(8,128)(2,1)} %get-tuple-element.553.refs_1_.refs_7_, bf16[2,512,512]{2,1,0:T(8,128)(2,1)} %get-tuple-element.554.refs_2_.refs_8_, ...), custom_call_target="tpu_custom_call" | custom-call | bytes 9250000 | tf_op jit(solution)/shard_map/cond/branch_1_fun/pick_1/pallas_call | solution.py:516
  63.4 12.4 %attend_0_2_4.8 = (bf16[2,272,256]{2,1,0:T(8,128)(2,1)S(1)}, bf16[2,272,256]{2,1,0:T(8,128)(2,1)S(1)}, bf16[2,272,256]{2,1,0:T(8,128)(2,1)S(1)}, bf16[2,272,256]{2,1,0:T(8,128)(2,1)S(1)}) custom-call(s32[51]{0:T(128)S(1)} %get-tuple-element.551.plan, bf16[1,4,32,2048]{3,2,1,0:T(8,128)(2,1)S(1)} %get-tuple-element.556.refs_0_, ...), custom_call_target="tpu_custom_call" | custom-call | bytes 48100000 | tf_op jit(solution)/shard_map/cond/branch_1_fun/attend_0_2_4/pallas_call | solution.py:533
  76.8 3.5 %collective-permute-start.37 = (bf16[2,272,256]{2,1,0:T(8,128)(2,1)S(1)}, bf16[2,272,256]{2,1,0:T(8,128)(2,1)}, u32[]{:S(2)}, u32[]{:S(2)}) collective-permute-start(bf16[2,272,256]{2,1,0:T(8,128)(2,1)S(1)} %get-tuple-element.565), channel_id=1, source_target_pairs={{0,3},{1,2},{2,1},{3,0},{4,7},{5,6},{6,5},{7,4},{8,11},{9,10},{10,... | collective-permute-start | bytes 835592 | tf_op jit(solution)/shard_map/cond/branch_1_fun/ppermute | solution.py:25
  80.3 4.4 %settle.8 = (bf16[1,4,512,1024]{3,2,1,0:T(8,128)(2,1)}, bf16[1,4,512,1024]{3,2,1,0:T(8,128)(2,1)}) custom-call(s32[51]{0:T(128)S(1)} %get-tuple-element.551.plan, bf16[1,4,512,1024]{3,2,1,0:T(8,128)(2,1)S(1)} %copy-done.1, bf16[1,4,512,1024]{3,2,1,0:T(8,128)(2,1)S(1)} %copy-done.8, bf16[2,512,512]{2,1,0:T(8,128)(2,1)} %get-tuple-element.554.refs_2_.refs_8_, ...), custom_call_target="tpu_custom_call" | custom-call | bytes 14800000 | tf_op jit(solution)/shard_map/cond/branch_1_fun/settle/pallas_call | solution.py:560
  84.8 1.8 %pick_2.15 = bf16[2,512,512]{2,1,0:T(8,128)(2,1)S(1)} custom-call(s32[51]{0:T(128)S(1)} %get-tuple-element.551.plan, bf16[1,4,512,1024]{3,2,1,0:T(8,128)(2,1)} %get-tuple-element.552.refs_0_.refs_6_, bf16[1,4,512,1024]{3,2,1,0:T(8,128)(2,1)} %get-tuple-element.553.refs_1_.refs_7_, bf16[2,512,512]{2,1,0:T(8,128)(2,1)} %get-tuple-element.554.refs_2_.refs_8_, ...), custom_call_target="tpu_custom_call" | custom-call | bytes 9250000 | tf_op jit(solution)/shard_map/cond/branch_1_fun/pick_2/pallas_call | solution.py:516
  86.6 1.8 %collective-permute-done.35 = bf16[2,272,256]{2,1,0:T(8,128)(2,1)} collective-permute-done((bf16[2,272,256]{2,1,0:T(8,128)(2,1)S(1)}, bf16[2,272,256]{2,1,0:T(8,128)(2,1)}, u32[]{:S(2)}, u32[]{:S(2)}) %collective-permute-start.35) | collective-permute-done | bytes 278560 | tf_op jit(solution)/shard_map/cond/branch_1_fun/ppermute | solution.py:25
  88.4 9.3 %collective-permute-done.36 = bf16[2,272,256]{2,1,0:T(8,128)(2,1)} collective-permute-done((bf16[2,272,256]{2,1,0:T(8,128)(2,1)S(1)}, bf16[2,272,256]{2,1,0:T(8,128)(2,1)}, u32[]{:S(2)}, u32[]{:S(2)}) %collective-permute-start.36) | collective-permute-done | bytes 278560 | tf_op jit(solution)/shard_map/cond/branch_1_fun/ppermute | solution.py:25
  97.7 7.2 %collective-permute-done.34 = bf16[2,512,512]{2,1,0:T(8,128)(2,1)} collective-permute-done((bf16[2,512,512]{2,1,0:T(8,128)(2,1)}, bf16[2,512,512]{2,1,0:T(8,128)(2,1)}, u32[]{:S(2)}, u32[]{:S(2)}) %collective-permute-start.34) | collective-permute-done | bytes 1048608 | tf_op jit(solution)/shard_map/cond/branch_1_fun/ppermute | solution.py:25
  104.9 45.8 %conditional.5 = (bf16[2,512,512]{2,1,0:T(8,128)(2,1)}, bf16[2,512,256]{2,1,0:T(8,128)(2,1)}, bf16[2,512,256]{2,1,0:T(8,128)(2,1)}, bf16[1,272,256]{2,1,0:T(8,12...) conditional(s32[]{:T(128)} %bitcast.16, ...), branch_computations={%region_14.15_spmd, %region_15.16_spmd, %region_16.17_spmd, %regio... | conditional | bytes 70931432 | solution.py:613
  104.9 1.5 collective-permute-start.93
  106.4 7.8 %attend_2_1_4.10 = (bf16[1,272,256]{2,1,0:T(8,128)(2,1)}, bf16[1,272,256]{2,1,0:T(8,128)(2,1)S(1)}, bf16[1,272,256]{2,1,0:T(8,128)(2,1)S(1)}, bf16[1,272,256]{2,1,0:T(8,128)(2,1)S(1)}) custom-call(s32[51]{0:T(128)S(1)} %get-tuple-element.731.plan, bf16[1,4,32,2048]{3,2,1,0:T(8,128)(2,1)S(1)} %get-tuple-element.738.refs_0_, ...), custom_call_target="tpu_custom_call" | custom-call | bytes 25900000 | tf_op jit(solution)/shard_map/cond/branch_3_fun/attend_2_1_4/pallas_call | solution.py:533
  114.2 2.7 %pick_2.24 = (bf16[2,512,256]{2,1,0:T(8,128)(2,1)}, bf16[2,512,256]{2,1,0:T(8,128)(2,1)}) custom-call(s32[51]{0:T(128)S(1)} %get-tuple-element.731.plan, bf16[1,4,512,1024]{3,2,1,0:T(8,128)(2,1)} %get-tuple-element.732.refs_6_.refs_0_, bf16[1,4,512,1024]{3,2,1,0:T(8,128)(2,1)} %get-tuple-element.733.refs_7_.refs_1_, ...), custom_call_target="tpu_custom_call" | custom-call | bytes 9250000 | tf_op jit(solution)/shard_map/cond/branch_3_fun/pick_2/pallas_call | solution.py:516
  117.5 1.5 collective-permute-start.95
  119.1 1.0 collective-permute-start.97
  120.0 11.0 %collective-permute-done.93.refs_4_ = bf16[2,512,512]{2,1,0:T(8,128)(2,1)} collective-permute-done((bf16[2,512,512]{2,1,0:T(8,128)(2,1)S(1)}, bf16[2,512,512]{2,1,0:T(8,128)(2,1)}, u32[]{:S(2)}, u32[]{:S(2)}) %collective-permute-start.93) | collective-permute-done | bytes 1048608 | tf_op jit(solution)/shard_map/cond/branch_3_fun/ppermute | solution.py:25
  131.7 4.6 %attend_3_1_2.10 = (bf16[1,272,256]{2,1,0:T(8,128)(2,1)S(1)}, bf16[1,272,256]{2,1,0:T(8,128)(2,1)S(1)}) custom-call(s32[51]{0:T(128)S(1)} %get-tuple-element.731.plan, bf16[1,4,32,2048]{3,2,1,0:T(8,128)(2,1)} %get-tuple-element.740.refs_2_.refs_0_, bf16[1,4,32,2048]{3,2,1,0:T(8,128)(2,1)S(1)} %get-tuple-element.741.refs_3_.refs_1_, ...), custom_call_target="tpu_custom_call" | custom-call | bytes 14800000 | tf_op jit(solution)/shard_map/cond/branch_3_fun/attend_3_1_2/pallas_call | solution.py:533
  136.3 3.2 %collective-permute-start.102 = (bf16[1,272,256]{2,1,0:T(8,128)(2,1)S(1)}, bf16[1,272,256]{2,1,0:T(8,128)(2,1)}, u32[]{:S(2)}, u32[]{:S(2)}) collective-permute-start(bf16[1,272,256]{2,1,0:T(8,128)(2,1)S(1)} %get-tuple-element.753), channel_id=1, source_target_pairs={{0,3},{1,2},{2,1},{3,0},{4,7},{5,6},{6,5},{7,4},{8,11},{9,10},{10,... | collective-permute-start | bytes 417800 | tf_op jit(solution)/shard_map/cond/branch_3_fun/ppermute | solution.py:25
  139.6 2.7 %collective-permute-done.94.refs_3_ = bf16[2,512,256]{2,1,0:T(8,128)(2,1)} collective-permute-done((bf16[2,512,256]{2,1,0:T(8,128)(2,1)}, bf16[2,512,256]{2,1,0:T(8,128)(2,1)}, u32[]{:S(2)}, u32[]{:S(2)}) %collective-permute-start.94) | collective-permute-done | bytes 524320 | tf_op jit(solution)/shard_map/cond/branch_3_fun/ppermute | solution.py:25
  142.3 3.1 %attend_3_1_1.10 = (bf16[1,128,256]{2,1,0:T(8,128)(2,1)S(1)}, bf16[1,144,256]{2,1,0:T(8,128)(2,1)S(1)}) custom-call(s32[51]{0:T(128)S(1)} %get-tuple-element.731.plan, bf16[1,4,32,2048]{3,2,1,0:T(8,128)(2,1)} %get-tuple-element.739.refs_1_.refs_0_, bf16[4,16,1024]{2,1,0:T(8,128)(2,1)S(1)} %get-tuple-element.742.refs_4_.refs_2_.refs_1_, ...), custom_call_target="tpu_custom_call" | custom-call | bytes 9250000 | tf_op jit(solution)/shard_map/cond/branch_3_fun/attend_3_1_1/pallas_call | solution.py:533
  145.5 2.0 %collective-permute-start.99 = (bf16[1,128,256]{2,1,0:T(8,128)(2,1)S(1)}, bf16[1,128,256]{2,1,0:T(8,128)(2,1)}, u32[]{:S(2)}, u32[]{:S(2)}) collective-permute-start(bf16[1,128,256]{2,1,0:T(8,128)(2,1)S(1)} %get-tuple-element.751), channel_id=1, source_target_pairs={{0,1},{1,0},{2,3},{3,2},{4,5},{5,4},{6,7},{7,6},{8,9},{9,8},{10,11... | collective-permute-start | bytes 196616 | tf_op jit(solution)/shard_map/cond/branch_3_fun/ppermute | solution.py:25
  147.5 2.8 %collective-permute-done.95 = bf16[2,512,256]{2,1,0:T(8,128)(2,1)} collective-permute-done((bf16[2,512,256]{2,1,0:T(8,128)(2,1)}, bf16[2,512,256]{2,1,0:T(8,128)(2,1)}, u32[]{:S(2)}, u32[]{:S(2)}) %collective-permute-start.95) | collective-permute-done | bytes 524320 | tf_op jit(solution)/shard_map/cond/branch_3_fun/ppermute | solution.py:25
  150.6 5.9 %finish.1 = (bf16[1,4,32,2048]{3,2,1,0:T(8,128)(2,1)}, bf16[1,4,512,1024]{3,2,1,0:T(8,128)(2,1)}, bf16[1,4,512,1024]{3,2,1,0:T(8,128)(2,1)}) custom-call(s32[51]{0:T(128)S(1)} %get-tuple-element.862.plan, bf16[2,512,512]{2,1,0:T(8,128)(2,1)} %get-tuple-element.878.refs_0_, ...), custom_call_target="tpu_custom_call", output_to_operand_aliasing={{1}: (25, {}), {2}: (26, {})} | custom-call | tf_op jit(solution)/shard_map/finish/pallas_call | solution.py:640
  (34 shorter events, 4.4 us)
Async XLA Ops:
  0.6 58.0 %collective-permute-start.133 = (bf16[1,4,32,2048]{3,2,1,0:T(8,128)(2,1)}, bf16[1,4,32,2048]{3,2,1,0:T(8,128)(2,1)S(1)}, u32[]{:S(2)}, u32[]{:S(2)}) collective-permute-start(bf16[1,4,32,2048]{3,2,1,0:T(8,128)(2,1)} %refs_9_.1), channel_id=1, source_target_pairs={{0,3},{1,2},{2,1},{3,0},{4,7},{5,6},{6,5},{7,4},{8,11},{9,10},{10,... | collective-permute-start | bytes 1572872 | tf_op jit(solution)/shard_map/ppermute | solution.py:25
  5.7 5.5 %copy-start.14 = (bf16[1,4,32,2048]{3,2,1,0:T(8,128)(2,1)S(1)}, bf16[1,4,32,2048]{3,2,1,0:T(8,128)(2,1)}, u32[]{:S(2)}) copy-start(bf16[1,4,32,2048]{3,2,1,0:T(8,128)(2,1)} %refs_9_.1) | copy-start | bytes 1572868
  5.7 5.5 %copy-start.15 = (bf16[1,4,8,1024]{3,2,1,0:T(8,128)(2,1)S(1)}, bf16[1,4,8,1024]{3,2,1,0:T(8,128)(2,1)}, u32[]{:S(2)}) copy-start(bf16[1,4,8,1024]{3,2,1,0:T(8,128)(2,1)} %param.33) | copy-start | bytes 196612
  5.8 5.5 %copy-start.16 = (bf16[1,4,8,1024]{3,2,1,0:T(8,128)(2,1)S(1)}, bf16[1,4,8,1024]{3,2,1,0:T(8,128)(2,1)}, u32[]{:S(2)}) copy-start(bf16[1,4,8,1024]{3,2,1,0:T(8,128)(2,1)} %param.34) | copy-start | bytes 196612
  11.3 26.3 %collective-permute-start.12 = (bf16[2,512,512]{2,1,0:T(8,128)(2,1)S(1)}, bf16[2,512,512]{2,1,0:T(8,128)(2,1)}, u32[]{:S(2)}, u32[]{:S(2)}) collective-permute-start(bf16[2,512,512]{2,1,0:T(8,128)(2,1)S(1)} %get-tuple-element.500), channel_id=1, source_target_pairs={{0,16},{4,20},{8,24},{12,28},{16,0},{20,4},{24,8},{28,12},{1,17},{... | collective-permute-start | bytes 3145736 | tf_op jit(solution)/shard_map/cond/branch_3_fun/ppermute | solution.py:25
  12.9 45.7 %collective-permute-start.13 = (bf16[2,512,512]{2,1,0:T(8,128)(2,1)}, bf16[2,512,512]{2,1,0:T(8,128)(2,1)}, u32[]{:S(2)}, u32[]{:S(2)}) collective-permute-start(bf16[2,512,512]{2,1,0:T(8,128)(2,1)} %get-tuple-element.501), channel_id=1, source_target_pairs={{0,16},{4,20},{8,24},{12,28},{16,0},{20,4},{24,8},{28,12},{1,17},{... | collective-permute-start | bytes 3145736 | tf_op jit(solution)/shard_map/cond/branch_3_fun/ppermute | solution.py:25
  13.4 37.4 %collective-permute-start.15 = (bf16[1,4,32,2048]{3,2,1,0:T(8,128)(2,1)S(1)}, bf16[1,4,32,2048]{3,2,1,0:T(8,128)(2,1)}, u32[]{:S(2)}, u32[]{:S(2)}) collective-permute-start(bf16[1,4,32,2048]{3,2,1,0:T(8,128)(2,1)S(1)} %get-tuple-element.505), channel_id=1, source_target_pairs={{0,2},{1,3},{2,0},{3,1},{4,6},{5,7},{6,4},{7,5},{8,10},{9,11},{10,... | collective-permute-start | bytes 1572872 | tf_op jit(solution)/shard_map/cond/branch_3_fun/ppermute | solution.py:25
  13.4 37.4 %collective-permute-start.14 = (bf16[1,4,32,2048]{3,2,1,0:T(8,128)(2,1)S(1)}, bf16[1,4,32,2048]{3,2,1,0:T(8,128)(2,1)}, u32[]{:S(2)}, u32[]{:S(2)}) collective-permute-start(bf16[1,4,32,2048]{3,2,1,0:T(8,128)(2,1)S(1)} %get-tuple-element.505), channel_id=1, source_target_pairs={{0,1},{1,0},{2,3},{3,2},{4,5},{5,4},{6,7},{7,6},{8,9},{9,8},{10,11... | collective-permute-start | bytes 1572872 | tf_op jit(solution)/shard_map/cond/branch_3_fun/ppermute | solution.py:25
  58.6 26.2 %collective-permute-start.33 = (bf16[2,512,512]{2,1,0:T(8,128)(2,1)S(1)}, bf16[2,512,512]{2,1,0:T(8,128)(2,1)}, u32[]{:S(2)}, u32[]{:S(2)}) collective-permute-start(bf16[2,512,512]{2,1,0:T(8,128)(2,1)S(1)} %get-tuple-element.550), channel_id=1, source_target_pairs={{0,8},{4,12},{8,0},{12,4},{16,24},{20,28},{24,16},{28,20},{1,9},{5... | collective-permute-start | bytes 3145736 | tf_op jit(solution)/shard_map/cond/branch_1_fun/ppermute | solution.py:25
  62.8 42.0 %collective-permute-start.34 = (bf16[2,512,512]{2,1,0:T(8,128)(2,1)}, bf16[2,512,512]{2,1,0:T(8,128)(2,1)}, u32[]{:S(2)}, u32[]{:S(2)}) collective-permute-start(bf16[2,512,512]{2,1,0:T(8,128)(2,1)} %pick_1.22), channel_id=1, source_target_pairs={{0,8},{4,12},{8,0},{12,4},{16,24},{20,28},{24,16},{28,20},{1,9},{5... | collective-permute-start | bytes 3145736 | tf_op jit(solution)/shard_map/cond/branch_1_fun/ppermute | solution.py:25
  63.4 16.9 %copy-start.1 = (bf16[1,4,512,1024]{3,2,1,0:T(8,128)(2,1)S(1)}, bf16[1,4,512,1024]{3,2,1,0:T(8,128)(2,1)}, u32[]{:S(2)}) copy-start(bf16[1,4,512,1024]{3,2,1,0:T(8,128)(2,1)} %get-tuple-element.552.refs_0_.refs_6_) | copy-start | bytes 12582916 | tf_op jit(solution)/shard_map/cond
  63.4 16.9 %copy-start.8 = (bf16[1,4,512,1024]{3,2,1,0:T(8,128)(2,1)S(1)}, bf16[1,4,512,1024]{3,2,1,0:T(8,128)(2,1)}, u32[]{:S(2)}) copy-start(bf16[1,4,512,1024]{3,2,1,0:T(8,128)(2,1)} %get-tuple-element.553.refs_1_.refs_7_) | copy-start | bytes 12582916 | tf_op jit(solution)/shard_map/cond
  75.9 12.5 %collective-permute-start.35 = (bf16[2,272,256]{2,1,0:T(8,128)(2,1)S(1)}, bf16[2,272,256]{2,1,0:T(8,128)(2,1)}, u32[]{:S(2)}, u32[]{:S(2)}) collective-permute-start(bf16[2,272,256]{2,1,0:T(8,128)(2,1)S(1)} %get-tuple-element.563), channel_id=1, source_target_pairs={{0,1},{1,0},{2,3},{3,2},{4,5},{5,4},{6,7},{7,6},{8,9},{9,8},{10,11... | collective-permute-start | bytes 835592 | tf_op jit(solution)/shard_map/cond/branch_1_fun/ppermute | solution.py:25
  76.0 21.7 %collective-permute-start.36 = (bf16[2,272,256]{2,1,0:T(8,128)(2,1)S(1)}, bf16[2,272,256]{2,1,0:T(8,128)(2,1)}, u32[]{:S(2)}, u32[]{:S(2)}) collective-permute-start(bf16[2,272,256]{2,1,0:T(8,128)(2,1)S(1)} %get-tuple-element.564), channel_id=1, source_target_pairs={{0,2},{1,3},{2,0},{3,1},{4,6},{5,7},{6,4},{7,5},{8,10},{9,11},{10,... | collective-permute-start | bytes 835592 | tf_op jit(solution)/shard_map/cond/branch_1_fun/ppermute | solution.py:25
  76.8 20.9 %collective-permute-start.37 = (bf16[2,272,256]{2,1,0:T(8,128)(2,1)S(1)}, bf16[2,272,256]{2,1,0:T(8,128)(2,1)}, u32[]{:S(2)}, u32[]{:S(2)}) collective-permute-start(bf16[2,272,256]{2,1,0:T(8,128)(2,1)S(1)} %get-tuple-element.565), channel_id=1, source_target_pairs={{0,3},{1,2},{2,1},{3,0},{4,7},{5,6},{6,5},{7,4},{8,11},{9,10},{10,... | collective-permute-start | bytes 835592 | tf_op jit(solution)/shard_map/cond/branch_1_fun/ppermute | solution.py:25
  104.9 26.2 %collective-permute-start.93 = (bf16[2,512,512]{2,1,0:T(8,128)(2,1)S(1)}, bf16[2,512,512]{2,1,0:T(8,128)(2,1)}, u32[]{:S(2)}, u32[]{:S(2)}) collective-permute-start(bf16[2,512,512]{2,1,0:T(8,128)(2,1)S(1)} %get-tuple-element.730), channel_id=1, source_target_pairs={{0,16},{4,20},{8,24},{12,28},{16,0},{20,4},{24,8},{28,12},{1,17},{... | collective-permute-start | bytes 3145736 | tf_op jit(solution)/shard_map/cond/branch_3_fun/ppermute | solution.py:25
  117.0 25.4 %collective-permute-start.94 = (bf16[2,512,256]{2,1,0:T(8,128)(2,1)}, bf16[2,512,256]{2,1,0:T(8,128)(2,1)}, u32[]{:S(2)}, u32[]{:S(2)}) collective-permute-start(bf16[2,512,256]{2,1,0:T(8,128)(2,1)} %get-tuple-element.745), channel_id=1, source_target_pairs={{0,16},{4,20},{8,24},{12,28},{16,0},{20,4},{24,8},{28,12},{1,17},{... | collective-permute-start | bytes 1572872 | tf_op jit(solution)/shard_map/cond/branch_3_fun/ppermute | solution.py:25
  117.5 32.7 %collective-permute-start.95 = (bf16[2,512,256]{2,1,0:T(8,128)(2,1)}, bf16[2,512,256]{2,1,0:T(8,128)(2,1)}, u32[]{:S(2)}, u32[]{:S(2)}) collective-permute-start(bf16[2,512,256]{2,1,0:T(8,128)(2,1)} %get-tuple-element.746), channel_id=1, source_target_pairs={{0,16},{4,20},{8,24},{12,28},{16,0},{20,4},{24,8},{28,12},{1,17},{... | collective-permute-start | bytes 1572872 | tf_op jit(solution)/shard_map/cond/branch_3_fun/ppermute | solution.py:25
  119.1 17.3 %collective-permute-start.96 = (bf16[1,272,256]{2,1,0:T(8,128)(2,1)S(1)}, bf16[1,272,256]{2,1,0:T(8,128)(2,1)}, u32[]{:S(2)}, u32[]{:S(2)}) collective-permute-start(bf16[1,272,256]{2,1,0:T(8,128)(2,1)S(1)} %get-tuple-element.747), channel_id=1, source_target_pairs={{0,1},{1,0},{2,3},{3,2},{4,5},{5,4},{6,7},{7,6},{8,9},{9,8},{10,11... | collective-permute-start | bytes 417800 | tf_op jit(solution)/shard_map/cond/branch_3_fun/ppermute | solution.py:25
  119.1 20.5 %collective-permute-start.97 = (bf16[1,272,256]{2,1,0:T(8,128)(2,1)S(1)}, bf16[1,272,256]{2,1,0:T(8,128)(2,1)}, u32[]{:S(2)}, u32[]{:S(2)}) collective-permute-start(bf16[1,272,256]{2,1,0:T(8,128)(2,1)S(1)} %get-tuple-element.748), channel_id=1, source_target_pairs={{0,2},{1,3},{2,0},{3,1},{4,6},{5,7},{6,4},{7,5},{8,10},{9,11},{10,... | collective-permute-start | bytes 417800 | tf_op jit(solution)/shard_map/cond/branch_3_fun/ppermute | solution.py:25
  131.1 8.5 %collective-permute-start.98 = (bf16[1,272,256]{2,1,0:T(8,128)(2,1)S(1)}, bf16[1,272,256]{2,1,0:T(8,128)(2,1)}, u32[]{:S(2)}, u32[]{:S(2)}) collective-permute-start(bf16[1,272,256]{2,1,0:T(8,128)(2,1)S(1)} %get-tuple-element.749), channel_id=1, source_target_pairs={{0,3},{1,2},{2,1},{3,0},{4,7},{5,6},{6,5},{7,4},{8,11},{9,10},{10,... | collective-permute-start | bytes 417800 | tf_op jit(solution)/shard_map/cond/branch_3_fun/ppermute | solution.py:25
  136.3 14.3 %collective-permute-start.102 = (bf16[1,272,256]{2,1,0:T(8,128)(2,1)S(1)}, bf16[1,272,256]{2,1,0:T(8,128)(2,1)}, u32[]{:S(2)}, u32[]{:S(2)}) collective-permute-start(bf16[1,272,256]{2,1,0:T(8,128)(2,1)S(1)} %get-tuple-element.753), channel_id=1, source_target_pairs={{0,3},{1,2},{2,1},{3,0},{4,7},{5,6},{6,5},{7,4},{8,11},{9,10},{10,... | collective-permute-start | bytes 417800 | tf_op jit(solution)/shard_map/cond/branch_3_fun/ppermute | solution.py:25
  139.6 11.0 %collective-permute-start.101 = (bf16[1,272,256]{2,1,0:T(8,128)(2,1)S(1)}, bf16[1,272,256]{2,1,0:T(8,128)(2,1)}, u32[]{:S(2)}, u32[]{:S(2)}) collective-permute-start(bf16[1,272,256]{2,1,0:T(8,128)(2,1)S(1)} %get-tuple-element.750.refs_4_), channel_id=1, source_target_pairs={{0,2},{1,3},{2,0},{3,1},{4,6},{5,7},{6,4},{7,5},{8,10},{9,11},{10,... | collective-permute-start | bytes 417800 | tf_op jit(solution)/shard_map/cond/branch_3_fun/ppermute | solution.py:25
  145.4 5.2 %collective-permute-start.100 = (bf16[1,144,256]{2,1,0:T(8,128)(2,1)S(1)}, bf16[1,144,256]{2,1,0:T(8,128)(2,1)}, u32[]{:S(2)}, u32[]{:S(2)}) collective-permute-start(bf16[1,144,256]{2,1,0:T(8,128)(2,1)S(1)} %get-tuple-element.752), channel_id=1, source_target_pairs={{0,1},{1,0},{2,3},{3,2},{4,5},{5,4},{6,7},{7,6},{8,9},{9,8},{10,11... | collective-permute-start | bytes 221192 | tf_op jit(solution)/shard_map/cond/branch_3_fun/ppermute | solution.py:25
  145.5 5.1 %collective-permute-start.99 = (bf16[1,128,256]{2,1,0:T(8,128)(2,1)S(1)}, bf16[1,128,256]{2,1,0:T(8,128)(2,1)}, u32[]{:S(2)}, u32[]{:S(2)}) collective-permute-start(bf16[1,128,256]{2,1,0:T(8,128)(2,1)S(1)} %get-tuple-element.751), channel_id=1, source_target_pairs={{0,1},{1,0},{2,3},{3,2},{4,5},{5,4},{6,7},{7,6},{8,9},{9,8},{10,11... | collective-permute-start | bytes 196616 | tf_op jit(solution)/shard_map/cond/branch_3_fun/ppermute | solution.py:25

commit v5 on v4

--- a/solution.py
+++ b/solution.py
@@ -494,15 +494,15 @@
         return jax.ShapeDtypeStruct((2, segment, len(pieces) * size.wide), BF16)
 
     plan, *scalars = pl.pallas_call(
-        functools.partial(plan_kernel, at, halves),
+        functools.partial(plan_kernel, at, halves[:1]),
         out_shape=(
             jax.ShapeDtypeStruct((at.size,), jnp.int32),
             *[jax.ShapeDtypeStruct((1,), jnp.int32)] * matchings,
-            *map(held, halves),
+            held(halves[0]),
         ),
         in_specs=[SMEM] * 4 + [ANY] * 2,
-        out_specs=(SMEM, *[SMEM] * matchings, *[VMEM] * len(halves)),
-        scratch_shapes=[pltpu.SemaphoreType.DMA((len(halves),))],
+        out_specs=(SMEM, *[SMEM] * matchings, VMEM),
+        scratch_shapes=[pltpu.SemaphoreType.DMA((1,))],
         name="plan",
     )(masks, movers, block_lists.transpose(0, 2, 1), lengths.T, *caches)
     indices, initial = scalars[:matchings], scalars[matchings:]
@@ -579,7 +579,8 @@
         return pick(step, halves[:1], [*sources, arrived[0], arrived[0]])[0]
 
     def first_branch(mask):
-        arrived = [exchange(block, "group", mask) for block in initial]
+        moving = [*initial, *pick(0, halves[1:], caches)]
+        arrived = [exchange(block, "group", mask) for block in moving]
         asked = [query] + [exchange(query, "ctx", piece) for piece in everyone[1:-1]]
         return arrived, prepare(1, caches, arrived), asked, pad_new()
 

time: 160 us -> 162 us (1.012); the launches traced: 157 us -> 162 us
  waiting for transfers between devices: 78 us -> 80.7 us
  starting transfers between devices: 24.9 us -> 27.3 us
    pallas_call x4 -> x5, Pallas kernels: 8.99 us -> 11.7 us  [pick(): pl.pallas_call(functools.partial(pick_kernel, at, step, choices), out_sha...]
    ppermute x20, waiting for transfers between devices: 78 us -> 80.7 us  [exchange(): lax.ppermute(block, axis, [(i, i ^ mask) for i in range(lax.axis_size(axi...]
    ppermute x20, starting transfers between devices: 24.9 us -> 27.3 us  [exchange(): lax.ppermute(block, axis, [(i, i ^ mask) for i in range(lax.axis_size(axi...]
  transfers between devices with their start and end apart: 20 -> 20, of which waited for: 10 -> 10; matrix products, arithmetic and copies ran while one was open for 0% -> 0% of each run, Pallas kernels for 29% -> 28%
where the time goes in v5:
time: 162 us
  waiting for transfers between devices  80.7 us (50%)
  Pallas kernels  51.3 us (32%)
  starting transfers between devices  27.3 us (17%)
  between operations  2.78 us (2%)
    ppermute x20, waiting for transfers between devices, exchange(): lax.ppermute(block, axis, [(i, i ^ mask) for i in range(lax.axis_size(axi...  80.7 us
    pallas_call x4, Pallas kernels, attend(): pl.pallas_call(functools.partial(attend_kernel, at, size, first, newest,...  27.9 us
    ppermute x20, starting transfers between devices, exchange(): lax.ppermute(block, axis, [(i, i ^ mask) for i in range(lax.axis_size(axi...  27.3 us
    pallas_call x5, Pallas kernels, pick(): pl.pallas_call(functools.partial(pick_kernel, at, step, choices), out_sha...  11.7 us
    pallas_call x1, Pallas kernels, shards(): pl.pallas_call(functools.partial(finish_kernel, at, size, parcels, lots,...  5.91 us
  transfers between devices with their start and end apart: 20, of which 10 were waited for; matrix products, arithmetic and copies ran while one was open for 0% of the time, Pallas kernels for 28%

profile of v5, /device:TPU:0, one launch (start us, length us, event | category | flops | bytes accessed | tf_op | source)
XLA Modules:
  0.0 162.3 jit_solution(4303421844271848276)
XLA Ops:
  0.6 5.1 %collective-permute-start.133 = (bf16[1,4,32,2048]{3,2,1,0:T(8,128)(2,1)}, bf16[1,4,32,2048]{3,2,1,0:T(8,128)(2,1)S(1)}, u32[]{:S(2)}, u32[]{:S(2)}) collective-permute-start(bf16[1,4,32,2048]{3,2,1,0:T(8,128)(2,1)} %refs_9_.1), channel_id=1, source_target_pairs={{0,3},{1,2},{2,1},{3,0},{4,7},{5,6},{6,5},{7,4},{8,11},{9,10},{10,... | collective-permute-start | bytes 1572872 | tf_op jit(solution)/shard_map/ppermute | solution.py:25
  5.8 2.8 %plan.1 = (s32[51]{0:T(128)S(1)}, s32[1]{0:T(128)}, s32[1]{0:T(128)}, s32[1]{0:T(128)}, bf16[2,512,512]{2,1,0:T(8,128)(2,1)S(1)}) custom-call(s32[3]{0:T(128)} %masks.1, s32[3,8]{1,0:T(4,128)} %movers.1, s32[3,4,8]{2,1,0:T(4,128)} %bitcast.33, s32[4,8]{1,0:T(4,128)} %bitcast.34, bf16[1,4,512,1024]{3,2,1,0:T(8,128)(2,1)} %refs_3_.1, ...), custom_call_target="tpu_custom_call" | custom-call | tf_op jit(solution)/shard_map/plan/pallas_call | solution.py:496
  10.5 48.2 %conditional.3 = (bf16[2,512,512]{2,1,0:T(8,128)(2,1)}, bf16[2,512,512]{2,1,0:T(8,128)(2,1)}, bf16[2,512,512]{2,1,0:T(8,128)(2,1)S(1)}, bf16[1,4,32,2048]{3,2,1,...) conditional(s32[]{:T(128)} %bitcast.18, ...), branch_computations={%region_0.1_spmd, %region_1.2_spmd, %region_2.3_spmd, %region_3.4_... | conditional | bytes 31476348 | solution.py:614
  10.6 2.5 %collective-permute-start.20 = (bf16[2,512,512]{2,1,0:T(8,128)(2,1)S(1)}, bf16[2,512,512]{2,1,0:T(8,128)(2,1)}, u32[]{:S(2)}, u32[]{:S(2)}) collective-permute-start(bf16[2,512,512]{2,1,0:T(8,128)(2,1)S(1)} %get-tuple-element.497), channel_id=1, source_target_pairs={{0,24},{4,28},{8,16},{12,20},{16,8},{20,12},{24,0},{28,4},{1,25},{... | collective-permute-start | bytes 3145736 | tf_op jit(solution)/shard_map/cond/branch_5_fun/ppermute | solution.py:25
  13.1 2.8 %pick_0.12 = bf16[2,512,512]{2,1,0:T(8,128)(2,1)} custom-call(s32[51]{0:T(128)S(1)} %get-tuple-element.498.plan, bf16[1,4,512,1024]{3,2,1,0:T(8,128)(2,1)} %get-tuple-element.499.refs_0_, bf16[1,4,512,1024]{3,2,1,0:T(8,128)(2,1)} %get-tuple-element.500.refs_1_), custom_call_target="tpu_custom_call" | custom-call | bytes 9250000 | tf_op jit(solution)/shard_map/cond/branch_5_fun/pick_0/pallas_call | solution.py:516
  17.0 20.7 %collective-permute-done.20.refs_2_.refs_3_ = bf16[2,512,512]{2,1,0:T(8,128)(2,1)} collective-permute-done((bf16[2,512,512]{2,1,0:T(8,128)(2,1)S(1)}, bf16[2,512,512]{2,1,0:T(8,128)(2,1)}, u32[]{:S(2)}, u32[]{:S(2)}) %collective-permute-start.20) | collective-permute-done | bytes 1048608 | tf_op jit(solution)/shard_map/cond/branch_5_fun/ppermute | solution.py:25
  37.7 1.8 %pick_1.19 = bf16[2,512,512]{2,1,0:T(8,128)(2,1)S(1)} custom-call(s32[51]{0:T(128)S(1)} %get-tuple-element.498.plan, bf16[1,4,512,1024]{3,2,1,0:T(8,128)(2,1)} %get-tuple-element.499.refs_0_, bf16[1,4,512,1024]{3,2,1,0:T(8,128)(2,1)} %get-tuple-element.500.refs_1_, bf16[2,512,512]{2,1,0:T(8,128)(2,1)} %collective-permute-done.20.refs_2_.refs_3_, ...), custom_call_target="tpu_custom_call" | custom-call | bytes 9250000 | tf_op jit(solution)/shard_map/cond/branch_5_fun/pick_1/pallas_call | solution.py:516
  39.5 11.3 %collective-permute-done.23 = bf16[1,4,32,2048]{3,2,1,0:T(8,128)(2,1)} collective-permute-done((bf16[1,4,32,2048]{3,2,1,0:T(8,128)(2,1)S(1)}, bf16[1,4,32,2048]{3,2,1,0:T(8,128)(2,1)}, u32[]{:S(2)}, u32[]{:S(2)}) %collective-permute-start.23) | collective-permute-done | bytes 524320 | tf_op jit(solution)/shard_map/cond/branch_5_fun/ppermute | solution.py:25
  50.8 7.9 %collective-permute-done.21 = bf16[2,512,512]{2,1,0:T(8,128)(2,1)} collective-permute-done((bf16[2,512,512]{2,1,0:T(8,128)(2,1)}, bf16[2,512,512]{2,1,0:T(8,128)(2,1)}, u32[]{:S(2)}, u32[]{:S(2)}) %collective-permute-start.21) | collective-permute-done | bytes 1048608 | tf_op jit(solution)/shard_map/cond/branch_5_fun/ppermute | solution.py:25
  58.7 48.8 %conditional.4 = (bf16[2,512,512]{2,1,0:T(8,128)(2,1)}, bf16[2,512,512]{2,1,0:T(8,128)(2,1)}, bf16[2,512,512]{2,1,0:T(8,128)(2,1)S(1)}, bf16[2,272,256]{2,1,0:T(...) conditional(s32[]{:T(128)} %bitcast.17, ...), branch_computations={%region_7.8_spmd, %region_8.9_spmd, %region_9.10_spmd, %region_10.... | conditional | bytes 126685712 | solution.py:614
  59.4 2.7 %pick_1.27 = bf16[2,512,512]{2,1,0:T(8,128)(2,1)} custom-call(s32[51]{0:T(128)S(1)} %get-tuple-element.620.plan, bf16[1,4,512,1024]{3,2,1,0:T(8,128)(2,1)} %get-tuple-element.621.refs_0_.refs_6_, bf16[1,4,512,1024]{3,2,1,0:T(8,128)(2,1)} %get-tuple-element.622.refs_1_.refs_7_, bf16[2,512,512]{2,1,0:T(8,128)(2,1)} %get-tuple-element.623.refs_2_.refs_8_, ...), custom_call_target="tpu_custom_call" | custom-call | bytes 9250000 | tf_op jit(solution)/shard_map/cond/branch_6_fun/pick_1/pallas_call | solution.py:516
  62.2 2.0 %collective-permute-start.59 = (bf16[2,512,512]{2,1,0:T(8,128)(2,1)}, bf16[2,512,512]{2,1,0:T(8,128)(2,1)}, u32[]{:S(2)}, u32[]{:S(2)}) collective-permute-start(bf16[2,512,512]{2,1,0:T(8,128)(2,1)} %pick_1.27), channel_id=1, source_target_pairs={{0,28},{4,24},{8,20},{12,16},{16,12},{20,8},{24,4},{28,0},{1,29},{... | collective-permute-start | bytes 3145736 | tf_op jit(solution)/shard_map/cond/branch_6_fun/ppermute | solution.py:25
  64.2 12.4 %attend_0_2_4.13 = (bf16[2,272,256]{2,1,0:T(8,128)(2,1)S(1)}, bf16[2,272,256]{2,1,0:T(8,128)(2,1)S(1)}, bf16[2,272,256]{2,1,0:T(8,128)(2,1)S(1)}, bf16[2,272,256]{2,1,0:T(8,128)(2,1)S(1)}) custom-call(s32[51]{0:T(128)S(1)} %get-tuple-element.620.plan, bf16[1,4,32,2048]{3,2,1,0:T(8,128)(2,1)S(1)} %get-tuple-element.625.refs_0_, ...), custom_call_target="tpu_custom_call" | custom-call | bytes 48100000 | tf_op jit(solution)/shard_map/cond/branch_6_fun/attend_0_2_4/pallas_call | solution.py:533
  77.6 3.5 %collective-permute-start.62 = (bf16[2,272,256]{2,1,0:T(8,128)(2,1)S(1)}, bf16[2,272,256]{2,1,0:T(8,128)(2,1)}, u32[]{:S(2)}, u32[]{:S(2)}) collective-permute-start(bf16[2,272,256]{2,1,0:T(8,128)(2,1)S(1)} %get-tuple-element.634), channel_id=1, source_target_pairs={{0,3},{1,2},{2,1},{3,0},{4,7},{5,6},{6,5},{7,4},{8,11},{9,10},{10,... | collective-permute-start | bytes 835592 | tf_op jit(solution)/shard_map/cond/branch_6_fun/ppermute | solution.py:25
  81.1 3.0 %settle.13 = (bf16[1,4,512,1024]{3,2,1,0:T(8,128)(2,1)}, bf16[1,4,512,1024]{3,2,1,0:T(8,128)(2,1)}) custom-call(s32[51]{0:T(128)S(1)} %get-tuple-element.620.plan, bf16[1,4,512,1024]{3,2,1,0:T(8,128)(2,1)S(1)} %copy-done.6, bf16[1,4,512,1024]{3,2,1,0:T(8,128)(2,1)S(1)} %copy-done.13, bf16[2,512,512]{2,1,0:T(8,128)(2,1)} %get-tuple-element.623.refs_2_.refs_8_, ...), custom_call_target="tpu_custom_call" | custom-call | bytes 14800000 | tf_op jit(solution)/shard_map/cond/branch_6_fun/settle/pallas_call | solution.py:560
  85.1 1.8 %pick_2.20 = bf16[2,512,512]{2,1,0:T(8,128)(2,1)S(1)} custom-call(s32[51]{0:T(128)S(1)} %get-tuple-element.620.plan, bf16[1,4,512,1024]{3,2,1,0:T(8,128)(2,1)} %get-tuple-element.621.refs_0_.refs_6_, bf16[1,4,512,1024]{3,2,1,0:T(8,128)(2,1)} %get-tuple-element.622.refs_1_.refs_7_, bf16[2,512,512]{2,1,0:T(8,128)(2,1)} %get-tuple-element.623.refs_2_.refs_8_, ...), custom_call_target="tpu_custom_call" | custom-call | bytes 9250000 | tf_op jit(solution)/shard_map/cond/branch_6_fun/pick_2/pallas_call | solution.py:516
  86.9 2.4 %collective-permute-done.60 = bf16[2,272,256]{2,1,0:T(8,128)(2,1)} collective-permute-done((bf16[2,272,256]{2,1,0:T(8,128)(2,1)S(1)}, bf16[2,272,256]{2,1,0:T(8,128)(2,1)}, u32[]{:S(2)}, u32[]{:S(2)}) %collective-permute-start.60) | collective-permute-done | bytes 278560 | tf_op jit(solution)/shard_map/cond/branch_6_fun/ppermute | solution.py:25
  89.2 10.0 %collective-permute-done.61 = bf16[2,272,256]{2,1,0:T(8,128)(2,1)} collective-permute-done((bf16[2,272,256]{2,1,0:T(8,128)(2,1)S(1)}, bf16[2,272,256]{2,1,0:T(8,128)(2,1)}, u32[]{:S(2)}, u32[]{:S(2)}) %collective-permute-start.61) | collective-permute-done | bytes 278560 | tf_op jit(solution)/shard_map/cond/branch_6_fun/ppermute | solution.py:25
  99.3 8.3 %collective-permute-done.59 = bf16[2,512,512]{2,1,0:T(8,128)(2,1)} collective-permute-done((bf16[2,512,512]{2,1,0:T(8,128)(2,1)}, bf16[2,512,512]{2,1,0:T(8,128)(2,1)}, u32[]{:S(2)}, u32[]{:S(2)}) %collective-permute-start.59) | collective-permute-done | bytes 1048608 | tf_op jit(solution)/shard_map/cond/branch_6_fun/ppermute | solution.py:25
  107.6 48.7 %conditional.5 = (bf16[2,512,512]{2,1,0:T(8,128)(2,1)}, bf16[2,512,256]{2,1,0:T(8,128)(2,1)}, bf16[2,512,256]{2,1,0:T(8,128)(2,1)}, bf16[1,272,256]{2,1,0:T(8,12...) conditional(s32[]{:T(128)} %bitcast.16, ...), branch_computations={%region_14.15_spmd, %region_15.16_spmd, %region_16.17_spmd, %regio... | conditional | bytes 70931432 | solution.py:614
  108.9 7.8 %attend_2_1_4.12 = (bf16[1,272,256]{2,1,0:T(8,128)(2,1)}, bf16[1,272,256]{2,1,0:T(8,128)(2,1)S(1)}, bf16[1,272,256]{2,1,0:T(8,128)(2,1)S(1)}, bf16[1,272,256]{2,1,0:T(8,128)(2,1)S(1)}) custom-call(s32[51]{0:T(128)S(1)} %get-tuple-element.758.plan, bf16[1,4,32,2048]{3,2,1,0:T(8,128)(2,1)S(1)} %get-tuple-element.765.refs_0_, ...), custom_call_target="tpu_custom_call" | custom-call | bytes 25900000 | tf_op jit(solution)/shard_map/cond/branch_5_fun/attend_2_1_4/pallas_call | solution.py:533
  116.8 2.7 %pick_2.26 = (bf16[2,512,256]{2,1,0:T(8,128)(2,1)}, bf16[2,512,256]{2,1,0:T(8,128)(2,1)}) custom-call(s32[51]{0:T(128)S(1)} %get-tuple-element.758.plan, bf16[1,4,512,1024]{3,2,1,0:T(8,128)(2,1)} %get-tuple-element.759.refs_6_.refs_0_, bf16[1,4,512,1024]{3,2,1,0:T(8,128)(2,1)} %get-tuple-element.760.refs_7_.refs_1_, ...), custom_call_target="tpu_custom_call" | custom-call | bytes 9250000 | tf_op jit(solution)/shard_map/cond/branch_5_fun/pick_2/pallas_call | solution.py:516
  119.5 1.6 collective-permute-start.114
  121.1 1.4 collective-permute-start.115
  123.5 11.1 %collective-permute-done.113.refs_4_ = bf16[2,512,512]{2,1,0:T(8,128)(2,1)} collective-permute-done((bf16[2,512,512]{2,1,0:T(8,128)(2,1)S(1)}, bf16[2,512,512]{2,1,0:T(8,128)(2,1)}, u32[]{:S(2)}, u32[]{:S(2)}) %collective-permute-start.113) | collective-permute-done | bytes 1048608 | tf_op jit(solution)/shard_map/cond/branch_5_fun/ppermute | solution.py:25
  134.9 4.6 %attend_3_1_2.12 = (bf16[1,272,256]{2,1,0:T(8,128)(2,1)S(1)}, bf16[1,272,256]{2,1,0:T(8,128)(2,1)S(1)}) custom-call(s32[51]{0:T(128)S(1)} %get-tuple-element.758.plan, bf16[1,4,32,2048]{3,2,1,0:T(8,128)(2,1)} %get-tuple-element.767.refs_2_.refs_0_, bf16[1,4,32,2048]{3,2,1,0:T(8,128)(2,1)S(1)} %get-tuple-element.768.refs_3_.refs_1_, ...), custom_call_target="tpu_custom_call" | custom-call | bytes 14800000 | tf_op jit(solution)/shard_map/cond/branch_5_fun/attend_3_1_2/pallas_call | solution.py:533
  139.5 3.6 %collective-permute-start.122 = (bf16[1,272,256]{2,1,0:T(8,128)(2,1)S(1)}, bf16[1,272,256]{2,1,0:T(8,128)(2,1)}, u32[]{:S(2)}, u32[]{:S(2)}) collective-permute-start(bf16[1,272,256]{2,1,0:T(8,128)(2,1)S(1)} %get-tuple-element.780), channel_id=1, source_target_pairs={{0,3},{1,2},{2,1},{3,0},{4,7},{5,6},{6,5},{7,4},{8,11},{9,10},{10,... | collective-permute-start | bytes 417800 | tf_op jit(solution)/shard_map/cond/branch_5_fun/ppermute | solution.py:25
  143.1 2.7 %collective-permute-done.114.refs_3_ = bf16[2,512,256]{2,1,0:T(8,128)(2,1)} collective-permute-done((bf16[2,512,256]{2,1,0:T(8,128)(2,1)}, bf16[2,512,256]{2,1,0:T(8,128)(2,1)}, u32[]{:S(2)}, u32[]{:S(2)}) %collective-permute-start.114) | collective-permute-done | bytes 524320 | tf_op jit(solution)/shard_map/cond/branch_5_fun/ppermute | solution.py:25
  145.8 3.1 %attend_3_1_1.12 = (bf16[1,128,256]{2,1,0:T(8,128)(2,1)S(1)}, bf16[1,144,256]{2,1,0:T(8,128)(2,1)S(1)}) custom-call(s32[51]{0:T(128)S(1)} %get-tuple-element.758.plan, bf16[1,4,32,2048]{3,2,1,0:T(8,128)(2,1)} %get-tuple-element.766.refs_1_.refs_0_, bf16[4,16,1024]{2,1,0:T(8,128)(2,1)S(1)} %get-tuple-element.769.refs_4_.refs_2_.refs_1_, ...), custom_call_target="tpu_custom_call" | custom-call | bytes 9250000 | tf_op jit(solution)/shard_map/cond/branch_5_fun/attend_3_1_1/pallas_call | solution.py:533
  149.0 2.0 %collective-permute-start.119 = (bf16[1,128,256]{2,1,0:T(8,128)(2,1)S(1)}, bf16[1,128,256]{2,1,0:T(8,128)(2,1)}, u32[]{:S(2)}, u32[]{:S(2)}) collective-permute-start(bf16[1,128,256]{2,1,0:T(8,128)(2,1)S(1)} %get-tuple-element.778), channel_id=1, source_target_pairs={{0,1},{1,0},{2,3},{3,2},{4,5},{5,4},{6,7},{7,6},{8,9},{9,8},{10,11... | collective-permute-start | bytes 196616 | tf_op jit(solution)/shard_map/cond/branch_5_fun/ppermute | solution.py:25
  151.0 5.2 %collective-permute-done.115 = bf16[2,512,256]{2,1,0:T(8,128)(2,1)} collective-permute-done((bf16[2,512,256]{2,1,0:T(8,128)(2,1)}, bf16[2,512,256]{2,1,0:T(8,128)(2,1)}, u32[]{:S(2)}, u32[]{:S(2)}) %collective-permute-start.115) | collective-permute-done | bytes 524320 | tf_op jit(solution)/shard_map/cond/branch_5_fun/ppermute | solution.py:25
  156.3 5.9 %finish.1 = (bf16[1,4,32,2048]{3,2,1,0:T(8,128)(2,1)}, bf16[1,4,512,1024]{3,2,1,0:T(8,128)(2,1)}, bf16[1,4,512,1024]{3,2,1,0:T(8,128)(2,1)}) custom-call(s32[51]{0:T(128)S(1)} %get-tuple-element.840.plan, bf16[2,512,512]{2,1,0:T(8,128)(2,1)} %get-tuple-element.855.refs_0_, ...), custom_call_target="tpu_custom_call", output_to_operand_aliasing={{1}: (25, {}), {2}: (26, {})} | custom-call | tf_op jit(solution)/shard_map/finish/pallas_call | solution.py:641
  (35 shorter events, 6.6 us)
Async XLA Ops:
  0.6 58.1 %collective-permute-start.133 = (bf16[1,4,32,2048]{3,2,1,0:T(8,128)(2,1)}, bf16[1,4,32,2048]{3,2,1,0:T(8,128)(2,1)S(1)}, u32[]{:S(2)}, u32[]{:S(2)}) collective-permute-start(bf16[1,4,32,2048]{3,2,1,0:T(8,128)(2,1)} %refs_9_.1), channel_id=1, source_target_pairs={{0,3},{1,2},{2,1},{3,0},{4,7},{5,6},{6,5},{7,4},{8,11},{9,10},{10,... | collective-permute-start | bytes 1572872 | tf_op jit(solution)/shard_map/ppermute | solution.py:25
  5.7 4.8 %copy-start.14 = (bf16[1,4,32,2048]{3,2,1,0:T(8,128)(2,1)S(1)}, bf16[1,4,32,2048]{3,2,1,0:T(8,128)(2,1)}, u32[]{:S(2)}) copy-start(bf16[1,4,32,2048]{3,2,1,0:T(8,128)(2,1)} %refs_9_.1) | copy-start | bytes 1572868
  5.7 4.8 %copy-start.15 = (bf16[1,4,8,1024]{3,2,1,0:T(8,128)(2,1)S(1)}, bf16[1,4,8,1024]{3,2,1,0:T(8,128)(2,1)}, u32[]{:S(2)}) copy-start(bf16[1,4,8,1024]{3,2,1,0:T(8,128)(2,1)} %param.33) | copy-start | bytes 196612
  5.8 4.8 %copy-start.16 = (bf16[1,4,8,1024]{3,2,1,0:T(8,128)(2,1)S(1)}, bf16[1,4,8,1024]{3,2,1,0:T(8,128)(2,1)}, u32[]{:S(2)}) copy-start(bf16[1,4,8,1024]{3,2,1,0:T(8,128)(2,1)} %param.34) | copy-start | bytes 196612
  10.6 27.2 %collective-permute-start.20 = (bf16[2,512,512]{2,1,0:T(8,128)(2,1)S(1)}, bf16[2,512,512]{2,1,0:T(8,128)(2,1)}, u32[]{:S(2)}, u32[]{:S(2)}) collective-permute-start(bf16[2,512,512]{2,1,0:T(8,128)(2,1)S(1)} %get-tuple-element.497), channel_id=1, source_target_pairs={{0,24},{4,28},{8,16},{12,20},{16,8},{20,12},{24,0},{28,4},{1,25},{... | collective-permute-start | bytes 3145736 | tf_op jit(solution)/shard_map/cond/branch_5_fun/ppermute | solution.py:25
  15.8 42.9 %collective-permute-start.21 = (bf16[2,512,512]{2,1,0:T(8,128)(2,1)}, bf16[2,512,512]{2,1,0:T(8,128)(2,1)}, u32[]{:S(2)}, u32[]{:S(2)}) collective-permute-start(bf16[2,512,512]{2,1,0:T(8,128)(2,1)} %pick_0.12), channel_id=1, source_target_pairs={{0,24},{4,28},{8,16},{12,20},{16,8},{20,12},{24,0},{28,4},{1,25},{... | collective-permute-start | bytes 3145736 | tf_op jit(solution)/shard_map/cond/branch_5_fun/ppermute | solution.py:25
  16.4 34.5 %collective-permute-start.23 = (bf16[1,4,32,2048]{3,2,1,0:T(8,128)(2,1)S(1)}, bf16[1,4,32,2048]{3,2,1,0:T(8,128)(2,1)}, u32[]{:S(2)}, u32[]{:S(2)}) collective-permute-start(bf16[1,4,32,2048]{3,2,1,0:T(8,128)(2,1)S(1)} %get-tuple-element.501), channel_id=1, source_target_pairs={{0,2},{1,3},{2,0},{3,1},{4,6},{5,7},{6,4},{7,5},{8,10},{9,11},{10,... | collective-permute-start | bytes 1572872 | tf_op jit(solution)/shard_map/cond/branch_5_fun/ppermute | solution.py:25
  16.4 34.5 %collective-permute-start.22 = (bf16[1,4,32,2048]{3,2,1,0:T(8,128)(2,1)S(1)}, bf16[1,4,32,2048]{3,2,1,0:T(8,128)(2,1)}, u32[]{:S(2)}, u32[]{:S(2)}) collective-permute-start(bf16[1,4,32,2048]{3,2,1,0:T(8,128)(2,1)S(1)} %get-tuple-element.501), channel_id=1, source_target_pairs={{0,1},{1,0},{2,3},{3,2},{4,5},{5,4},{6,7},{7,6},{8,9},{9,8},{10,11... | collective-permute-start | bytes 1572872 | tf_op jit(solution)/shard_map/cond/branch_5_fun/ppermute | solution.py:25
  58.7 26.4 %collective-permute-start.58 = (bf16[2,512,512]{2,1,0:T(8,128)(2,1)S(1)}, bf16[2,512,512]{2,1,0:T(8,128)(2,1)}, u32[]{:S(2)}, u32[]{:S(2)}) collective-permute-start(bf16[2,512,512]{2,1,0:T(8,128)(2,1)S(1)} %get-tuple-element.619), channel_id=1, source_target_pairs={{0,28},{4,24},{8,20},{12,16},{16,12},{20,8},{24,4},{28,0},{1,29},{... | collective-permute-start | bytes 3145736 | tf_op jit(solution)/shard_map/cond/branch_6_fun/ppermute | solution.py:25
  62.2 45.4 %collective-permute-start.59 = (bf16[2,512,512]{2,1,0:T(8,128)(2,1)}, bf16[2,512,512]{2,1,0:T(8,128)(2,1)}, u32[]{:S(2)}, u32[]{:S(2)}) collective-permute-start(bf16[2,512,512]{2,1,0:T(8,128)(2,1)} %pick_1.27), channel_id=1, source_target_pairs={{0,28},{4,24},{8,20},{12,16},{16,12},{20,8},{24,4},{28,0},{1,29},{... | collective-permute-start | bytes 3145736 | tf_op jit(solution)/shard_map/cond/branch_6_fun/ppermute | solution.py:25
  64.2 16.9 %copy-start.6 = (bf16[1,4,512,1024]{3,2,1,0:T(8,128)(2,1)S(1)}, bf16[1,4,512,1024]{3,2,1,0:T(8,128)(2,1)}, u32[]{:S(2)}) copy-start(bf16[1,4,512,1024]{3,2,1,0:T(8,128)(2,1)} %get-tuple-element.621.refs_0_.refs_6_) | copy-start | bytes 12582916 | tf_op jit(solution)/shard_map/cond
  64.2 16.9 %copy-start.13 = (bf16[1,4,512,1024]{3,2,1,0:T(8,128)(2,1)S(1)}, bf16[1,4,512,1024]{3,2,1,0:T(8,128)(2,1)}, u32[]{:S(2)}) copy-start(bf16[1,4,512,1024]{3,2,1,0:T(8,128)(2,1)} %get-tuple-element.622.refs_1_.refs_7_) | copy-start | bytes 12582916 | tf_op jit(solution)/shard_map/cond
  76.6 12.6 %collective-permute-start.60 = (bf16[2,272,256]{2,1,0:T(8,128)(2,1)S(1)}, bf16[2,272,256]{2,1,0:T(8,128)(2,1)}, u32[]{:S(2)}, u32[]{:S(2)}) collective-permute-start(bf16[2,272,256]{2,1,0:T(8,128)(2,1)S(1)} %get-tuple-element.632), channel_id=1, source_target_pairs={{0,1},{1,0},{2,3},{3,2},{4,5},{5,4},{6,7},{7,6},{8,9},{9,8},{10,11... | collective-permute-start | bytes 835592 | tf_op jit(solution)/shard_map/cond/branch_6_fun/ppermute | solution.py:25
  76.7 22.5 %collective-permute-start.61 = (bf16[2,272,256]{2,1,0:T(8,128)(2,1)S(1)}, bf16[2,272,256]{2,1,0:T(8,128)(2,1)}, u32[]{:S(2)}, u32[]{:S(2)}) collective-permute-start(bf16[2,272,256]{2,1,0:T(8,128)(2,1)S(1)} %get-tuple-element.633), channel_id=1, source_target_pairs={{0,2},{1,3},{2,0},{3,1},{4,6},{5,7},{6,4},{7,5},{8,10},{9,11},{10,... | collective-permute-start | bytes 835592 | tf_op jit(solution)/shard_map/cond/branch_6_fun/ppermute | solution.py:25
  77.6 21.7 %collective-permute-start.62 = (bf16[2,272,256]{2,1,0:T(8,128)(2,1)S(1)}, bf16[2,272,256]{2,1,0:T(8,128)(2,1)}, u32[]{:S(2)}, u32[]{:S(2)}) collective-permute-start(bf16[2,272,256]{2,1,0:T(8,128)(2,1)S(1)} %get-tuple-element.634), channel_id=1, source_target_pairs={{0,3},{1,2},{2,1},{3,0},{4,7},{5,6},{6,5},{7,4},{8,11},{9,10},{10,... | collective-permute-start | bytes 835592 | tf_op jit(solution)/shard_map/cond/branch_6_fun/ppermute | solution.py:25
  107.6 27.0 %collective-permute-start.113 = (bf16[2,512,512]{2,1,0:T(8,128)(2,1)S(1)}, bf16[2,512,512]{2,1,0:T(8,128)(2,1)}, u32[]{:S(2)}, u32[]{:S(2)}) collective-permute-start(bf16[2,512,512]{2,1,0:T(8,128)(2,1)S(1)} %get-tuple-element.757), channel_id=1, source_target_pairs={{0,24},{4,28},{8,16},{12,20},{16,8},{20,12},{24,0},{28,4},{1,25},{... | collective-permute-start | bytes 3145736 | tf_op jit(solution)/shard_map/cond/branch_5_fun/ppermute | solution.py:25
  119.5 26.3 %collective-permute-start.114 = (bf16[2,512,256]{2,1,0:T(8,128)(2,1)}, bf16[2,512,256]{2,1,0:T(8,128)(2,1)}, u32[]{:S(2)}, u32[]{:S(2)}) collective-permute-start(bf16[2,512,256]{2,1,0:T(8,128)(2,1)} %get-tuple-element.772), channel_id=1, source_target_pairs={{0,24},{4,28},{8,16},{12,20},{16,8},{20,12},{24,0},{28,4},{1,25},{... | collective-permute-start | bytes 1572872 | tf_op jit(solution)/shard_map/cond/branch_5_fun/ppermute | solution.py:25
  121.1 35.1 %collective-permute-start.115 = (bf16[2,512,256]{2,1,0:T(8,128)(2,1)}, bf16[2,512,256]{2,1,0:T(8,128)(2,1)}, u32[]{:S(2)}, u32[]{:S(2)}) collective-permute-start(bf16[2,512,256]{2,1,0:T(8,128)(2,1)} %get-tuple-element.773), channel_id=1, source_target_pairs={{0,24},{4,28},{8,16},{12,20},{16,8},{20,12},{24,0},{28,4},{1,25},{... | collective-permute-start | bytes 1572872 | tf_op jit(solution)/shard_map/cond/branch_5_fun/ppermute | solution.py:25
  122.5 17.0 %collective-permute-start.116 = (bf16[1,272,256]{2,1,0:T(8,128)(2,1)S(1)}, bf16[1,272,256]{2,1,0:T(8,128)(2,1)}, u32[]{:S(2)}, u32[]{:S(2)}) collective-permute-start(bf16[1,272,256]{2,1,0:T(8,128)(2,1)S(1)} %get-tuple-element.774), channel_id=1, source_target_pairs={{0,1},{1,0},{2,3},{3,2},{4,5},{5,4},{6,7},{7,6},{8,9},{9,8},{10,11... | collective-permute-start | bytes 417800 | tf_op jit(solution)/shard_map/cond/branch_5_fun/ppermute | solution.py:25
  122.5 20.6 %collective-permute-start.117 = (bf16[1,272,256]{2,1,0:T(8,128)(2,1)S(1)}, bf16[1,272,256]{2,1,0:T(8,128)(2,1)}, u32[]{:S(2)}, u32[]{:S(2)}) collective-permute-start(bf16[1,272,256]{2,1,0:T(8,128)(2,1)S(1)} %get-tuple-element.775), channel_id=1, source_target_pairs={{0,2},{1,3},{2,0},{3,1},{4,6},{5,7},{6,4},{7,5},{8,10},{9,11},{10,... | collective-permute-start | bytes 417800 | tf_op jit(solution)/shard_map/cond/branch_5_fun/ppermute | solution.py:25
  134.6 8.5 %collective-permute-start.118 = (bf16[1,272,256]{2,1,0:T(8,128)(2,1)S(1)}, bf16[1,272,256]{2,1,0:T(8,128)(2,1)}, u32[]{:S(2)}, u32[]{:S(2)}) collective-permute-start(bf16[1,272,256]{2,1,0:T(8,128)(2,1)S(1)} %get-tuple-element.776), channel_id=1, source_target_pairs={{0,3},{1,2},{2,1},{3,0},{4,7},{5,6},{6,5},{7,4},{8,11},{9,10},{10,... | collective-permute-start | bytes 417800 | tf_op jit(solution)/shard_map/cond/branch_5_fun/ppermute | solution.py:25
  139.5 16.7 %collective-permute-start.122 = (bf16[1,272,256]{2,1,0:T(8,128)(2,1)S(1)}, bf16[1,272,256]{2,1,0:T(8,128)(2,1)}, u32[]{:S(2)}, u32[]{:S(2)}) collective-permute-start(bf16[1,272,256]{2,1,0:T(8,128)(2,1)S(1)} %get-tuple-element.780), channel_id=1, source_target_pairs={{0,3},{1,2},{2,1},{3,0},{4,7},{5,6},{6,5},{7,4},{8,11},{9,10},{10,... | collective-permute-start | bytes 417800 | tf_op jit(solution)/shard_map/cond/branch_5_fun/ppermute | solution.py:25
  143.1 13.1 %collective-permute-start.121 = (bf16[1,272,256]{2,1,0:T(8,128)(2,1)S(1)}, bf16[1,272,256]{2,1,0:T(8,128)(2,1)}, u32[]{:S(2)}, u32[]{:S(2)}) collective-permute-start(bf16[1,272,256]{2,1,0:T(8,128)(2,1)S(1)} %get-tuple-element.777.refs_4_), channel_id=1, source_target_pairs={{0,2},{1,3},{2,0},{3,1},{4,6},{5,7},{6,4},{7,5},{8,10},{9,11},{10,... | collective-permute-start | bytes 417800 | tf_op jit(solution)/shard_map/cond/branch_5_fun/ppermute | solution.py:25
  148.9 7.3 %collective-permute-start.120 = (bf16[1,144,256]{2,1,0:T(8,128)(2,1)S(1)}, bf16[1,144,256]{2,1,0:T(8,128)(2,1)}, u32[]{:S(2)}, u32[]{:S(2)}) collective-permute-start(bf16[1,144,256]{2,1,0:T(8,128)(2,1)S(1)} %get-tuple-element.779), channel_id=1, source_target_pairs={{0,1},{1,0},{2,3},{3,2},{4,5},{5,4},{6,7},{7,6},{8,9},{9,8},{10,11... | collective-permute-start | bytes 221192 | tf_op jit(solution)/shard_map/cond/branch_5_fun/ppermute | solution.py:25
  149.0 7.3 %collective-permute-start.119 = (bf16[1,128,256]{2,1,0:T(8,128)(2,1)S(1)}, bf16[1,128,256]{2,1,0:T(8,128)(2,1)}, u32[]{:S(2)}, u32[]{:S(2)}) collective-permute-start(bf16[1,128,256]{2,1,0:T(8,128)(2,1)S(1)} %get-tuple-element.778), channel_id=1, source_target_pairs={{0,1},{1,0},{2,3},{3,2},{4,5},{5,4},{6,7},{7,6},{8,9},{9,8},{10,11... | collective-permute-start | bytes 196616 | tf_op jit(solution)/shard_map/cond/branch_5_fun/ppermute | solution.py:25
